TPU v7x, 32 devices: a whole 2x2x4 slice. The times are simulated.
32 devices in a mesh: rows: 16 (over z, y, core), seq: 2 (over x).
Axes of the slice: x: 2, y: 2, z: 4, core: 2. Of those that a mesh axis runs over, the one named last changes fastest.
Arguments:
- inputs: bfloat16 [16, 1024, 768], P('rows', 'seq'), may hold values from -6 to 6
- seg_start: int32 [16, 1024], P('rows', 'seq'), may hold values from -1 to 576, as said below
- w_query: bfloat16 [2, 768, 768], P(None, 'rows'), may hold values from -0.21875 to 0.21875
- w_key: bfloat16 [2, 768, 768], P(None, 'rows'), may hold values from -0.21875 to 0.21875
- w_value: bfloat16 [2, 768, 768], P(None, 'rows'), may hold values from -0.21875 to 0.21875
- w_out: bfloat16 [2, 768, 768], P(None, 'rows'), may hold values from -1.75 to 1.75
- w_gate: bfloat16 [2, 768, 2048], P(None, 'rows'), may hold values from -0.21875 to 0.21875
- w_up: bfloat16 [2, 768, 2048], P(None, 'rows'), may hold values from -0.21875 to 0.21875
- w_down: bfloat16 [2, 2048, 768], P(None, 'rows'), may hold values from -0.125 to 0.125
- norm_attn: bfloat16 [2, 768], P(None, 'rows'), may hold values from 0.5 to 1.5
- norm_mlp: bfloat16 [2, 768], P(None, 'rows'), may hold values from 0.5 to 1.5
- cotangent: bfloat16 [16, 1024, 768], P('rows', 'seq'), may hold values from -6 to 6
Outputs:
- output: float32 [16, 1024, 768], P('rows', 'seq')
- grad_input: float32 [16, 1024, 768], P('rows', 'seq')
- grad_query: float32 [2, 768, 768], P(None, 'rows')
- grad_key: float32 [2, 768, 768], P(None, 'rows')
- grad_value: float32 [2, 768, 768], P(None, 'rows')
- grad_out: float32 [2, 768, 768], P(None, 'rows')
- grad_gate: float32 [2, 768, 2048], P(None, 'rows')
- grad_up: float32 [2, 768, 2048], P(None, 'rows')
- grad_down: float32 [2, 2048, 768], P(None, 'rows')
- grad_norm_attn: float32 [2, 768], P(None, 'rows')
- grad_norm_mlp: float32 [2, 768], P(None, 'rows')
Inputs may be any that keep to these rules, and one draw needn't show every extreme that they name: `seg_start`: each row holds whole images of 576 or 256 tokens laid end to end from position 0, none beginning after position 576; every token of an image carries the image's first position; the rest of the row, one position or more, is padding and carries -1.
All inputs are finite; a program needn't handle non-finite values.
Results may differ from a plain program's by a relative error of at most 0.025.
Values may be sent and summed in bfloat16 or wider, within the bound.
No kernel may reach another device: no remote copies, remote signals or barrier semaphores. Data moves between devices by JAX's collectives and lax.ppermute only.
A program may use at most 448 MiB of HBM per device.

v0:
```python
import jax
import jax.numpy as jnp
from jax import lax
from jax.sharding import PartitionSpec as P

HEADS = 12
HEAD_DIM = 64
LAYERS = 2


EPS = 1e-05
NEG_BIG = -1e30
THETA = 10000.0


def as_sent(value):

    def short(part):
        return part.astype(jnp.bfloat16) if part.dtype == jnp.float32 else part

    return jax.tree.map(short, value)


def rope_tables(positions):
    half = HEAD_DIM // 2
    inverse = THETA ** (-jnp.arange(half, dtype=jnp.float32) * 2.0 / HEAD_DIM)
    angles = positions.astype(jnp.float32)[..., None] * inverse
    return (jnp.cos(angles)[..., None, :], jnp.sin(angles)[..., None, :])


def rotate(tensor, cosine, sine):
    half = tensor.shape[-1] // 2
    first = tensor[..., :half]
    second = tensor[..., half:]
    return jnp.concatenate([first * cosine - second * sine, second * cosine + first * sine], -1)


def unrotate(tensor, cosine, sine):
    half = tensor.shape[-1] // 2
    first = tensor[..., :half]
    second = tensor[..., half:]
    return jnp.concatenate([first * cosine + second * sine, second * cosine - first * sine], -1)


def project(left, matrix):
    return jnp.einsum("rtd,df->rtf", left, matrix, preferred_element_type=jnp.float32)


def project_back(grad_rows, matrix):
    return jnp.einsum("rtf,df->rtd", grad_rows, matrix, preferred_element_type=jnp.float32)


def weight_term(left, grad_rows):
    flat_left = left.reshape(-1, left.shape[-1])
    flat_grad = grad_rows.reshape(-1, grad_rows.shape[-1])
    return lax.dot_general(
        flat_left, flat_grad, (((0,), (0,)), ((), ())), preferred_element_type=jnp.float32
    )


def normalize(hidden):
    factor = lax.rsqrt(jnp.mean(hidden * hidden, -1, keepdims=True) + EPS)
    return (factor, hidden * factor)


def norm_back(grad_normed, gain, factor, normed):
    shaped = grad_normed * gain.astype(jnp.float32)
    grad_in = factor * (shaped - normed * jnp.mean(shaped * normed, -1, keepdims=True))
    return (grad_in, jnp.sum(grad_normed * normed, axis=(0, 1)))


def masked_scores(queries, key_block, allow_block):
    scores = jnp.einsum(
        "rqhd,rkhd->rhqk", queries, key_block, preferred_element_type=jnp.float32
    ) * HEAD_DIM ** (-0.5)
    return jnp.where(allow_block[:, None] > 0, scores, NEG_BIG)


def on_device(
    inputs,
    seg_start,
    w_query,
    w_key,
    w_value,
    w_out,
    w_gate,
    w_up,
    w_down,
    norm_attn,
    norm_mlp,
    cotangent,
):
    rows_here, band, width = inputs.shape
    cycle_size = lax.axis_size("seq")
    seq_pos = lax.axis_index("seq")
    all_starts = lax.all_gather(seg_start, "seq", axis=1, tiled=True)
    total_len = all_starts.shape[1]
    bands_per_block = min(cycle_size, max(1, 512 // band))
    while cycle_size % bands_per_block != 0:
        bands_per_block = bands_per_block - 1
    block_len = band * bands_per_block
    block_count = total_len // block_len
    needed = ((seq_pos + 1) * band - 1) // block_len + 1
    first_block = seq_pos * band // block_len
    scale = HEAD_DIM ** (-0.5)
    query_index = seq_pos * band + jnp.arange(band, dtype=jnp.int32)
    key_index = jnp.arange(total_len, dtype=jnp.int32)
    positions = jnp.where(seg_start >= 0, query_index[None, :] - seg_start, 0)
    cosine, sine = rope_tables(positions)
    same_image = (
        (seg_start[:, :, None] == all_starts[:, None, :])
        & (seg_start[:, :, None] >= 0)
        & (key_index[None, None, :] <= query_index[None, :, None])
    )
    allowed = (same_image | (key_index[None, None, :] == query_index[None, :, None])).astype(
        jnp.int32
    )

    def key_slice(array, block):
        return lax.dynamic_slice_in_dim(array, block * block_len, block_len, 1)

    def allow_slice(block):
        return lax.dynamic_slice_in_dim(allowed, block * block_len, block_len, 2)

    def attention_forward(queries, key_all, value_all):

        def fill(block, buffer):
            allow_block = allow_slice(block)

            def compute(inner):
                scores = masked_scores(queries, key_slice(key_all, block), allow_block)
                return lax.dynamic_update_slice_in_dim(inner, scores, block * block_len, 3)

            return lax.cond(jnp.any(allow_block > 0), compute, lambda inner: inner, buffer)

        scores = lax.fori_loop(
            0, needed, fill, jnp.full((rows_here, HEADS, band, total_len), NEG_BIG, jnp.float32)
        )
        highest = jnp.max(scores, -1, keepdims=True)
        expd = jnp.exp(scores - highest)
        totals = jnp.sum(expd, -1, keepdims=True)
        probs_low = (expd / totals).astype(jnp.bfloat16)

        def mix(block, accum):
            allow_block = allow_slice(block)

            def compute(inner):
                probs_block = lax.dynamic_slice_in_dim(probs_low, block * block_len, block_len, 3)
                return inner + jnp.einsum(
                    "rhqk,rkhd->rqhd",
                    probs_block,
                    key_slice(value_all, block),
                    preferred_element_type=jnp.float32,
                )

            return lax.cond(jnp.any(allow_block > 0), compute, lambda inner: inner, accum)

        mixed = lax.fori_loop(
            0, needed, mix, jnp.zeros((rows_here, band, HEADS, HEAD_DIM), jnp.float32)
        )
        return (mixed.astype(jnp.bfloat16), highest + jnp.log(totals))

    def fetch(layer_idx):
        return (
            lax.all_gather(w_query[layer_idx], "rows", axis=0, tiled=True),
            lax.all_gather(w_key[layer_idx], "rows", axis=0, tiled=True),
            lax.all_gather(w_value[layer_idx], "rows", axis=0, tiled=True),
            lax.all_gather(w_out[layer_idx], "rows", axis=0, tiled=True),
            lax.all_gather(w_gate[layer_idx], "rows", axis=0, tiled=True),
            lax.all_gather(w_up[layer_idx], "rows", axis=0, tiled=True),
            lax.all_gather(w_down[layer_idx], "rows", axis=0, tiled=True),
            lax.all_gather(norm_attn[layer_idx], "rows", axis=0, tiled=True),
            lax.all_gather(norm_mlp[layer_idx], "rows", axis=0, tiled=True),
        )

    def run_layer(layer_in, weights, kept_attn):
        w_q, w_k, w_v, w_o, w_g, w_u, w_d, gain_attn, gain_mlp = weights
        factor1, normed1 = normalize(layer_in)
        hidden = (normed1 * gain_attn.astype(jnp.float32)).astype(jnp.bfloat16)
        q_pre = project(hidden, w_q).reshape(rows_here, band, HEADS, HEAD_DIM)
        k_pre = project(hidden, w_k).reshape(rows_here, band, HEADS, HEAD_DIM)
        queries = rotate(q_pre, cosine, sine).astype(jnp.bfloat16)
        key_band = rotate(k_pre, cosine, sine).astype(jnp.bfloat16).reshape(rows_here, band, width)
        value_band = project(hidden, w_v).astype(jnp.bfloat16)
        key_all, value_all = (
            lax.all_gather(key_band, "seq", axis=1, tiled=True),
            lax.all_gather(value_band, "seq", axis=1, tiled=True),
        )
        key_all = key_all.reshape(rows_here, total_len, HEADS, HEAD_DIM)
        value_all = value_all.reshape(rows_here, total_len, HEADS, HEAD_DIM)
        if kept_attn is None:
            attended, lse_band = attention_forward(queries, key_all, value_all)
        else:
            attended, lse_band = kept_attn
        attended_flat = attended.reshape(rows_here, band, width)
        x_mid = layer_in + project(attended_flat, w_o)
        factor2, normed2 = normalize(x_mid)
        hidden2 = (normed2 * gain_mlp.astype(jnp.float32)).astype(jnp.bfloat16)
        gate = project(hidden2, w_g)
        up_val = project(hidden2, w_u)
        act = (gate * jax.nn.sigmoid(gate) * up_val).astype(jnp.bfloat16)
        layer_out = x_mid + project(act, w_d)
        return dict(
            out=layer_out,
            attended=attended,
            attended_flat=attended_flat,
            lse_band=lse_band,
            factor1=factor1,
            normed1=normed1,
            hidden=hidden,
            queries=queries,
            key_band=key_band.reshape(rows_here, band, HEADS, HEAD_DIM),
            value_band=value_band.reshape(rows_here, band, HEADS, HEAD_DIM),
            key_all=key_all,
            value_all=value_all,
            factor2=factor2,
            normed2=normed2,
            hidden2=hidden2,
            gate=gate,
            up_val=up_val,
            act=act,
        )

    layer_inputs = []
    kept_attn = []
    current = inputs.astype(jnp.float32)
    for layer_idx in range(LAYERS):
        weights = fetch(layer_idx)
        layer_inputs.append(current)
        state = run_layer(current, weights, None)
        kept_attn.append((state["attended"], state["lse_band"]))
        current = state["out"]
    grad_lists = [[] for _ in range(9)]
    flow = cotangent.astype(jnp.float32)
    for layer_idx in reversed(range(LAYERS)):
        weights = fetch(layer_idx)
        w_q, w_k, w_v, w_o, w_g, w_u, w_d, gain_attn, gain_mlp = weights
        state = run_layer(layer_inputs[layer_idx], weights, kept_attn[layer_idx])
        d_branch = flow.astype(jnp.bfloat16)
        d_act = project_back(d_branch, w_d)
        term_down = weight_term(state["act"], d_branch)
        gate = state["gate"]
        sigma = jax.nn.sigmoid(gate)
        d_gate = (d_act * state["up_val"] * sigma * (1.0 + gate * (1.0 - sigma))).astype(
            jnp.bfloat16
        )
        d_up = (d_act * gate * sigma).astype(jnp.bfloat16)
        term_gate = weight_term(state["hidden2"], d_gate)
        term_up = weight_term(state["hidden2"], d_up)
        d_hidden2 = project_back(d_gate, w_g) + project_back(d_up, w_u)
        d_mid_norm, term_gain_mlp = norm_back(
            d_hidden2, gain_mlp, state["factor2"], state["normed2"]
        )
        d_mid = flow + d_mid_norm
        d_attn = d_mid.astype(jnp.bfloat16)
        term_out = weight_term(state["attended_flat"], d_attn)
        d_attended = (
            project_back(d_attn, w_o).astype(jnp.bfloat16).reshape(rows_here, band, HEADS, HEAD_DIM)
        )
        queries = state["queries"]
        lse_band = state["lse_band"]
        attention_key_all = state["key_all"]
        attention_value_all = state["value_all"]
        grad_mixed = d_attended

        def attention_fill(block, buffers):
            allow_block = allow_slice(block)

            def compute(inner):
                probs_buf, dprob_buf = inner
                scores = masked_scores(queries, key_slice(attention_key_all, block), allow_block)
                probs = jnp.exp(scores - lse_band)
                grad_probs = jnp.einsum(
                    "rqhd,rkhd->rhqk",
                    grad_mixed,
                    key_slice(attention_value_all, block),
                    preferred_element_type=jnp.float32,
                )
                return (
                    lax.dynamic_update_slice_in_dim(probs_buf, probs, block * block_len, 3),
                    lax.dynamic_update_slice_in_dim(dprob_buf, grad_probs, block * block_len, 3),
                )

            return lax.cond(jnp.any(allow_block > 0), compute, lambda inner: inner, buffers)

        blank = jnp.zeros((rows_here, HEADS, band, total_len), jnp.float32)
        probs, grad_probs = lax.fori_loop(0, needed, attention_fill, (blank, blank))
        delta = jnp.sum(probs * grad_probs, -1, keepdims=True)
        grad_low = (probs * (grad_probs - delta)).astype(jnp.bfloat16)
        attention_probs_low = probs.astype(jnp.bfloat16)

        def attention_mix(block, accum):
            allow_block = allow_slice(block)

            def compute(inner):
                grad_block = lax.dynamic_slice_in_dim(grad_low, block * block_len, block_len, 3)
                return inner + jnp.einsum(
                    "rhqk,rkhd->rqhd",
                    grad_block,
                    key_slice(attention_key_all, block),
                    preferred_element_type=jnp.float32,
                )

            return lax.cond(jnp.any(allow_block > 0), compute, lambda inner: inner, accum)

        grad_query = (
            lax.fori_loop(
                0, needed, attention_mix, jnp.zeros((rows_here, band, HEADS, HEAD_DIM), jnp.float32)
            )
            * scale
        )
        d_queries, grad_low_all, probs_low_all, delta = (
            grad_query,
            grad_low,
            attention_probs_low,
            delta,
        )
        query_all, grad_att_all = (
            lax.all_gather(as_sent(queries), "seq", axis=1, tiled=True).astype(queries.dtype),
            lax.all_gather(d_attended, "seq", axis=1, tiled=True),
        )
        lse_all, delta_all = (
            lax.all_gather(lse_band, "seq", axis=2, tiled=True),
            lax.all_gather(delta, "seq", axis=2, tiled=True),
        )
        own_keys = seq_pos * band + jnp.arange(band, dtype=jnp.int32)
        image_match = (
            (all_starts[:, :, None] == seg_start[:, None, :])
            & (all_starts[:, :, None] >= 0)
            & (own_keys[None, None, :] <= key_index[None, :, None])
        )
        allowed_back = (image_match | (own_keys[None, None, :] == key_index[None, :, None])).astype(
            jnp.int32
        )
        key_band = state["key_band"]
        value_band = state["value_band"]

        def key_side(block, accums):
            allow_block = lax.dynamic_slice_in_dim(allowed_back, block * block_len, block_len, 1)

            def compute(inner):
                key_acc, value_acc = inner
                query_block = key_slice(query_all, block)
                grad_block = key_slice(grad_att_all, block)
                lse_block = lax.dynamic_slice_in_dim(lse_all, block * block_len, block_len, 2)
                delta_block = lax.dynamic_slice_in_dim(delta_all, block * block_len, block_len, 2)
                scores = masked_scores(query_block, key_band, allow_block)
                probs = jnp.exp(scores - lse_block)
                grad_probs = jnp.einsum(
                    "rqhd,rkhd->rhqk", grad_block, value_band, preferred_element_type=jnp.float32
                )
                grad_low = (probs * (grad_probs - delta_block)).astype(jnp.bfloat16)
                key_acc = (
                    key_acc
                    + jnp.einsum(
                        "rhqk,rqhd->rkhd", grad_low, query_block, preferred_element_type=jnp.float32
                    )
                    * scale
                )
                value_acc = value_acc + jnp.einsum(
                    "rhqk,rqhd->rkhd",
                    probs.astype(jnp.bfloat16),
                    grad_block,
                    preferred_element_type=jnp.float32,
                )
                return (key_acc, value_acc)

            return lax.cond(jnp.any(allow_block > 0), compute, lambda inner: inner, accums)

        blank_band = jnp.zeros((rows_here, band, HEADS, HEAD_DIM), jnp.float32)
        key_grad, value_grad = lax.fori_loop(
            first_block, block_count, key_side, (blank_band, blank_band)
        )
        value_grad = value_grad.reshape(rows_here, band, width)
        d_q = unrotate(d_queries, cosine, sine).astype(jnp.bfloat16).reshape(rows_here, band, width)
        d_k = unrotate(key_grad, cosine, sine).astype(jnp.bfloat16).reshape(rows_here, band, width)
        d_v = value_grad.astype(jnp.bfloat16)
        hidden = state["hidden"]
        term_query = weight_term(hidden, d_q)
        term_key = weight_term(hidden, d_k)
        term_value = weight_term(hidden, d_v)
        d_hidden = project_back(d_q, w_q) + project_back(d_k, w_k) + project_back(d_v, w_v)
        d_in_norm, term_gain_attn = norm_back(
            d_hidden, gain_attn, state["factor1"], state["normed1"]
        )
        flow = d_mid + d_in_norm
        terms = (
            term_query,
            term_key,
            term_value,
            term_out,
            term_gate,
            term_up,
            term_down,
            term_gain_attn,
            term_gain_mlp,
        )
        shares = (
            lax.psum_scatter(
                terms[0].astype(jnp.bfloat16), "rows", scatter_dimension=0, tiled=True
            ).astype(jnp.float32),
            lax.psum_scatter(
                terms[1].astype(jnp.bfloat16), "rows", scatter_dimension=0, tiled=True
            ).astype(jnp.float32),
            lax.psum_scatter(
                terms[2].astype(jnp.bfloat16), "rows", scatter_dimension=0, tiled=True
            ).astype(jnp.float32),
            lax.psum_scatter(
                terms[3].astype(jnp.bfloat16), "rows", scatter_dimension=0, tiled=True
            ).astype(jnp.float32),
            lax.psum_scatter(
                terms[4].astype(jnp.bfloat16), "rows", scatter_dimension=0, tiled=True
            ).astype(jnp.float32),
            lax.psum_scatter(
                terms[5].astype(jnp.bfloat16), "rows", scatter_dimension=0, tiled=True
            ).astype(jnp.float32),
            lax.psum_scatter(
                terms[6].astype(jnp.bfloat16), "rows", scatter_dimension=0, tiled=True
            ).astype(jnp.float32),
            lax.psum_scatter(
                terms[7].astype(jnp.bfloat16), "rows", scatter_dimension=0, tiled=True
            ).astype(jnp.float32),
            lax.psum_scatter(
                terms[8].astype(jnp.bfloat16), "rows", scatter_dimension=0, tiled=True
            ).astype(jnp.float32),
        )
        summed_grads = (
            lax.psum(shares[0].astype(jnp.bfloat16), "seq").astype(jnp.float32),
            lax.psum(shares[1].astype(jnp.bfloat16), "seq").astype(jnp.float32),
            lax.psum(shares[2].astype(jnp.bfloat16), "seq").astype(jnp.float32),
            lax.psum(shares[3].astype(jnp.bfloat16), "seq").astype(jnp.float32),
            lax.psum(shares[4].astype(jnp.bfloat16), "seq").astype(jnp.float32),
            lax.psum(shares[5].astype(jnp.bfloat16), "seq").astype(jnp.float32),
            lax.psum(shares[6].astype(jnp.bfloat16), "seq").astype(jnp.float32),
            lax.psum(shares[7].astype(jnp.bfloat16), "seq").astype(jnp.float32),
            lax.psum(shares[8].astype(jnp.bfloat16), "seq").astype(jnp.float32),
        )
        for position, grad_piece in enumerate(summed_grads):
            grad_lists[position].insert(0, grad_piece)
    stacked = [jnp.stack(pieces, 0) for pieces in grad_lists]
    return (
        current,
        flow,
        stacked[0],
        stacked[1],
        stacked[2],
        stacked[3],
        stacked[4],
        stacked[5],
        stacked[6],
        stacked[7],
        stacked[8],
    )


def solution(mesh):
    placed = (
        P("rows", "seq", None),
        P("rows", "seq"),
        P(None, "rows", None),
        P(None, "rows", None),
        P(None, "rows", None),
        P(None, "rows", None),
        P(None, "rows", None),
        P(None, "rows", None),
        P(None, "rows", None),
        P(None, "rows"),
        P(None, "rows"),
        P("rows", "seq", None),
    )
    return jax.shard_map(
        on_device,
        mesh=mesh,
        in_specs=placed,
        out_specs=(
            P("rows", "seq", None),
            P("rows", "seq", None),
            P(None, "rows", None),
            P(None, "rows", None),
            P(None, "rows", None),
            P(None, "rows", None),
            P(None, "rows", None),
            P(None, "rows", None),
            P(None, "rows", None),
            P(None, "rows"),
            P(None, "rows"),
        ),
        check_vma=False,
    )
```

profile of v0, /device:TPU:0, one launch (start us, length us, event | category | flops | bytes accessed | tf_op | source)
XLA Modules:
  0.0 1984.9 jit_solution(14709155091770832935)
XLA Ops:
  17.2 35.7 %all-reduce.9 = (bf16[768]{0:T(1024)(128)(2,1)S(1)}, bf16[768]{0:T(1024)(128)(2,1)S(1)}, bf16[768]{0:T(1024)(128)(2,1)S(1)}, bf16[768]{0:T(1024)(128)(2,1)S(1)}) all-reduce(bf16[768]{0:T(1024)(128)(2,1)S(1)} %dynamic-update-slice, bf16[768]{0:T(1024)(128)(2,1)S(1)} %dynamic-update-slice.1, ...), channel_id=2, replica_groups=mesh['rows'=16,'seq'=2] {'rows'}, use_global_device_ids=true, to_apply=%add | all-reduce | flops 3072 | bytes 12288
  57.5 34.8 %all-gather.59.cloned.1.call-done = bf16[1,768,768]{2,1,0:T(8,128)(2,1)} async-done(((bf16[1,48,768]{2,1,0:T(8,128)(2,1)}), bf16[1,768,768]{2,1,0:T(8,128)(2,1)}) %all-gather.59.cloned.1.call-update) | async-done | bytes 1179664 | tf_op jit(solution)/shard_map/all_gather | solution.py:167
  137.3 35.3 %all-gather.79.cloned.1.call-done = bf16[1,768,768]{2,1,0:T(8,128)(2,1)} async-done(((bf16[1,48,768]{2,1,0:T(8,128)(2,1)}), bf16[1,768,768]{2,1,0:T(8,128)(2,1)}) %all-gather.79.cloned.1.call-update) | async-done | bytes 1179664 | tf_op jit(solution)/shard_map/all_gather | solution.py:166
  175.9 24.9 %all-gather.47.cloned.1.call-done = bf16[1,1024,768]{1,2,0:T(8,128)(2,1)} async-done(((bf16[1,512,768]{1,2,0:T(8,128)(2,1)}), bf16[1,1024,768]{1,2,0:T(8,128)(2,1)}) %all-gather.47.cloned.1.call-update) | async-done | bytes 1572880 | tf_op jit(solution)/shard_map/all_gather | solution.py:186
  323.3 41.2 %all-gather.71.cloned.1.call-done = bf16[1,768,2048]{2,1,0:T(8,128)(2,1)} async-done(((bf16[1,48,2048]{2,1,0:T(8,128)(2,1)}), bf16[1,768,2048]{2,1,0:T(8,128)(2,1)}) %all-gather.71.cloned.1.call-update) | async-done | bytes 3145744 | tf_op jit(solution)/shard_map/all_gather | solution.py:170
  372.3 38.4 %all-gather.73.cloned.1.call-done = bf16[1,2048,768]{2,1,0:T(8,128)(2,1)} async-done(((bf16[1,128,768]{2,1,0:T(8,128)(2,1)}), bf16[1,2048,768]{2,1,0:T(8,128)(2,1)}) %all-gather.73.cloned.1.call-update) | async-done | bytes 3145744 | tf_op jit(solution)/shard_map/all_gather | solution.py:171
  419.8 30.4 %all-gather.75.cloned.1.call-done = bf16[1,768,768]{2,1,0:T(8,128)(2,1)} async-done(((bf16[1,48,768]{2,1,0:T(8,128)(2,1)}), bf16[1,768,768]{2,1,0:T(8,128)(2,1)}) %all-gather.75.cloned.1.call-update) | async-done | bytes 1179664 | tf_op jit(solution)/shard_map/all_gather | solution.py:167
  455.6 34.1 %all-gather.81.cloned.1.call-done = bf16[1,768,768]{2,1,0:T(8,128)(2,1)} async-done(((bf16[1,48,768]{2,1,0:T(8,128)(2,1)}), bf16[1,768,768]{2,1,0:T(8,128)(2,1)}) %all-gather.81.cloned.1.call-update) | async-done | bytes 1179664 | tf_op jit(solution)/shard_map/all_gather | solution.py:165
  495.5 40.7 %all-gather.89.cloned.1.call-done = bf16[1,2048,768]{2,1,0:T(8,128)(2,1)} async-done(((bf16[1,128,768]{2,1,0:T(8,128)(2,1)}), bf16[1,2048,768]{2,1,0:T(8,128)(2,1)}) %all-gather.89.cloned.1.call-update) | async-done | bytes 3145744 | tf_op jit(solution)/shard_map/all_gather | solution.py:171
  685.3 41.1 %all-gather.85.cloned.1.call-done = bf16[1,768,2048]{2,1,0:T(8,128)(2,1)} async-done(((bf16[1,48,2048]{2,1,0:T(8,128)(2,1)}), bf16[1,768,2048]{2,1,0:T(8,128)(2,1)}) %all-gather.85.cloned.1.call-update) | async-done | bytes 3145744 | tf_op jit(solution)/shard_map/all_gather | solution.py:169
  909.6 44.9 %while.132 = (s32[]{:T(128)}, f32[1,512,12,64]{1,3,2,0:T(8,128)}, f32[1,512,12,64]{1,3,2,0:T(8,128)}, s32[1,1024,512]{2,1,0:T(8,128)S(1)}, bf16[1,1024,12,64]{1,...) while((s32[]{:T(128)}, f32[1,512,12,64]{1,3,2,0:T(8,128)}, ...), condition=%wide.region_44.45_spmd, body=%wide.region_40.0_spmd.sunk | while | flops 1644036096 | bytes 125224440 | solution.py:371
  1078.5 25.0 %copy.84 = f32[1,12,512,1024]{3,2,1,0:T(8,128)} copy(f32[1,12,512,1024]{2,3,1,0:T(8,128)} %get-tuple-element.673) | data formatting | bytes 50331648 | tf_op jit(solution)/shard_map/while | solution.py:287
  1185.2 47.4 %while.135 = (s32[]{:T(128)}, f32[1,512,12,64]{1,3,2,0:T(8,128)}, f32[1,512,12,64]{1,3,2,0:T(8,128)}, s32[1,1024,512]{2,1,0:T(8,128)S(1)}, bf16[1,1024,12,64]{1,...) while((s32[]{:T(128)}, f32[1,512,12,64]{1,3,2,0:T(8,128)}, ...), condition=%wide.region_62.63_spmd, body=%wide.region_58.62_spmd.sunk | while | flops 1644036096 | bytes 125429304 | solution.py:371
  1269.8 43.9 %reduce-scatter.25.cloned.1.call-done = bf16[48,768]{1,0:T(8,128)(2,1)} async-done(((bf16[768,768]{1,0:T(8,128)(2,1)}), bf16[48,768]{1,0:T(8,128)(2,1)}) %reduce-scatter.25.cloned.1.call-update) | async-done | bytes 73744 | tf_op jit(solution)/shard_map/reduce_scatter | solution.py:405
  1313.7 69.1 %reduce-scatter.33.cloned.1.call-done = bf16[48,2048]{1,0:T(8,128)(2,1)} async-done(((bf16[768,2048]{1,0:T(8,128)(2,1)}), bf16[48,2048]{1,0:T(8,128)(2,1)}) %reduce-scatter.33.cloned.1.call-update) | async-done | bytes 196624 | tf_op jit(solution)/shard_map/reduce_scatter | solution.py:411
  1382.8 69.0 %reduce-scatter.37.cloned.1.call-done = bf16[48,2048]{1,0:T(8,128)(2,1)} async-done(((bf16[768,2048]{1,0:T(8,128)(2,1)}), bf16[48,2048]{1,0:T(8,128)(2,1)}) %reduce-scatter.37.cloned.1.call-update) | async-done | bytes 196624 | tf_op jit(solution)/shard_map/reduce_scatter | solution.py:414
  1451.9 68.8 %reduce-scatter.41.cloned.1.call-done = bf16[128,768]{1,0:T(8,128)(2,1)} async-done(((bf16[2048,768]{1,0:T(8,128)(2,1)}), bf16[128,768]{1,0:T(8,128)(2,1)}) %reduce-scatter.41.cloned.1.call-update) | async-done | bytes 196624 | tf_op jit(solution)/shard_map/reduce_scatter | solution.py:417
  1520.7 60.6 %reduce-scatter.19.cloned.1.call-done = bf16[48,768]{1,0:T(8,128)(2,1)} async-done(((bf16[768,768]{1,0:T(8,128)(2,1)}), bf16[48,768]{1,0:T(8,128)(2,1)}) %reduce-scatter.19.cloned.1.call-update) | async-done | bytes 73744 | tf_op jit(solution)/shard_map/reduce_scatter | solution.py:402
  1581.3 60.7 %reduce-scatter.15.cloned.1.call-done = bf16[48,768]{1,0:T(8,128)(2,1)} async-done(((bf16[768,768]{1,0:T(8,128)(2,1)}), bf16[48,768]{1,0:T(8,128)(2,1)}) %reduce-scatter.15.cloned.1.call-update) | async-done | bytes 73744 | tf_op jit(solution)/shard_map/reduce_scatter | solution.py:399
  1642.0 60.6 %reduce-scatter.23.cloned.1.call-done = bf16[48,768]{1,0:T(8,128)(2,1)} async-done(((bf16[768,768]{1,0:T(8,128)(2,1)}), bf16[48,768]{1,0:T(8,128)(2,1)}) %reduce-scatter.23.cloned.1.call-update) | async-done | bytes 73744 | tf_op jit(solution)/shard_map/reduce_scatter | solution.py:405
  1702.6 69.0 %reduce-scatter.39.cloned.1.call-done = bf16[128,768]{1,0:T(8,128)(2,1)} async-done(((bf16[2048,768]{1,0:T(8,128)(2,1)}), bf16[128,768]{1,0:T(8,128)(2,1)}) %reduce-scatter.39.cloned.1.call-update) | async-done | bytes 196624 | tf_op jit(solution)/shard_map/reduce_scatter | solution.py:417
  1771.6 69.1 %reduce-scatter.31.cloned.1.call-done = bf16[48,2048]{1,0:T(8,128)(2,1)} async-done(((bf16[768,2048]{1,0:T(8,128)(2,1)}), bf16[48,2048]{1,0:T(8,128)(2,1)}) %reduce-scatter.31.cloned.1.call-update) | async-done | bytes 196624 | tf_op jit(solution)/shard_map/reduce_scatter | solution.py:411
  1840.7 68.8 %reduce-scatter.35.cloned.1.call-done = bf16[48,2048]{1,0:T(8,128)(2,1)} async-done(((bf16[768,2048]{1,0:T(8,128)(2,1)}), bf16[48,2048]{1,0:T(8,128)(2,1)}) %reduce-scatter.35.cloned.1.call-update) | async-done | bytes 196624 | tf_op jit(solution)/shard_map/reduce_scatter | solution.py:414
  1914.1 30.2 %all-reduce.8 = (bf16[768]{0:T(1024)(128)(2,1)S(1)}, bf16[768]{0:T(1024)(128)(2,1)S(1)}, bf16[768]{0:T(1024)(128)(2,1)S(1)}, bf16[768]{0:T(1024)(128)(2,1)S(1)}) all-reduce(bf16[768]{0:T(1024)(128)(2,1)S(1)} %copy-done.114, bf16[768]{0:T(1024)(128)(2,1)S(1)} %get-tuple-element.811, ...), channel_id=41, replica_groups=mesh['rows'=16,'seq'=2] {'rows'}, use_global_device_ids=true, to_apply=%region_96.97.clone | all-reduce | flops 3072 | bytes 12288
  (614 shorter events, 1157.4 us)
Async XLA Ops:
  97.8 312.9 %all-gather.73.cloned.1.call-start = ((), (), s32[]{:S(2)}) async-start(), calls=%async_computation.41 | async-start | bytes 3342336 | tf_op jit(solution)/shard_map/all_gather | solution.py:171
  98.6 351.6 %all-gather.75.cloned.1.call-start = ((), (), s32[]{:S(2)}) async-start(), calls=%async_computation.42 | async-start | bytes 1253376 | tf_op jit(solution)/shard_map/all_gather | solution.py:167
  99.4 390.3 %all-gather.81.cloned.1.call-start = ((), (), s32[]{:S(2)}) async-start(), calls=%async_computation.45 | async-start | bytes 1253376 | tf_op jit(solution)/shard_map/all_gather | solution.py:165
  99.9 436.2 %all-gather.89.cloned.1.call-start = ((), (), s32[]{:S(2)}) async-start(), calls=%async_computation.49 | async-start | bytes 3342336 | tf_op jit(solution)/shard_map/all_gather | solution.py:171
  100.7 462.9 %all-gather.49.cloned.1.call-start = ((), (), s32[]{:S(2)}) async-start(), calls=%async_computation.15 | async-start | bytes 2359296 | tf_op jit(solution)/shard_map/all_gather | solution.py:186
  455.1 451.8 %all-gather.51.cloned.1.call-start = ((), (), s32[]{:S(2)}) async-start(), calls=%async_computation.16 | async-start | bytes 2359296 | tf_op jit(solution)/shard_map/all_gather | solution.py:319
  495.4 411.5 %all-gather.53.cloned.1.call-start = ((), (), s32[]{:S(2)}) async-start(), calls=%async_computation.17 | async-start | bytes 2359296 | tf_op jit(solution)/shard_map/all_gather | solution.py:320
  744.6 437.9 %all-gather.55.cloned.1.call-start = ((), (), s32[]{:S(2)}) async-start(), calls=%async_computation.18 | async-start | bytes 2359296 | tf_op jit(solution)/shard_map/all_gather | solution.py:319
  746.6 435.9 %all-gather.57.cloned.1.call-start = ((), (), s32[]{:S(2)}) async-start(), calls=%async_computation.19 | async-start | bytes 2359296 | tf_op jit(solution)/shard_map/all_gather | solution.py:320
  983.8 286.0 %reduce-scatter.29.cloned.1.call-start = ((), (), s32[]{:S(2)}) async-start(), calls=%async_computation.27 | async-start | bytes 1253376 | tf_op jit(solution)/shard_map/reduce_scatter | solution.py:408
  986.8 283.0 %reduce-scatter.17.cloned.1.call-start = ((), (), s32[]{:S(2)}) async-start(), calls=%async_computation.21 | async-start | bytes 1253376 | tf_op jit(solution)/shard_map/reduce_scatter | solution.py:399
  990.2 279.6 %reduce-scatter.21.cloned.1.call-start = ((), (), s32[]{:S(2)}) async-start(), calls=%async_computation.23 | async-start | bytes 1253376 | tf_op jit(solution)/shard_map/reduce_scatter | solution.py:402
  993.6 276.2 %reduce-scatter.27.cloned.1.call-start = ((), (), s32[]{:S(2)}) async-start(), calls=%async_computation.26 | async-start | bytes 1253376 | tf_op jit(solution)/shard_map/reduce_scatter | solution.py:408
  995.5 318.2 %reduce-scatter.25.cloned.1.call-start = ((), (), s32[]{:S(2)}) async-start(), calls=%async_computation.25 | async-start | bytes 1253376 | tf_op jit(solution)/shard_map/reduce_scatter | solution.py:405
  998.6 384.2 %reduce-scatter.33.cloned.1.call-start = ((), (), s32[]{:S(2)}) async-start(), calls=%async_computation.29 | async-start | bytes 3342336 | tf_op jit(solution)/shard_map/reduce_scatter | solution.py:411
  1004.0 447.9 %reduce-scatter.37.cloned.1.call-start = ((), (), s32[]{:S(2)}) async-start(), calls=%async_computation.31 | async-start | bytes 3342336 | tf_op jit(solution)/shard_map/reduce_scatter | solution.py:414
  1009.1 511.6 %reduce-scatter.41.cloned.1.call-start = ((), (), s32[]{:S(2)}) async-start(), calls=%async_computation.33 | async-start | bytes 3342336 | tf_op jit(solution)/shard_map/reduce_scatter | solution.py:417
  1021.1 560.2 %reduce-scatter.19.cloned.1.call-start = ((), (), s32[]{:S(2)}) async-start(), calls=%async_computation.22 | async-start | bytes 1253376 | tf_op jit(solution)/shard_map/reduce_scatter | solution.py:402
  1238.5 403.5 %reduce-scatter.15.cloned.1.call-start = ((), (), s32[]{:S(2)}) async-start(), calls=%async_computation.20 | async-start | bytes 1253376 | tf_op jit(solution)/shard_map/reduce_scatter | solution.py:399
  1241.7 460.9 %reduce-scatter.23.cloned.1.call-start = ((), (), s32[]{:S(2)}) async-start(), calls=%async_computation.24 | async-start | bytes 1253376 | tf_op jit(solution)/shard_map/reduce_scatter | solution.py:405
  1244.0 527.7 %reduce-scatter.39.cloned.1.call-start = ((), (), s32[]{:S(2)}) async-start(), calls=%async_computation.32 | async-start | bytes 3342336 | tf_op jit(solution)/shard_map/reduce_scatter | solution.py:417
  1249.2 591.5 %reduce-scatter.31.cloned.1.call-start = ((), (), s32[]{:S(2)}) async-start(), calls=%async_computation.28 | async-start | bytes 3342336 | tf_op jit(solution)/shard_map/reduce_scatter | solution.py:411
  1255.4 654.1 %reduce-scatter.35.cloned.1.call-start = ((), (), s32[]{:S(2)}) async-start(), calls=%async_computation.30 | async-start | bytes 3342336 | tf_op jit(solution)/shard_map/reduce_scatter | solution.py:414
  1260.7 709.1 %all-reduce.14.cloned.1.call-start = ((), (), s32[]{:S(2)}) async-start(), calls=%async_computation.50 | async-start | bytes 3538944 | tf_op jit(solution)/shard_map/psum | solution.py:428
  (157 other events, 5646.0 us)
Sparse Core Ops, SparseCore 0:
  10.9 41.1 all-gather.62
  232.2 38.3 all-gather.66
  273.5 44.1 all-gather.68
  320.5 43.9 all-gather.70
  366.7 43.9 all-gather.72
  491.9 44.1 all-gather.88
  594.4 38.3 all-gather.82
  635.5 44.1 all-gather.86
  682.4 43.9 all-gather.84
  1013.2 58.0 reduce-scatter.28
  1074.8 57.1 reduce-scatter.16
  1135.5 57.0 reduce-scatter.20
  1196.1 57.0 reduce-scatter.26
  1256.7 57.0 reduce-scatter.24
  1317.5 65.2 reduce-scatter.32
  1386.7 65.1 reduce-scatter.36
  1455.5 65.1 reduce-scatter.40
  1524.3 56.9 reduce-scatter.18
  1584.9 57.0 reduce-scatter.14
  1645.5 57.0 reduce-scatter.22
  1706.4 65.1 reduce-scatter.38
  1775.4 65.2 reduce-scatter.30
  1844.3 65.1 reduce-scatter.34
  1912.6 57.0 all-reduce.13
  (13 shorter events, 398.3 us)
where the time goes:
time: 2000 us; the launch traced here: 1980 us
  waiting for transfers between devices  1060 us (53%)
  local copies, waits for them, and re-layouts  306 us (15%)
  matrix products  281 us (14%)
  other arithmetic  184 us (9%)
  blocking collectives  126 us (6%)
    reduce_scatter x2, waiting for transfers between devices, on_device(): lax.psum_scatter(terms[4].astype(jnp.bfloat16), 'rows', scatter_dimension...  138 us
    reduce_scatter x2, waiting for transfers between devices, on_device(): lax.psum_scatter(terms[5].astype(jnp.bfloat16), 'rows', scatter_dimension...  138 us
    reduce_scatter x2, waiting for transfers between devices, on_device(): lax.psum_scatter(terms[6].astype(jnp.bfloat16), 'rows', scatter_dimension...  138 us
    reduce_scatter x2, waiting for transfers between devices, on_device(): lax.psum_scatter(terms[2].astype(jnp.bfloat16), 'rows', scatter_dimension...  105 us
    while x4, local copies, waits for them, and re-layouts, on_device(): probs, grad_probs = lax.fori_loop(0, needed, attention_fill, (blank, blank))  99.4 us
    another operation x14, local copies, waits for them, and re-layouts  82.5 us
    all_gather x2, waiting for transfers between devices, fetch(): lax.all_gather(w_down[layer_idx], 'rows', axis=0, tiled=True)  79.1 us
    unnamed x2, blocking collectives  65.9 us
  transfers between devices with their start and end apart: 37, of which 24 were waited for; matrix products, arithmetic and copies ran while one was open for 37% of the time, Pallas kernels for 0%

commit v1 on v0

v1 whole, which is shorter than its diff:
```python
import functools

import jax
import jax.numpy as jnp
from jax import lax
from jax.experimental import pallas as pl
from jax.experimental.pallas import tpu as pltpu
from jax.sharding import PartitionSpec as P

HEADS = 12
HEAD_DIM = 64
LAYERS = 2
EPS = 1e-05
NEG_BIG = -1e30
THETA = 10000.0
F32 = jnp.float32
BF16 = jnp.bfloat16
BOTH = ("rows", "seq")
SMEM = pl.BlockSpec(memory_space=pltpu.SMEM)
VMEM = pl.BlockSpec(memory_space=pltpu.VMEM)
ANY = pl.BlockSpec(memory_space=pl.ANY)
VMEM_BYTES = 56 * 1024 * 1024
Q_TILE = 128
K_TILE = 256


def dot(left, right):
    return jnp.dot(left, right, preferred_element_type=F32)


def dot_nt(left, right):
    return lax.dot_general(left, right, (((1,), (1,)), ((), ())), preferred_element_type=F32)


def swap_halves(block):
    lane = lax.broadcasted_iota(jnp.int32, block.shape, 1)
    return jnp.where(lane % 64 < 32, pltpu.roll(block, 96, 1), pltpu.roll(block, 32, 1))


def start_weights(order, refs, held, sem):
    rows = refs[0].shape[0]
    for index, ref in enumerate(refs):
        at = pl.multiple_of(order[index] * rows, 16)
        pltpu.make_async_copy(ref, held.at[pl.ds(at, rows), :], sem).start()


def wait_whole(held, sem):
    pltpu.make_async_copy(held, held, sem).wait()


def send_out(order, whole, refs, sem):
    index = 0
    for ref in refs:
        for part in range(ref.shape[0]):
            rows = ref.shape[1]
            at = pl.multiple_of(order[index] * rows, 16)
            pltpu.make_async_copy(whole.at[pl.ds(at, rows), :], ref.at[part], sem).start()
            index += 1


def call(kernel, name, out_shape, in_specs, out_specs, scratch, args, flops, nbytes):
    return pl.pallas_call(
        kernel,
        name=name,
        out_shape=out_shape,
        in_specs=in_specs,
        out_specs=out_specs,
        scratch_shapes=scratch,
        compiler_params=pltpu.CompilerParams(vmem_limit_bytes=VMEM_BYTES),
        cost_estimate=pl.CostEstimate(flops=flops, bytes_accessed=nbytes, transcendentals=0),
    )(*args)


def row_tile(tokens):
    return min(256, tokens)


def pre_kernel(n_w, order, x_ref, cos_ref, sin_ref, *refs):
    w_refs = refs[:n_w]
    q_ref, kv_ref, gains_ref, w_s, hid_s, sem = refs[n_w:]
    tokens, width = x_ref.shape
    start_weights(order, w_refs, w_s, sem)
    wait_whole(w_s, sem)
    gains_ref[...] = w_s[:, 3 * width : 3 * width + 128].astype(F32).T[:8]
    gain = gains_ref[0:1, :]
    tile = row_tile(tokens)

    def body(step, carry):
        at = pl.ds(pl.multiple_of(step * tile, tile), tile)
        x = x_ref[at, :].astype(F32)
        factor = lax.rsqrt(jnp.mean(x * x, -1, keepdims=True) + EPS)
        hidden = (x * factor * gain).astype(BF16)
        cosine, sine = cos_ref[at, :], sin_ref[at, :]
        for col in range(0, 3 * width, 256):
            part = dot(hidden, w_s[:, col : col + 256])
            if col < 2 * width:
                halves = []
                for lane in (0, 128):
                    block = part[:, lane : lane + 128]
                    halves.append(block * cosine + swap_halves(block) * sine)
                part = jnp.concatenate(halves, 1)
            if col < width:
                q_ref[at, col : col + 256] = (part * HEAD_DIM**-0.5).astype(BF16)
            else:
                kv_ref[at, col - width : col - width + 256] = part.astype(BF16)
        return carry

    lax.fori_loop(0, tokens // tile, body, 0)


def pre(order, x, cosine, sine, weights):
    tokens, width = x.shape
    cols = weights[0].shape[1]
    return call(
        functools.partial(pre_kernel, len(weights)),
        "pre",
        (
            jax.ShapeDtypeStruct((tokens, width), BF16),
            jax.ShapeDtypeStruct((tokens, 2 * width), BF16),
            jax.ShapeDtypeStruct((8, width), F32),
        ),
        [SMEM, VMEM, VMEM, VMEM] + [ANY] * len(weights),
        (VMEM, VMEM, VMEM),
        [
            pltpu.VMEM((width, cols), BF16),
            pltpu.VMEM((tokens, width), BF16),
            pltpu.SemaphoreType.DMA,
        ],
        (order, x, cosine, sine, *weights),
        2 * tokens * width * 3 * width,
        width * cols * 2 + tokens * width * 10,
    )


def load_bands(bands, kv_refs, kv_s, sem):
    tokens = kv_refs[0].shape[0]
    for index, ref in enumerate(kv_refs):
        at = pl.multiple_of(bands[index + 1] * tokens, tokens)
        pltpu.make_async_copy(ref, kv_s.at[pl.ds(at, tokens), :], sem).start()


def bias_tile(mark_col, mark_row, k_at, q_at, k_tile, q_tile):
    key = k_at + lax.broadcasted_iota(jnp.int32, (k_tile, q_tile), 0)
    query = q_at + lax.broadcasted_iota(jnp.int32, (k_tile, q_tile), 1)
    return jnp.where((mark_col == mark_row) & (key <= query), 0.0, NEG_BIG)


def head_pair(block):
    lane = lax.broadcasted_iota(jnp.int32, block.shape, 1)
    zero = jnp.zeros_like(block)
    return jnp.concatenate(
        [jnp.where(lane < 64, block, zero), jnp.where(lane >= 64, block, zero)], 0
    )


def transpose_into(dest, source, first, columns, rows):
    for col in range(0, columns, 128):
        for row in range(0, rows, 128):
            block = source[row : row + 128, first + col : first + col + 128]
            dest[col : col + 128, row : row + 128] = block.astype(F32).T.astype(BF16)


def attend_kernel(n_kv, low, bands, q_ref, row_ref, col_ref, *refs):
    kv_refs = refs[:n_kv]
    out_ref, lse_ref, kv_s, vt_s, acc_s, max_s, sum_s, sem = refs[n_kv:]
    tokens, width = q_ref.shape
    total = kv_s.shape[0]
    load_bands(bands, kv_refs, kv_s, sem)
    wait_whole(kv_s, sem)
    transpose_into(vt_s, kv_s, width, width, total)
    first = bands[0] * tokens
    lse_ref[...] = jnp.zeros_like(lse_ref)

    def q_step(q_index, carry):
        q_at = pl.multiple_of(q_index * Q_TILE, Q_TILE)
        max_s[...] = jnp.full_like(max_s, NEG_BIG)
        sum_s[...] = jnp.zeros_like(sum_s)
        acc_s[...] = jnp.zeros_like(acc_s)
        mark_row = row_ref[0:1, pl.ds(q_at, Q_TILE)]

        def k_step(k_index, inner):
            k_at = pl.multiple_of(k_index * K_TILE, K_TILE)
            bias = bias_tile(
                col_ref[pl.ds(k_at, K_TILE), :], mark_row, k_at, first + q_at, K_TILE, Q_TILE
            )
            bias = jnp.concatenate([bias, bias], 1)
            for pair in range(HEADS // 2):
                lanes = slice(128 * pair, 128 * pair + 128)
                queries = head_pair(q_ref[pl.ds(q_at, Q_TILE), lanes])
                scores = dot_nt(kv_s[pl.ds(k_at, K_TILE), lanes], queries) + bias
                before = max_s[pair : pair + 1, :]
                highest = jnp.maximum(before, jnp.max(scores, 0, keepdims=True))
                shrink = jnp.exp(before - highest)
                expd = jnp.exp(scores - highest)
                max_s[pair : pair + 1, :] = highest
                sum_s[pair : pair + 1, :] = sum_s[pair : pair + 1, :] * shrink + jnp.sum(
                    expd, 0, keepdims=True
                )
                low_p = expd.astype(BF16)
                for side in (0, 1):
                    heads = slice(128 * pair + 64 * side, 128 * pair + 64 * side + 64)
                    part = slice(Q_TILE * side, Q_TILE * side + Q_TILE)
                    mixed = dot(vt_s[heads, pl.ds(k_at, K_TILE)], low_p[:, part])
                    acc_s[heads, :] = acc_s[heads, :] * shrink[:, part] + mixed
            return inner

        high = (first + q_at + Q_TILE - 1) // K_TILE + 1
        lax.fori_loop(low[q_index], high, k_step, 0)
        for pair in range(HEADS // 2):
            lanes = slice(128 * pair, 128 * pair + 128)
            scale = 1.0 / sum_s[pair : pair + 1, :]
            lse = max_s[pair : pair + 1, :] + jnp.log(sum_s[pair : pair + 1, :])
            both = []
            for side in (0, 1):
                heads = slice(128 * pair + 64 * side, 128 * pair + 64 * side + 64)
                part = slice(Q_TILE * side, Q_TILE * side + Q_TILE)
                both.append(acc_s[heads, :] * scale[:, part])
                row = 2 * pair + side
                lse_ref[row : row + 1, pl.ds(q_at, Q_TILE)] = lse[:, part]
            out_ref[pl.ds(q_at, Q_TILE), lanes] = jnp.concatenate(both, 0).T.astype(BF16)
        return carry

    lax.fori_loop(0, tokens // Q_TILE, q_step, 0)


def attend(low, bands, queries, mark_row, mark_col, kv_list, total):
    tokens, width = queries.shape
    return call(
        functools.partial(attend_kernel, len(kv_list)),
        "attend",
        (
            jax.ShapeDtypeStruct((tokens, width), BF16),
            jax.ShapeDtypeStruct((16, tokens), F32),
        ),
        [SMEM, SMEM, VMEM, VMEM, VMEM] + [ANY] * len(kv_list),
        (VMEM, VMEM),
        [
            pltpu.VMEM((total, 2 * width), BF16),
            pltpu.VMEM((width, total), BF16),
            pltpu.VMEM((width, Q_TILE), F32),
            pltpu.VMEM((8, 2 * Q_TILE), F32),
            pltpu.VMEM((8, 2 * Q_TILE), F32),
            pltpu.SemaphoreType.DMA,
        ],
        (low, bands, queries, mark_row, mark_col, *kv_list),
        8 * tokens * total * width,
        total * width * 4 + tokens * width * 4,
    )


def post_kernel(n_w, order, x_ref, att_ref, gains_ref, *refs):
    a_refs, d_refs = refs[:n_w], refs[n_w : 2 * n_w]
    out_ref, mid_ref, gu_ref, a_s, d_s, act_s, sem_a, sem_d = refs[2 * n_w :]
    tokens, width = x_ref.shape
    ff = d_s.shape[0]
    start_weights(order, a_refs, a_s, sem_a)
    start_weights(order, d_refs, d_s, sem_d)
    wait_whole(a_s, sem_a)
    wait_whole(d_s, sem_d)
    gain = gains_ref[1:2, :]
    tile = row_tile(tokens)

    def body(step, carry):
        at = pl.ds(pl.multiple_of(step * tile, tile), tile)
        mid = x_ref[at, :].astype(F32) + dot(att_ref[at, :], a_s[:, :width])
        mid_ref[at, :] = mid
        factor = lax.rsqrt(jnp.mean(mid * mid, -1, keepdims=True) + EPS)
        hidden = (mid * factor * gain).astype(BF16)
        for col in range(0, ff, 256):
            gate = dot(hidden, a_s[:, width + col : width + col + 256])
            up = dot(hidden, a_s[:, width + ff + col : width + ff + col + 256])
            gu_ref[at, col : col + 256] = gate.astype(BF16)
            gu_ref[at, ff + col : ff + col + 256] = up.astype(BF16)
            act_s[:, col : col + 256] = (gate * jax.nn.sigmoid(gate) * up).astype(BF16)
        out_ref[at, :] = mid + dot(act_s[...], d_s[...])
        return carry

    lax.fori_loop(0, tokens // tile, body, 0)


def post(order, x, attended, gains, w_a, w_d):
    tokens, width = x.shape
    cols = w_a[0].shape[1]
    ff = (cols - width) // 2
    return call(
        functools.partial(post_kernel, len(w_a)),
        "post",
        (
            jax.ShapeDtypeStruct((tokens, width), F32),
            jax.ShapeDtypeStruct((tokens, width), F32),
            jax.ShapeDtypeStruct((tokens, 2 * ff), BF16),
        ),
        [SMEM, VMEM, VMEM, VMEM] + [ANY] * (2 * len(w_a)),
        (VMEM, VMEM, VMEM),
        [
            pltpu.VMEM((width, cols), BF16),
            pltpu.VMEM((ff, width), BF16),
            pltpu.VMEM((row_tile(tokens), ff), BF16),
            pltpu.SemaphoreType.DMA,
            pltpu.SemaphoreType.DMA,
        ],
        (order, x, attended, gains, *w_a, *w_d),
        2 * tokens * width * (cols + ff),
        (width * cols + ff * width) * 2 + tokens * width * 14 + tokens * ff * 4,
    )


def mlp_back_kernel(n_w, n_g, order, order_g, flow_ref, mid_ref, gu_ref, att_ref, gains_ref, *refs):
    a_refs, d_refs = refs[:n_w], refs[n_w : 2 * n_w]
    refs = refs[2 * n_w :]
    dmid_ref, datt_ref, ggain_ref = refs[:3]
    ga_refs, gd_refs = refs[3 : 3 + n_g], refs[3 + n_g : 3 + 2 * n_g]
    a_s, d_s, actt_s, db_s, dgu_s, hidt_s, attt_s, dattn_s, ga_s, gd_s, sem_a, sem_d = refs[
        3 + 2 * n_g :
    ]
    tokens, width = mid_ref.shape
    ff = d_s.shape[0]
    start_weights(order, d_refs, d_s, sem_d)
    start_weights(order, a_refs, a_s, sem_a)
    gain = gains_ref[1:2, :]
    tile = row_tile(tokens)
    wait_whole(d_s, sem_d)
    wait_whole(a_s, sem_a)
    ggain = jnp.zeros((1, width), F32)
    for start in range(0, tokens, tile):
        at = slice(start, start + tile)
        low_flow = flow_ref[at, :].astype(BF16)
        db_s[at, :] = low_flow

        def columns(step, carry, at=at, low_flow=low_flow):
            col = pl.multiple_of(step * 256, 256)
            d_act = dot_nt(low_flow, d_s[pl.ds(col, 256), :])
            gate = gu_ref[at, pl.ds(col, 256)].astype(F32)
            up = gu_ref[at, pl.ds(ff + col, 256)].astype(F32)
            sigma = jax.nn.sigmoid(gate)
            silu = gate * sigma
            actt_s[pl.ds(col, 256), at] = (silu * up).T.astype(BF16)
            dgu_s[at, pl.ds(col, 256)] = (
                d_act * up * (sigma * (1.0 + gate * (1.0 - sigma)))
            ).astype(BF16)
            dgu_s[at, pl.ds(ff + col, 256)] = (d_act * silu).astype(BF16)
            return carry

        lax.fori_loop(0, ff // 256, columns, 0)
        mid = mid_ref[at, :]
        factor = lax.rsqrt(jnp.mean(mid * mid, -1, keepdims=True) + EPS)
        normed = mid * factor
        hidt_s[:, at] = (normed * gain).T.astype(BF16)
        attt_s[:, at] = att_ref[at, :].astype(F32).T.astype(BF16)
        d_hid = dot_nt(dgu_s[at, :], a_s[:, width:])
        ggain = ggain + jnp.sum(d_hid * normed, 0, keepdims=True)
        shaped = d_hid * gain
        d_mid = flow_ref[at, :].astype(F32) + factor * (
            shaped - normed * jnp.mean(shaped * normed, -1, keepdims=True)
        )
        dmid_ref[at, :] = d_mid
        d_attn = d_mid.astype(BF16)
        dattn_s[at, :] = d_attn
        datt_ref[at, :] = dot_nt(d_attn, a_s[:, :width]).astype(BF16)
    ggain_ref[...] = jnp.broadcast_to(ggain, ggain_ref.shape)

    def down_rows(step, carry):
        at = pl.ds(pl.multiple_of(step * 256, 256), 256)
        gd_s[at, :] = dot(actt_s[at, :], db_s[...]).astype(BF16)
        return carry

    lax.fori_loop(0, ff // 256, down_rows, 0)
    send_out(order_g, gd_s, gd_refs, sem_d)
    ga_s[:, :width] = dot(attt_s[...], dattn_s[...]).astype(BF16)

    def gu_columns(step, carry):
        col = pl.multiple_of(step * 256, 256)
        ga_s[:, pl.ds(width + col, 256)] = dot(hidt_s[...], dgu_s[:, pl.ds(col, 256)]).astype(BF16)
        return carry

    lax.fori_loop(0, 2 * ff // 256, gu_columns, 0)
    send_out(order_g, ga_s, ga_refs, sem_a)
    wait_whole(gd_s, sem_d)
    wait_whole(ga_s, sem_a)


def mlp_back(order, order_g, parts, flow, mid, gu, attended, gains, w_a, w_d):
    tokens, width = mid.shape
    cols = w_a[0].shape[1]
    ff = (cols - width) // 2
    n_g, per, pieces = parts
    ga = jax.ShapeDtypeStruct((per, width // pieces, cols), BF16)
    gd = jax.ShapeDtypeStruct((per, ff // pieces, width), BF16)
    return call(
        functools.partial(mlp_back_kernel, len(w_a), n_g),
        "mlp_back",
        (
            jax.ShapeDtypeStruct((tokens, width), F32),
            jax.ShapeDtypeStruct((tokens, width), BF16),
            jax.ShapeDtypeStruct((8, width), F32),
            *([ga] * n_g),
            *([gd] * n_g),
        ),
        [SMEM, SMEM] + [VMEM] * 5 + [ANY] * (2 * len(w_a)),
        (VMEM, VMEM, VMEM, *([ANY] * (2 * n_g))),
        [
            pltpu.VMEM((width, cols), BF16),
            pltpu.VMEM((ff, width), BF16),
            pltpu.VMEM((ff, tokens), BF16),
            pltpu.VMEM((tokens, width), BF16),
            pltpu.VMEM((tokens, 2 * ff), BF16),
            pltpu.VMEM((width, tokens), BF16),
            pltpu.VMEM((width, tokens), BF16),
            pltpu.VMEM((tokens, width), BF16),
            pltpu.VMEM((width, cols), BF16),
            pltpu.VMEM((ff, width), BF16),
            pltpu.SemaphoreType.DMA,
            pltpu.SemaphoreType.DMA,
        ],
        (order, order_g, flow, mid, gu, attended, gains, *w_a, *w_d),
        4 * tokens * width * (cols + ff),
        (width * cols + ff * width) * 4 + tokens * width * 16 + tokens * ff * 4,
    )


def attend_back_kernel(
    n_kv, low, bands, q_ref, do_ref, out_ref, lse_ref, row_ref, col_ref, cos_ref, sin_ref, *refs
):
    kv_refs = refs[:n_kv]
    dq_ref = refs[n_kv]
    dkv_refs = refs[n_kv + 1 : 2 * n_kv + 1]
    kv_s, kt_s, dqt_s, dkv_s, dlow_s, delta_s, sem = refs[2 * n_kv + 1 :]
    tokens, width = q_ref.shape
    total = kv_s.shape[0]
    load_bands(bands, kv_refs, kv_s, sem)
    head_of = lax.broadcasted_iota(jnp.int32, (16, width), 1) // HEAD_DIM
    picks = (head_of == lax.broadcasted_iota(jnp.int32, (16, width), 0)).astype(BF16)
    product = do_ref[...].astype(F32) * out_ref[...].astype(F32)
    upper = product.astype(BF16)
    lower = (product - upper.astype(F32)).astype(BF16)
    delta_s[...] = dot_nt(picks, upper) + dot_nt(picks, lower)
    dkv_s[...] = jnp.zeros_like(dkv_s)
    wait_whole(kv_s, sem)
    transpose_into(kt_s, kv_s, 0, width, total)
    first = bands[0] * tokens

    def q_step(q_index, carry):
        q_at = pl.multiple_of(q_index * Q_TILE, Q_TILE)
        q_rows = pl.ds(q_at, Q_TILE)
        dqt_s[...] = jnp.zeros_like(dqt_s)
        mark_row = row_ref[0:1, q_rows]

        def k_step(k_index, inner):
            k_at = pl.multiple_of(k_index * K_TILE, K_TILE)
            k_rows = pl.ds(k_at, K_TILE)
            bias = bias_tile(col_ref[k_rows, :], mark_row, k_at, first + q_at, K_TILE, Q_TILE)
            bias = jnp.concatenate([bias, bias], 1)
            for pair in range(HEADS // 2):
                lanes = slice(128 * pair, 128 * pair + 128)
                v_lanes = slice(width + 128 * pair, width + 128 * pair + 128)
                queries = head_pair(q_ref[q_rows, lanes])
                d_out = head_pair(do_ref[q_rows, lanes])
                lse = jnp.concatenate(
                    [lse_ref[2 * pair + side : 2 * pair + side + 1, q_rows] for side in (0, 1)], 1
                )
                delta = jnp.concatenate(
                    [delta_s[2 * pair + side : 2 * pair + side + 1, q_rows] for side in (0, 1)], 1
                )
                scores = dot_nt(kv_s[k_rows, lanes], queries) + bias
                probs = jnp.exp(scores - lse)
                d_probs = dot_nt(kv_s[k_rows, v_lanes], d_out)
                d_scores = (probs * (d_probs - delta)).astype(BF16)
                dkv_s[k_rows, v_lanes] += dot(probs.astype(BF16), d_out)
                dkv_s[k_rows, lanes] += dot(d_scores, queries)
                for side in (0, 1):
                    heads = slice(128 * pair + 64 * side, 128 * pair + 64 * side + 64)
                    part = slice(Q_TILE * side, Q_TILE * side + Q_TILE)
                    dqt_s[heads, :] += dot(kt_s[heads, k_rows], d_scores[:, part])
            return inner

        high = (first + q_at + Q_TILE - 1) // K_TILE + 1
        lax.fori_loop(low[q_index], high, k_step, 0)
        cosine, sine = cos_ref[q_rows, :], sin_ref[q_rows, :]
        for pair in range(HEADS // 2):
            lanes = slice(128 * pair, 128 * pair + 128)
            block = dqt_s[lanes, :].T * HEAD_DIM**-0.5
            dq_ref[q_rows, lanes] = (block * cosine - swap_halves(block) * sine).astype(BF16)
        return carry

    lax.fori_loop(0, tokens // Q_TILE, q_step, 0)
    for index, ref in enumerate(dkv_refs):
        at = pl.multiple_of(bands[index + 1] * tokens, tokens)
        dlow_s[index] = dkv_s[pl.ds(at, tokens), :].astype(BF16)
        pltpu.make_async_copy(dlow_s.at[index], ref, sem).start()
    wait_whole(dlow_s, sem)


def attend_back(low, bands, queries, d_out, out, lse, mark_row, mark_col, cosine, sine, kv_list, total):
    tokens, width = queries.shape
    n_kv = len(kv_list)
    return call(
        functools.partial(attend_back_kernel, n_kv),
        "attend_back",
        (
            jax.ShapeDtypeStruct((tokens, width), BF16),
            *([jax.ShapeDtypeStruct((tokens, 2 * width), BF16)] * n_kv),
        ),
        [SMEM, SMEM] + [VMEM] * 8 + [ANY] * n_kv,
        (VMEM, *([ANY] * n_kv)),
        [
            pltpu.VMEM((total, 2 * width), BF16),
            pltpu.VMEM((width, total), BF16),
            pltpu.VMEM((width, Q_TILE), F32),
            pltpu.VMEM((total, 2 * width), F32),
            pltpu.VMEM((n_kv, tokens, 2 * width), BF16),
            pltpu.VMEM((16, tokens), F32),
            pltpu.SemaphoreType.DMA,
        ],
        (low, bands, queries, d_out, out, lse, mark_row, mark_col, cosine, sine, *kv_list),
        20 * tokens * total * width,
        total * width * 8 + tokens * width * 8,
    )


def pre_back_kernel(
    n_w, n_g, n_kv, order, order_g, x_ref, dq_ref, cos_ref, sin_ref, gains_ref, dmid_ref, ggain_ref, *refs
):
    dkv_refs, w_refs = refs[:n_kv], refs[n_kv : n_kv + n_w]
    refs = refs[n_kv + n_w :]
    flow_ref, g_refs = refs[0], refs[1 : 1 + n_g]
    w_s, hidt_s, dqkv_s, g_s, sem = refs[1 + n_g :]
    tokens, width = x_ref.shape
    start_weights(order, w_refs, w_s, sem)
    gain = gains_ref[0:1, :]
    tile = row_tile(tokens)
    wait_whole(w_s, sem)
    ggain = jnp.zeros((1, width), F32)
    for start in range(0, tokens, tile):
        at = slice(start, start + tile)
        x = x_ref[at, :].astype(F32)
        factor = lax.rsqrt(jnp.mean(x * x, -1, keepdims=True) + EPS)
        normed = x * factor
        hidt_s[:, at] = (normed * gain).T.astype(BF16)
        cosine, sine = cos_ref[at, :], sin_ref[at, :]
        dqkv_s[at, :width] = dq_ref[at, :]
        for col in range(0, 2 * width, 128):
            block = dkv_refs[0][at, col : col + 128].astype(F32)
            for ref in dkv_refs[1:]:
                block = block + ref[at, col : col + 128].astype(F32)
            if col < width:
                block = block * cosine - swap_halves(block) * sine
            dqkv_s[at, width + col : width + col + 128] = block.astype(BF16)
        d_hid = dot_nt(dqkv_s[at, :], w_s[:, : 3 * width])
        ggain = ggain + jnp.sum(d_hid * normed, 0, keepdims=True)
        shaped = d_hid * gain
        flow_ref[at, :] = dmid_ref[at, :] + factor * (
            shaped - normed * jnp.mean(shaped * normed, -1, keepdims=True)
        )
    row = lax.broadcasted_iota(jnp.int32, (128, width), 0)
    both = jnp.where(row == 0, ggain, jnp.where(row == 1, ggain_ref[0:1, :], 0.0))
    g_s[:, 3 * width :] = both.T.astype(BF16)

    def columns(step, carry):
        col = pl.multiple_of(step * 256, 256)
        g_s[:, pl.ds(col, 256)] = dot(hidt_s[...], dqkv_s[:, pl.ds(col, 256)]).astype(BF16)
        return carry

    lax.fori_loop(0, 3 * width // 256, columns, 0)
    send_out(order_g, g_s, g_refs, sem)
    wait_whole(g_s, sem)


def pre_back(order, order_g, parts, x, dq, cosine, sine, gains, d_mid, ggain, dkv_list, weights):
    tokens, width = x.shape
    cols = weights[0].shape[1]
    n_g, per, pieces = parts
    return call(
        functools.partial(pre_back_kernel, len(weights), n_g, len(dkv_list)),
        "pre_back",
        (
            jax.ShapeDtypeStruct((tokens, width), F32),
            *([jax.ShapeDtypeStruct((per, width // pieces, cols), BF16)] * n_g),
        ),
        [SMEM, SMEM] + [VMEM] * (7 + len(dkv_list)) + [ANY] * len(weights),
        (VMEM, *([ANY] * n_g)),
        [
            pltpu.VMEM((width, cols), BF16),
            pltpu.VMEM((width, tokens), BF16),
            pltpu.VMEM((tokens, 3 * width), BF16),
            pltpu.VMEM((width, cols), BF16),
            pltpu.SemaphoreType.DMA,
        ],
        (order, order_g, x, dq, cosine, sine, gains, d_mid, ggain, *dkv_list, *weights),
        4 * tokens * width * 3 * width,
        width * cols * 4 + tokens * width * 20,
    )


class Layout:
    def __init__(self, n_rows, n_seq, width, ff):
        self.n_rows, self.n_seq = n_rows, n_seq
        self.paired = n_rows % 2 == 0 and n_seq % 2 == 0
        self.ringed = (
            n_rows % 4 == 0 and (width // n_rows) % 16 == 0 and (ff // n_rows) % 16 == 0
        )

    def device(self, row, seq):
        return row * self.n_seq + seq

    def pairs(self, move):
        return [
            (self.device(row, seq), self.device(*move(row, seq)))
            for row in range(self.n_rows)
            for seq in range(self.n_seq)
        ]

    def send(self, value, move):
        return lax.ppermute(value, BOTH, self.pairs(move))

    def to_core(self, value):
        return self.send(value, lambda row, seq: (row ^ 1, seq))

    def to_y(self, value):
        return self.send(value, lambda row, seq: (row ^ 2, seq))

    def to_z(self, value):
        return self.send(value, lambda row, seq: ((row + 4) % self.n_rows, seq))

    def to_x(self, value):
        return self.send(value, lambda row, seq: (row, (seq + 1) % self.n_seq))

    def regroup(self, row, seq):
        if not self.paired:
            return (row, seq)
        return (row - row % 2 + seq % 2, (row % 2) * (self.n_seq // 2) + seq // 2)

    def into_groups(self, value):
        return self.send(value, self.regroup) if self.paired else value

    def out_of_groups(self, value):
        if not self.paired:
            return value
        back = [(there, here) for here, there in self.pairs(self.regroup)]
        return lax.ppermute(value, BOTH, back)

    def band(self, row, seq):
        if not self.paired:
            return seq
        return (seq % (self.n_seq // 2)) * 2 + row % 2

    def groups(self):
        places = {}
        for row in range(self.n_rows):
            for seq in range(self.n_seq):
                there = self.regroup(row, seq)
                places.setdefault(row, {})[seq] = self.device(*there)
        return [[places[row][seq] for seq in range(self.n_seq)] for row in range(self.n_rows)]


def on_device(n_rows, n_seq, *args):
    inputs, seg_start, w_q, w_k, w_v, w_o, w_g, w_u, w_d, norm_attn, norm_mlp, cotangent = args
    _, tokens, width = inputs.shape
    ff = w_g.shape[2]
    total = tokens * n_seq
    lay = Layout(n_rows, n_seq, width, ff)
    row_at, seq_at = lax.axis_index("rows"), lax.axis_index("seq")

    def bundles(layer):
        gains = jnp.stack([norm_attn[layer], norm_mlp[layer]], 1)
        gains = jnp.pad(gains, ((0, 0), (0, 126)))
        return (
            jnp.concatenate([w_q[layer], w_k[layer], w_v[layer], gains], 1),
            jnp.concatenate([w_o[layer], w_g[layer], w_u[layer]], 1),
            w_d[layer],
        )

    def gather(shard):
        if not lay.ringed:
            return [lax.all_gather(shard, "rows", axis=0, tiled=True)]
        here = [shard]
        while len(here) < n_rows // 4:
            here.append(lay.to_z(here[-1]))
        here = here + [lay.to_y(chunk) for chunk in here]
        return here + [lay.to_core(chunk) for chunk in here]

    if lay.ringed:
        depth = n_rows // 4
        order, order_g = [], []
        for core in (0, 1):
            for side in (0, 2):
                for hop in range(depth):
                    order.append(((row_at - 4 * hop) % n_rows) ^ core ^ side)
                    order_g.append(((row_at + 4 * hop) % n_rows) ^ core ^ side)
        order, order_g = jnp.stack(order).astype(jnp.int32), jnp.stack(order_g).astype(jnp.int32)
        parts = (4, depth, n_rows)
    else:
        order = order_g = jnp.zeros((1,), jnp.int32)
        parts = (1, 1, 1)

    def scatter(stacks):
        if not lay.ringed:
            summed = lax.psum_scatter(stacks[0][0], "rows", scatter_dimension=0, tiled=True)
            return lax.psum(summed, "seq").astype(F32)
        far = (stacks[1].astype(F32) + lay.to_core(stacks[3]).astype(F32)).astype(BF16)
        far = lay.to_y(far).astype(F32)
        near = stacks[0].astype(F32) + lay.to_core(stacks[2]).astype(F32)
        both = near + far
        depth = both.shape[0]
        moving = both[depth - 1].astype(BF16)
        for hop in range(depth - 2, -1, -1):
            moving = (lay.to_z(moving).astype(F32) + both[hop]).astype(BF16)
        if n_seq != 2:
            return lax.psum(moving, "seq").astype(F32)
        return moving.astype(F32) + lay.to_x(moving).astype(F32)

    x_in = lay.into_groups(inputs[0])
    starts_mine = lay.into_groups(seg_start[0])
    d_top = lay.into_groups(cotangent[0])
    groups = lay.groups()
    half = n_seq // 2
    band = (seq_at % half) * 2 + row_at % 2 if lay.paired else seq_at
    two = lay.paired and n_seq == 2

    def exchange(value):
        if two:
            return [value, lay.to_core(value)]
        whole = lax.all_gather(value, BOTH, axis=0, axis_index_groups=groups)
        return [whole[index] for index in range(n_seq)]

    if two:
        bands = jnp.stack([band, band, 1 - band]).astype(jnp.int32)
    else:
        bands = jnp.concatenate([band[None], jnp.arange(n_seq)]).astype(jnp.int32)

    index = band * tokens + jnp.arange(tokens, dtype=jnp.int32)
    positions = jnp.where(starts_mine >= 0, index - starts_mine, 0)
    inverse = THETA ** (-jnp.arange(HEAD_DIM // 2, dtype=F32) * 2.0 / HEAD_DIM)
    angles = positions.astype(F32)[:, None] * inverse
    cosine = jnp.tile(jnp.cos(angles), (1, 4))
    sine = jnp.sin(angles)
    sine = jnp.concatenate([-sine, sine, -sine, sine], 1)
    marks = jnp.where(starts_mine >= 0, starts_mine, -1 - index)
    mark_row = jnp.broadcast_to(marks[None, :], (8, tokens))
    pieces = exchange(marks)
    if two:
        marks_all = jnp.where(
            band == 0, jnp.concatenate(pieces), jnp.concatenate([pieces[1], pieces[0]])
        )
    else:
        marks_all = jnp.concatenate(pieces)
    mark_col = jnp.broadcast_to(marks_all[:, None], (total, 128))
    reach = jnp.where(starts_mine >= 0, starts_mine, index)
    low = (jnp.min(reach.reshape(-1, Q_TILE), 1) // K_TILE).astype(jnp.int32)

    kept = []
    current = x_in
    for layer in range(LAYERS):
        qkv_shard, ogu_shard, down_shard = bundles(layer)
        w_qkv = gather(qkv_shard)
        w_ogu = gather(ogu_shard)
        w_down = gather(down_shard)
        queries, kv, gains = pre(order, current, cosine, sine, w_qkv)
        kv_list = exchange(kv)
        attended, lse = attend(low, bands, queries, mark_row, mark_col, kv_list, total)
        following, mid, gu = post(order, current, attended, gains, w_ogu, w_down)
        kept.append((current, queries, kv_list, attended, lse, mid, gu, gains, w_qkv, w_ogu, w_down))
        current = following
    output = lay.out_of_groups(current)

    grads = [None] * LAYERS
    flow = d_top
    for layer in reversed(range(LAYERS)):
        x, queries, kv_list, attended, lse, mid, gu, gains, w_qkv, w_ogu, w_down = kept[layer]
        n_g = parts[0]
        results = mlp_back(order, order_g, parts, flow, mid, gu, attended, gains, w_ogu, w_down)
        d_mid, d_att, ggain = results[:3]
        g_ogu = scatter(results[3 : 3 + n_g])
        g_down = scatter(results[3 + n_g : 3 + 2 * n_g])
        results = attend_back(
            low,
            bands,
            queries,
            d_att,
            attended,
            lse,
            mark_row,
            mark_col,
            cosine,
            sine,
            kv_list,
            total,
        )
        dq, dkv = results[0], results[1:]
        if two:
            dkv_list = [dkv[0], lay.to_core(dkv[1])]
        else:
            dkv_list = [
                lax.psum_scatter(
                    jnp.stack(dkv), BOTH, scatter_dimension=0, axis_index_groups=groups
                )
            ]
        results = pre_back(
            order, order_g, parts, x, dq, cosine, sine, gains, d_mid, ggain, dkv_list, w_qkv
        )
        flow = results[0]
        g_qkv = scatter(results[1:])
        grads[layer] = (g_qkv, g_ogu, g_down)
    grad_input = lay.out_of_groups(flow)

    def stack(which, first, size):
        return jnp.stack([grads[layer][which][:, first : first + size] for layer in range(LAYERS)])

    return (
        output[None],
        grad_input[None],
        stack(0, 0, width),
        stack(0, width, width),
        stack(0, 2 * width, width),
        stack(1, 0, width),
        stack(1, width, ff),
        stack(1, width + ff, ff),
        stack(2, 0, width),
        stack(0, 3 * width, 1)[..., 0],
        stack(0, 3 * width + 1, 1)[..., 0],
    )


def solution(mesh):
    rows3, rows2 = P("rows", "seq", None), P("rows", "seq")
    weight, vector = P(None, "rows", None), P(None, "rows")
    return jax.shard_map(
        functools.partial(on_device, mesh.shape["rows"], mesh.shape["seq"]),
        mesh=mesh,
        in_specs=(rows3, rows2, *([weight] * 7), vector, vector, rows3),
        out_specs=(rows3, rows3, *([weight] * 7), vector, vector),
        check_vma=False,
    )
```

time: 2000 us -> 757 us (0.38)
  waiting for transfers between devices: 1060 us -> 402 us
  local copies, waits for them, and re-layouts: 306 us -> 16.5 us
  matrix products: 281 us -> 0 us
  Pallas kernels: 0 us -> 206 us
  other arithmetic: 184 us -> 23 us
  blocking collectives: 126 us -> 0 us
  starting transfers between devices: 2.56 us -> 96.6 us
    reduce_scatter x14 -> x0, waiting for transfers between devices: 640 us -> none  [the longest x2 138 us: on_device(): lax.psum_scatter(terms[4].astype(jnp.bfloat16), 'rows', scatter_dimension...]
    ppermute x0 -> x142, waiting for transfers between devices: none -> 402 us  [the longest x140 402 us: send(): return lax.ppermute(value, BOTH, self.pairs(move))]
    all_gather x22 -> x0, waiting for transfers between devices: 397 us -> none  [the longest x2 79.1 us: fetch(): lax.all_gather(w_down[layer_idx], 'rows', axis=0, tiled=True)]
    dot_general x64 -> x0, matrix products: 281 us -> none  [the longest x14 55.4 us: project(): jnp.einsum('rtd,df->rtf', left, matrix, preferred_element_type=jnp.float32)]
    pallas_call x0 -> x12, Pallas kernels: none -> 206 us  [call(): pl.pallas_call(kernel, name=name, out_shape=out_shape, in_specs=in_specs,...]
    while x7 -> x0, local copies, waits for them, and re-layouts: 151 us -> none  [the longest x4 99.4 us: on_device(): probs, grad_probs = lax.fori_loop(0, needed, attention_fill, (blank, blank))]
    ppermute x0 -> x142, starting transfers between devices: none -> 96.6 us  [the longest x140 93.7 us: send(): return lax.ppermute(value, BOTH, self.pairs(move))]
    another operation x18 -> x14, local copies, waits for them, and re-layouts: 82.8 us -> 4.1 us  [the longest x4 1.68 us: bundles(): gains = jnp.stack([norm_attn[layer], norm_mlp[layer]], 1)]
  transfers between devices with their start and end apart: 37 -> 142, of which waited for: 24 -> 49; matrix products, arithmetic and copies ran while one was open for 37% -> 4% of each run, Pallas kernels for 0% -> 23%
where the time goes in v1:
time: 757 us; the launch traced here: 747 us
  waiting for transfers between devices  402 us (53%)
  Pallas kernels  206 us (27%)
  starting transfers between devices  96.6 us (13%)
  other arithmetic  23 us (3%)
  local copies, waits for them, and re-layouts  16.5 us (2%)
    ppermute x140, waiting for transfers between devices, send(): return lax.ppermute(value, BOTH, self.pairs(move))  402 us
    pallas_call x12, Pallas kernels, call(): pl.pallas_call(kernel, name=name, out_shape=out_shape, in_specs=in_specs,...  206 us
    ppermute x140, starting transfers between devices, send(): return lax.ppermute(value, BOTH, self.pairs(move))  93.7 us
  transfers between devices with their start and end apart: 142, of which 49 were waited for; matrix products, arithmetic and copies ran while one was open for 4% of the time, Pallas kernels for 23%

profile of v1, /device:TPU:0, one launch (start us, length us, event | category | flops | bytes accessed | tf_op | source)
XLA Modules:
  0.0 746.9 jit_solution(12910434630579603999)
XLA Ops:
  55.0 12.8 %collective-permute-done.53.refs_5_.refs_7_ = bf16[48,2432]{1,0:T(8,128)(2,1)S(1)} collective-permute-done((bf16[48,2432]{1,0:T(8,128)(2,1)S(1)}, bf16[48,2432]{1,0:T(8,128)(2,1)S(1)}, u32[]{:S(2)}, u32[]{:S(2)}) %collective-permute-start.53) | collective-permute-done | bytes 233504 | tf_op jit(solution)/shard_map/ppermute | solution.py:613
  83.0 13.0 %collective-permute-done.39.refs_22_ = bf16[128,768]{1,0:T(8,128)(2,1)} collective-permute-done((bf16[128,768]{1,0:T(8,128)(2,1)}, bf16[128,768]{1,0:T(8,128)(2,1)}, u32[]{:S(2)}, u32[]{:S(2)}) %collective-permute-start.39) | collective-permute-done | bytes 196640 | tf_op jit(solution)/shard_map/ppermute | solution.py:613
  111.9 10.2 %collective-permute-done.51.refs_3_.refs_5_ = bf16[48,2432]{1,0:T(8,128)(2,1)S(1)} collective-permute-done((bf16[48,2432]{1,0:T(8,128)(2,1)S(1)}, bf16[48,2432]{1,0:T(8,128)(2,1)S(1)}, u32[]{:S(2)}, u32[]{:S(2)}) %collective-permute-start.51) | collective-permute-done | bytes 233504 | tf_op jit(solution)/shard_map/ppermute | solution.py:613
  141.7 10.1 %collective-permute-done.23.refs_5_ = bf16[48,4864]{1,0:T(8,128)(2,1)} collective-permute-done((bf16[48,4864]{1,0:T(8,128)(2,1)}, bf16[48,4864]{1,0:T(8,128)(2,1)}, u32[]{:S(2)}, u32[]{:S(2)}) %collective-permute-start.23) | collective-permute-done | bytes 466976 | tf_op jit(solution)/shard_map/ppermute | solution.py:613
  173.1 14.2 %attend.2 = (bf16[512,768]{1,0:T(8,128)(2,1)}, f32[16,512]{1,0:T(8,128)}) custom-call(s32[4]{0:T(128)} %and_select_fusion.low, s32[3]{0:T(128)} %pad_add_fusion.bands, bf16[512,768]{1,0:T(8,128)(2,1)} %get-tuple-element.65.q_ref, s32[8,512]{1,0:T(8,128)} %broadcast_in_dim.10.row_ref, s32[1024,128]{1,0:T(8,128)} %broadcast_in_dim.11.col_ref, ...), custom_call_target="tpu_custom_call" | custom-call | flops 3221225472 | bytes 4718592 | tf_op jit(solution)/shard_map/attend/pallas_call | solution.py:62
  192.4 14.2 %post.2 = (f32[512,768]{1,0:T(8,128)}, f32[512,768]{1,0:T(8,128)}, bf16[512,4096]{1,0:T(8,128)(2,1)}) custom-call(s32[16]{0:T(128)} %stack.207.order, bf16[512,768]{1,0:T(8,128)(2,1)} %collective-permute-done.x_ref, bf16[512,768]{1,0:T(8,128)(2,1)} %get-tuple-element.67.att_ref.out_ref, f32[8,768]{1,0:T(8,128)} %get-tuple-element.68.gains_ref, ...), custom_call_target="tpu_custom_call" | custom-call | flops 5435817984 | bytes 20316160 | tf_op jit(solution)/shard_map/post/pallas_call | solution.py:62
  224.1 11.1 %collective-permute-done.82.refs_19_ = bf16[128,768]{1,0:T(8,128)(2,1)S(1)} collective-permute-done((bf16[128,768]{1,0:T(8,128)(2,1)S(1)}, bf16[128,768]{1,0:T(8,128)(2,1)S(1)}, u32[]{:S(2)}, u32[]{:S(2)}) %collective-permute-start.82) | collective-permute-done | bytes 196640 | tf_op jit(solution)/shard_map/ppermute | solution.py:613
  237.7 14.9 %collective-permute-done.86.refs_23_ = bf16[128,768]{1,0:T(8,128)(2,1)S(1)} collective-permute-done((bf16[128,768]{1,0:T(8,128)(2,1)S(1)}, bf16[128,768]{1,0:T(8,128)(2,1)S(1)}, u32[]{:S(2)}, u32[]{:S(2)}) %collective-permute-start.86) | collective-permute-done | bytes 196640 | tf_op jit(solution)/shard_map/ppermute | solution.py:613
  257.3 9.8 %collective-permute-done.70.refs_6_ = bf16[48,4864]{1,0:T(8,128)(2,1)} collective-permute-done((bf16[48,4864]{1,0:T(8,128)(2,1)}, bf16[48,4864]{1,0:T(8,128)(2,1)}, u32[]{:S(2)}, u32[]{:S(2)}) %collective-permute-start.70) | collective-permute-done | bytes 466976 | tf_op jit(solution)/shard_map/ppermute | solution.py:613
  278.0 14.2 %attend.3 = (bf16[512,768]{1,0:T(8,128)(2,1)}, f32[16,512]{1,0:T(8,128)}) custom-call(s32[4]{0:T(128)} %and_select_fusion.low, s32[3]{0:T(128)} %pad_add_fusion.bands, bf16[512,768]{1,0:T(8,128)(2,1)} %get-tuple-element.70.q_ref, s32[8,512]{1,0:T(8,128)} %broadcast_in_dim.10.row_ref, s32[1024,128]{1,0:T(8,128)} %broadcast_in_dim.11.col_ref, ...), custom_call_target="tpu_custom_call" | custom-call | flops 3221225472 | bytes 4718592 | tf_op jit(solution)/shard_map/attend/pallas_call | solution.py:62
  292.3 14.5 %post.3 = (f32[512,768]{1,0:T(8,128)}, f32[512,768]{1,0:T(8,128)}, bf16[512,4096]{1,0:T(8,128)(2,1)}) custom-call(s32[16]{0:T(128)} %stack.207.order, f32[512,768]{1,0:T(8,128)} %get-tuple-element.69.x_ref, bf16[512,768]{1,0:T(8,128)(2,1)} %get-tuple-element.72.att_ref.out_ref, f32[8,768]{1,0:T(8,128)} %get-tuple-element.73.gains_ref, ...), custom_call_target="tpu_custom_call" | custom-call | flops 5435817984 | bytes 20316160 | tf_op jit(solution)/shard_map/post/pallas_call | solution.py:62
  307.8 33.4 %mlp_back.2 = (f32[512,768]{1,0:T(8,128)}, bf16[512,768]{1,0:T(8,128)(2,1)}, f32[8,768]{1,0:T(8,128)}, bf16[4,48,4864]{2,1,0:T(8,128)(2,1)}, bf16[4,48,4864]{2,1...) custom-call(s32[16]{0:T(128)} %stack.207.order, ...), custom_call_target="tpu_custom_call" | custom-call | flops 10871635968 | bytes 31719424 | tf_op jit(solution)/shard_map/mlp_back/pallas_call | solution.py:62
  345.8 19.0 %attend_back.2 = (bf16[512,768]{1,0:T(8,128)(2,1)}, bf16[512,1536]{1,0:T(8,128)(2,1)}, bf16[512,1536]{1,0:T(8,128)(2,1)}) custom-call(s32[4]{0:T(128)} %and_select_fusion.low, s32[3]{0:T(128)} %pad_add_fusion.bands, bf16[512,768]{1,0:T(8,128)(2,1)} %get-tuple-element.70.q_ref, bf16[512,768]{1,0:T(8,128)(2,1)} %get-tuple-element.77.do_ref, ...), custom_call_target="tpu_custom_call" | custom-call | flops 8053063680 | bytes 9437184 | tf_op jit(solution)/shard_map/attend_back/pallas_call | solution.py:62
  373.6 13.2 %collective-permute-done.137 = bf16[4,128,768]{2,1,0:T(8,128)(2,1)S(1)} collective-permute-done((bf16[4,128,768]{2,1,0:T(8,128)(2,1)S(1)}, bf16[4,128,768]{2,1,0:T(8,128)(2,1)S(1)}, u32[]{:S(2)}, u32[]{:S(2)}) %collective-permute-start.137) | collective-permute-done | bytes 786464 | tf_op jit(solution)/shard_map/ppermute | solution.py:613
  387.1 14.4 %pre_back.2 = (f32[512,768]{1,0:T(8,128)}, bf16[4,48,2432]{2,1,0:T(8,128)(2,1)}, bf16[4,48,2432]{2,1,0:T(8,128)(2,1)}, bf16[4,48,2432]{2,1,0:T(8,128)(2,1)}, bf16[4,48,2432]{2,1,0:T(8,128)(2,1)}) custom-call(s32[16]{0:T(128)} %stack.207.order, s32[16]{0:T(128)} %stack.225.order_g, f32[512,768]{1,0:T(8,128)} %get-tuple-element.69.x_ref, ...), custom_call_target="tpu_custom_call" | custom-call | flops 3623878656 | bytes 15335424 | tf_op jit(solution)/shard_map/pre_back/pallas_call | solution.py:62
  401.5 33.7 %mlp_back.3 = (f32[512,768]{1,0:T(8,128)}, bf16[512,768]{1,0:T(8,128)(2,1)}, f32[8,768]{1,0:T(8,128)}, bf16[4,48,4864]{2,1,0:T(8,128)(2,1)}, bf16[4,48,4864]{2,1...) custom-call(s32[16]{0:T(128)} %stack.207.order, ...), custom_call_target="tpu_custom_call" | custom-call | flops 10871635968 | bytes 31719424 | tf_op jit(solution)/shard_map/mlp_back/pallas_call | solution.py:62
  436.7 19.0 %attend_back.3 = (bf16[512,768]{1,0:T(8,128)(2,1)}, bf16[512,1536]{1,0:T(8,128)(2,1)}, bf16[512,1536]{1,0:T(8,128)(2,1)}) custom-call(s32[4]{0:T(128)} %and_select_fusion.low, s32[3]{0:T(128)} %pad_add_fusion.bands, bf16[512,768]{1,0:T(8,128)(2,1)} %get-tuple-element.65.q_ref, bf16[512,768]{1,0:T(8,128)(2,1)} %get-tuple-element.87.do_ref, ...), custom_call_target="tpu_custom_call" | custom-call | flops 8053063680 | bytes 9437184 | tf_op jit(solution)/shard_map/attend_back/pallas_call | solution.py:62
  480.1 15.8 %collective-permute-done.130 = bf16[4,128,768]{2,1,0:T(8,128)(2,1)S(1)} collective-permute-done((bf16[4,128,768]{2,1,0:T(8,128)(2,1)S(1)}, bf16[4,128,768]{2,1,0:T(8,128)(2,1)S(1)}, u32[]{:S(2)}, u32[]{:S(2)}) %collective-permute-start.130) | collective-permute-done | bytes 786464 | tf_op jit(solution)/shard_map/ppermute | solution.py:613
  498.5 14.2 %pre_back.3 = (f32[512,768]{1,0:T(8,128)}, bf16[4,48,2432]{2,1,0:T(8,128)(2,1)}, bf16[4,48,2432]{2,1,0:T(8,128)(2,1)}, bf16[4,48,2432]{2,1,0:T(8,128)(2,1)}, bf16[4,48,2432]{2,1,0:T(8,128)(2,1)}) custom-call(s32[16]{0:T(128)} %stack.207.order, s32[16]{0:T(128)} %stack.225.order_g, bf16[512,768]{1,0:T(8,128)(2,1)} %collective-permute-done.x_ref, ...), custom_call_target="tpu_custom_call" | custom-call | flops 3623878656 | bytes 15335424 | tf_op jit(solution)/shard_map/pre_back/pallas_call | solution.py:62
  517.1 59.0 %collective-permute-done.109 = bf16[4,48,2432]{2,1,0:T(8,128)(2,1)S(1)} collective-permute-done((bf16[4,48,2432]{2,1,0:T(8,128)(2,1)}, bf16[4,48,2432]{2,1,0:T(8,128)(2,1)S(1)}, u32[]{:S(2)}, u32[]{:S(2)}) %collective-permute-start.109) | collective-permute-done | bytes 933920 | tf_op jit(solution)/shard_map/ppermute | solution.py:613
  630.3 12.2 %collective-permute-done.124 = bf16[48,4864]{1,0:T(8,128)(2,1)S(1)} collective-permute-done((bf16[48,4864]{1,0:T(8,128)(2,1)S(1)}, bf16[48,4864]{1,0:T(8,128)(2,1)S(1)}, u32[]{:S(2)}, u32[]{:S(2)}) %collective-permute-start.124) | collective-permute-done | bytes 466976 | tf_op jit(solution)/shard_map/ppermute | solution.py:613
  649.7 11.6 %collective-permute-done.125 = bf16[48,4864]{1,0:T(8,128)(2,1)S(1)} collective-permute-done((bf16[48,4864]{1,0:T(8,128)(2,1)S(1)}, bf16[48,4864]{1,0:T(8,128)(2,1)S(1)}, u32[]{:S(2)}, u32[]{:S(2)}) %collective-permute-start.125) | collective-permute-done | bytes 466976 | tf_op jit(solution)/shard_map/ppermute | solution.py:613
  661.8 19.4 %collective-permute-done.102 = bf16[4,48,2432]{2,1,0:T(8,128)(2,1)S(1)} collective-permute-done((bf16[4,48,2432]{2,1,0:T(8,128)(2,1)S(1)}, bf16[4,48,2432]{2,1,0:T(8,128)(2,1)S(1)}, u32[]{:S(2)}, u32[]{:S(2)}) %collective-permute-start.102) | collective-permute-done | bytes 933920 | tf_op jit(solution)/shard_map/ppermute | solution.py:613
  700.3 9.7 %collective-permute-done.117 = bf16[48,4864]{1,0:T(8,128)(2,1)S(1)} collective-permute-done((bf16[48,4864]{1,0:T(8,128)(2,1)S(1)}, bf16[48,4864]{1,0:T(8,128)(2,1)S(1)}, u32[]{:S(2)}, u32[]{:S(2)}) %collective-permute-start.117) | collective-permute-done | bytes 466976 | tf_op jit(solution)/shard_map/ppermute | solution.py:613
  (564 shorter events, 330.3 us)
Async XLA Ops:
  110.0 60.5 %collective-permute-start.18 = (bf16[512,1536]{1,0:T(8,128)(2,1)}, bf16[512,1536]{1,0:T(8,128)(2,1)}, u32[]{:S(2)}, u32[]{:S(2)}) collective-permute-start(bf16[512,1536]{1,0:T(8,128)(2,1)} %get-tuple-element.66.refs_0_), channel_id=1, source_target_pairs={{0,2},{1,3},{2,0},{3,1},{4,6},{5,7},{6,4},{7,5},{8,10},{9,11},{10,... | collective-permute-start | bytes 4718600 | tf_op jit(solution)/shard_map/ppermute | solution.py:613
  140.0 30.6 %collective-permute-start.25 = (bf16[48,4864]{1,0:T(8,128)(2,1)S(1)}, bf16[48,4864]{1,0:T(8,128)(2,1)}, u32[]{:S(2)}, u32[]{:S(2)}) collective-permute-start(bf16[48,4864]{1,0:T(8,128)(2,1)S(1)} %collective-permute-done.21.refs_3_), channel_id=1, source_target_pairs={{0,4},{1,5},{2,6},{3,7},{4,0},{5,1},{6,2},{7,3},{8,12},{9,13},{10,... | collective-permute-start | bytes 1400840 | tf_op jit(solution)/shard_map/ppermute | solution.py:613
  151.8 37.2 %collective-permute-start.28 = (bf16[48,4864]{1,0:T(8,128)(2,1)}, bf16[48,4864]{1,0:T(8,128)(2,1)S(1)}, u32[]{:S(2)}, u32[]{:S(2)}) collective-permute-start(bf16[48,4864]{1,0:T(8,128)(2,1)} %collective-permute-done.20.refs_2_), channel_id=1, source_target_pairs={{0,2},{1,3},{2,0},{3,1},{4,6},{5,7},{6,4},{7,5},{8,10},{9,11},{10,... | collective-permute-start | bytes 1400840 | tf_op jit(solution)/shard_map/ppermute | solution.py:613
  151.9 35.6 %collective-permute-start.31 = (bf16[48,4864]{1,0:T(8,128)(2,1)}, bf16[48,4864]{1,0:T(8,128)(2,1)S(1)}, u32[]{:S(2)}, u32[]{:S(2)}) collective-permute-start(bf16[48,4864]{1,0:T(8,128)(2,1)} %collective-permute-done.23.refs_5_), channel_id=1, source_target_pairs={{0,2},{1,3},{2,0},{3,1},{4,6},{5,7},{6,4},{7,5},{8,10},{9,11},{10,... | collective-permute-start | bytes 1400840 | tf_op jit(solution)/shard_map/ppermute | solution.py:613
  187.5 29.5 %collective-permute-start.72 = (bf16[48,4864]{1,0:T(8,128)(2,1)S(1)}, bf16[48,4864]{1,0:T(8,128)(2,1)S(1)}, u32[]{:S(2)}, u32[]{:S(2)}) collective-permute-start(bf16[48,4864]{1,0:T(8,128)(2,1)S(1)} %pad_maximum_fusion.4.refs_0_), channel_id=1, source_target_pairs={{0,2},{1,3},{2,0},{3,1},{4,6},{5,7},{6,4},{7,5},{8,10},{9,11},{10,... | collective-permute-start | bytes 1400840 | tf_op jit(solution)/shard_map/ppermute | solution.py:613
  216.0 60.9 %collective-permute-start.64 = (bf16[512,1536]{1,0:T(8,128)(2,1)}, bf16[512,1536]{1,0:T(8,128)(2,1)S(1)}, u32[]{:S(2)}, u32[]{:S(2)}) collective-permute-start(bf16[512,1536]{1,0:T(8,128)(2,1)} %get-tuple-element.71.refs_0_), channel_id=1, source_target_pairs={{0,2},{1,3},{2,0},{3,1},{4,6},{5,7},{6,4},{7,5},{8,10},{9,11},{10,... | collective-permute-start | bytes 4718600 | tf_op jit(solution)/shard_map/ppermute | solution.py:613
  256.7 35.6 %collective-permute-start.74 = (bf16[48,4864]{1,0:T(8,128)(2,1)}, bf16[48,4864]{1,0:T(8,128)(2,1)}, u32[]{:S(2)}, u32[]{:S(2)}) collective-permute-start(bf16[48,4864]{1,0:T(8,128)(2,1)} %collective-permute-done.66.refs_2_), channel_id=1, source_target_pairs={{0,2},{1,3},{2,0},{3,1},{4,6},{5,7},{6,4},{7,5},{8,10},{9,11},{10,... | collective-permute-start | bytes 1400840 | tf_op jit(solution)/shard_map/ppermute | solution.py:613
  256.8 35.4 %collective-permute-start.75 = (bf16[48,4864]{1,0:T(8,128)(2,1)}, bf16[48,4864]{1,0:T(8,128)(2,1)}, u32[]{:S(2)}, u32[]{:S(2)}) collective-permute-start(bf16[48,4864]{1,0:T(8,128)(2,1)} %collective-permute-done.67.refs_3_), channel_id=1, source_target_pairs={{0,2},{1,3},{2,0},{3,1},{4,6},{5,7},{6,4},{7,5},{8,10},{9,11},{10,... | collective-permute-start | bytes 1400840 | tf_op jit(solution)/shard_map/ppermute | solution.py:613
  276.9 29.9 %collective-permute-start.96 = (bf16[512,768]{1,0:T(8,128)(2,1)S(1)}, bf16[512,768]{1,0:T(8,128)(2,1)S(1)}, u32[]{:S(2)}, u32[]{:S(2)}) collective-permute-start(bf16[512,768]{1,0:T(8,128)(2,1)S(1)} %bitcast.240), channel_id=1, source_target_pairs={{0,0},{1,2},{2,1},{3,3},{4,4},{5,6},{6,5},{7,7},{8,8},{9,10},{10,9... | collective-permute-start | bytes 2359304 | tf_op jit(solution)/shard_map/ppermute | solution.py:613
  368.6 66.6 %collective-permute-start.95 = (f32[512,768]{1,0:T(8,128)}, f32[512,768]{1,0:T(8,128)S(1)}, u32[]{:S(2)}, u32[]{:S(2)}) collective-permute-start(f32[512,768]{1,0:T(8,128)} %get-tuple-element.74), channel_id=1, source_target_pairs={{0,0},{2,1},{1,2},{3,3},{4,4},{6,5},{5,6},{7,7},{8,8},{10,9},{9,10... | collective-permute-start | bytes 4718600 | tf_op jit(solution)/shard_map/ppermute | solution.py:639
  370.7 222.1 %collective-permute-start.121 = (bf16[4,48,4864]{2,1,0:T(8,128)(2,1)}, bf16[4,48,4864]{2,1,0:T(8,128)(2,1)S(1)}, u32[]{:S(2)}, u32[]{:S(2)}) collective-permute-start(bf16[4,48,4864]{2,1,0:T(8,128)(2,1)} %get-tuple-element.108), channel_id=1, source_target_pairs={{0,2},{1,3},{2,0},{3,1},{4,6},{5,7},{6,4},{7,5},{8,10},{9,11},{10,... | collective-permute-start | bytes 5603336 | tf_op jit(solution)/shard_map/ppermute | solution.py:613
  373.5 84.1 %collective-permute-start.122 = (bf16[4,48,4864]{2,1,0:T(8,128)(2,1)}, bf16[4,48,4864]{2,1,0:T(8,128)(2,1)S(1)}, u32[]{:S(2)}, u32[]{:S(2)}) collective-permute-start(bf16[4,48,4864]{2,1,0:T(8,128)(2,1)} %get-tuple-element.110), channel_id=1, source_target_pairs={{0,2},{1,3},{2,0},{3,1},{4,6},{5,7},{6,4},{7,5},{8,10},{9,11},{10,... | collective-permute-start | bytes 5603336 | tf_op jit(solution)/shard_map/ppermute | solution.py:613
  387.0 48.8 %collective-permute-start.138 = (bf16[128,768]{1,0:T(8,128)(2,1)S(1)}, bf16[128,768]{1,0:T(8,128)(2,1)S(1)}, u32[]{:S(2)}, u32[]{:S(2)}) collective-permute-start(bf16[128,768]{1,0:T(8,128)(2,1)S(1)} %fusion.45), channel_id=1, source_target_pairs={{0,8},{1,9},{2,10},{3,11},{4,12},{5,13},{6,14},{7,15},{8,16},{9,17... | collective-permute-start | bytes 589832 | tf_op jit(solution)/shard_map/ppermute | solution.py:613
  435.3 44.4 %collective-permute-start.128 = (bf16[4,128,768]{2,1,0:T(8,128)(2,1)}, bf16[4,128,768]{2,1,0:T(8,128)(2,1)}, u32[]{:S(2)}, u32[]{:S(2)}) collective-permute-start(bf16[4,128,768]{2,1,0:T(8,128)(2,1)} %get-tuple-element.112), channel_id=1, source_target_pairs={{0,2},{1,3},{2,0},{3,1},{4,6},{5,7},{6,4},{7,5},{8,10},{9,11},{10,... | collective-permute-start | bytes 2359304 | tf_op jit(solution)/shard_map/ppermute | solution.py:613
  435.3 31.2 %collective-permute-start.129 = (bf16[4,128,768]{2,1,0:T(8,128)(2,1)}, bf16[4,128,768]{2,1,0:T(8,128)(2,1)S(1)}, u32[]{:S(2)}, u32[]{:S(2)}) collective-permute-start(bf16[4,128,768]{2,1,0:T(8,128)(2,1)} %get-tuple-element.114), channel_id=1, source_target_pairs={{0,2},{1,3},{2,0},{3,1},{4,6},{5,7},{6,4},{7,5},{8,10},{9,11},{10,... | collective-permute-start | bytes 2359304 | tf_op jit(solution)/shard_map/ppermute | solution.py:613
  466.5 30.9 %collective-permute-start.98 = (bf16[512,1536]{1,0:T(8,128)(2,1)S(1)}, bf16[512,1536]{1,0:T(8,128)(2,1)S(1)}, u32[]{:S(2)}, u32[]{:S(2)}) collective-permute-start(bf16[512,1536]{1,0:T(8,128)(2,1)S(1)} %copy-done.25), channel_id=1, source_target_pairs={{0,2},{1,3},{2,0},{3,1},{4,6},{5,7},{6,4},{7,5},{8,10},{9,11},{10,... | collective-permute-start | bytes 4718600 | tf_op jit(solution)/shard_map/ppermute | solution.py:613
  478.4 36.2 %collective-permute-start.115 = (bf16[4,48,4864]{2,1,0:T(8,128)(2,1)}, bf16[4,48,4864]{2,1,0:T(8,128)(2,1)}, u32[]{:S(2)}, u32[]{:S(2)}) collective-permute-start(bf16[4,48,4864]{2,1,0:T(8,128)(2,1)} %get-tuple-element.106), channel_id=1, source_target_pairs={{0,2},{1,3},{2,0},{3,1},{4,6},{5,7},{6,4},{7,5},{8,10},{9,11},{10,... | collective-permute-start | bytes 5603336 | tf_op jit(solution)/shard_map/ppermute | solution.py:613
  479.6 37.4 %collective-permute-start.107 = (bf16[4,48,2432]{2,1,0:T(8,128)(2,1)}, bf16[4,48,2432]{2,1,0:T(8,128)(2,1)}, u32[]{:S(2)}, u32[]{:S(2)}) collective-permute-start(bf16[4,48,2432]{2,1,0:T(8,128)(2,1)} %get-tuple-element.100), channel_id=1, source_target_pairs={{0,2},{1,3},{2,0},{3,1},{4,6},{5,7},{6,4},{7,5},{8,10},{9,11},{10,... | collective-permute-start | bytes 2801672 | tf_op jit(solution)/shard_map/ppermute | solution.py:613
  495.9 193.6 %collective-permute-start.114 = (bf16[4,48,4864]{2,1,0:T(8,128)(2,1)}, bf16[4,48,4864]{2,1,0:T(8,128)(2,1)S(1)}, u32[]{:S(2)}, u32[]{:S(2)}) collective-permute-start(bf16[4,48,4864]{2,1,0:T(8,128)(2,1)} %get-tuple-element.104), channel_id=1, source_target_pairs={{0,2},{1,3},{2,0},{3,1},{4,6},{5,7},{6,4},{7,5},{8,10},{9,11},{10,... | collective-permute-start | bytes 5603336 | tf_op jit(solution)/shard_map/ppermute | solution.py:613
  512.7 80.8 %collective-permute-start.123 = (bf16[4,48,4864]{2,1,0:T(8,128)(2,1)}, bf16[4,48,4864]{2,1,0:T(8,128)(2,1)S(1)}, u32[]{:S(2)}, u32[]{:S(2)}) collective-permute-start(bf16[4,48,4864]{2,1,0:T(8,128)(2,1)} %add_convert_fusion), channel_id=1, source_target_pairs={{0,4},{1,5},{2,6},{3,7},{4,0},{5,1},{6,2},{7,3},{8,12},{9,13},{10,... | collective-permute-start | bytes 5603336 | tf_op jit(solution)/shard_map/ppermute | solution.py:613
  514.6 61.6 %collective-permute-start.109 = (bf16[4,48,2432]{2,1,0:T(8,128)(2,1)}, bf16[4,48,2432]{2,1,0:T(8,128)(2,1)S(1)}, u32[]{:S(2)}, u32[]{:S(2)}) collective-permute-start(bf16[4,48,2432]{2,1,0:T(8,128)(2,1)} %add_convert_fusion.2), channel_id=1, source_target_pairs={{0,4},{1,5},{2,6},{3,7},{4,0},{5,1},{6,2},{7,3},{8,12},{9,13},{10,... | collective-permute-start | bytes 2801672 | tf_op jit(solution)/shard_map/ppermute | solution.py:613
  517.0 144.7 %collective-permute-start.100 = (bf16[4,48,2432]{2,1,0:T(8,128)(2,1)S(1)}, bf16[4,48,2432]{2,1,0:T(8,128)(2,1)S(1)}, u32[]{:S(2)}, u32[]{:S(2)}) collective-permute-start(bf16[4,48,2432]{2,1,0:T(8,128)(2,1)S(1)} %copy-done.27), channel_id=1, source_target_pairs={{0,2},{1,3},{2,0},{3,1},{4,6},{5,7},{6,4},{7,5},{8,10},{9,11},{10,... | collective-permute-start | bytes 2801672 | tf_op jit(solution)/shard_map/ppermute | solution.py:613
  592.8 68.9 %collective-permute-start.99 = (f32[512,768]{1,0:T(8,128)S(1)}, f32[512,768]{1,0:T(8,128)S(1)}, u32[]{:S(2)}, u32[]{:S(2)}) collective-permute-start(f32[512,768]{1,0:T(8,128)S(1)} %copy-done.24), channel_id=1, source_target_pairs={{0,0},{2,1},{1,2},{3,3},{4,4},{6,5},{5,6},{7,7},{8,8},{10,9},{9,10... | collective-permute-start | bytes 4718600 | tf_op jit(solution)/shard_map/ppermute | solution.py:639
  619.4 70.1 %collective-permute-start.116 = (bf16[4,48,4864]{2,1,0:T(8,128)(2,1)S(1)}, bf16[4,48,4864]{2,1,0:T(8,128)(2,1)S(1)}, u32[]{:S(2)}, u32[]{:S(2)}) collective-permute-start(bf16[4,48,4864]{2,1,0:T(8,128)(2,1)S(1)} %add_convert_fusion.1), channel_id=1, source_target_pairs={{0,4},{1,5},{2,6},{3,7},{4,0},{5,1},{6,2},{7,3},{8,12},{9,13},{10,... | collective-permute-start | bytes 5603336 | tf_op jit(solution)/shard_map/ppermute | solution.py:613
  (219 other events, 4082.0 us)

commit v2 on v1

--- a/solution.py
+++ b/solution.py
@@ -22,6 +22,15 @@
 VMEM_BYTES = 56 * 1024 * 1024
 Q_TILE = 128
 K_TILE = 256
+FLOPS_PER_US = 1.1e9
+IN_PARTS = (
+    ([(1.0, "whole")], [(0.5, "whole"), (0.5, "half")], [(1.0, "half")]),
+    ([(1.0, "half")], [(1.0, "whole")], [(1.0, "half")]),
+)
+OUT_PARTS = (
+    ([(0.5, "whole"), (0.5, "half")], [(1.0, "offload")], [(1.0, "half")]),
+    ([(1.0, "half")], [(1.0, "offload")], [(1.0, "half")]),
+)
 
 
 def dot(left, right):
@@ -37,38 +46,61 @@
     return jnp.where(lane % 64 < 32, pltpu.roll(block, 96, 1), pltpu.roll(block, 32, 1))
 
 
-def start_weights(order, refs, held, sem):
-    rows = refs[0].shape[0]
-    for index, ref in enumerate(refs):
-        at = pl.multiple_of(order[index] * rows, 16)
-        pltpu.make_async_copy(ref, held.at[pl.ds(at, rows), :], sem).start()
-
-
-def wait_whole(held, sem):
-    pltpu.make_async_copy(held, held, sem).wait()
-
-
-def send_out(order, whole, refs, sem):
+def place(table, index, rows, cols, whole):
+    at = pl.ds(pl.multiple_of(table[0, index] * rows, 16), rows)
+    if cols == whole.shape[1]:
+        return whole.at[at, :]
+    return whole.at[at, pl.ds(pl.multiple_of(table[1, index] * 128, 128), cols)]
+
+
+def start_weights(table, refs, held, sem):
     index = 0
     for ref in refs:
         for part in range(ref.shape[0]):
-            rows = ref.shape[1]
-            at = pl.multiple_of(order[index] * rows, 16)
-            pltpu.make_async_copy(whole.at[pl.ds(at, rows), :], ref.at[part], sem).start()
+            target = place(table, index, ref.shape[1], ref.shape[2], held)
+            pltpu.make_async_copy(ref.at[part], target, sem).start()
             index += 1
 
 
-def call(kernel, name, out_shape, in_specs, out_specs, scratch, args, flops, nbytes):
-    return pl.pallas_call(
-        kernel,
+def wait_whole(held, sem):
+    pltpu.make_async_copy(held, held, sem).wait()
+
+
+def send_out(table, whole, refs, sem):
+    index = 0
+    for ref in refs:
+        for part in range(ref.shape[0]):
+            source = place(table, index, ref.shape[1], ref.shape[2], whole)
+            pltpu.make_async_copy(source, ref.at[part], sem).start()
+            index += 1
+
+
+def call(kernel, name, out_shape, in_specs, out_specs, scratch, args, micros, ride=(), before=()):
+    n_in, n_out, n_ride = len(in_specs), len(out_specs), len(ride)
+    n_more = n_ride + len(before)
+
+    def wrapped(*refs):
+        outs_at = n_in + n_more
+        kernel(*refs[:n_in], *refs[outs_at : outs_at + n_out], *refs[outs_at + n_out + n_ride :])
+
+    results = pl.pallas_call(
+        wrapped,
         name=name,
-        out_shape=out_shape,
-        in_specs=in_specs,
-        out_specs=out_specs,
+        out_shape=(*out_shape, *(jax.ShapeDtypeStruct(a.shape, a.dtype) for a in ride)),
+        in_specs=[*in_specs, *([ANY] * n_more)],
+        out_specs=(*out_specs, *([ANY] * n_ride)),
         scratch_shapes=scratch,
+        input_output_aliases={n_in + i: n_out + i for i in range(n_ride)},
         compiler_params=pltpu.CompilerParams(vmem_limit_bytes=VMEM_BYTES),
-        cost_estimate=pl.CostEstimate(flops=flops, bytes_accessed=nbytes, transcendentals=0),
-    )(*args)
+        cost_estimate=pl.CostEstimate(
+            flops=int(micros * FLOPS_PER_US), bytes_accessed=0, transcendentals=0
+        ),
+    )(*args, *ride, *before)
+    return results[:n_out], list(results[n_out:])
+
+
+def qkv_cols(width):
+    return 3 * width + 256
 
 
 def row_tile(tokens):
@@ -108,9 +140,9 @@
     lax.fori_loop(0, tokens // tile, body, 0)
 
 
-def pre(order, x, cosine, sine, weights):
+def pre(order, x, cosine, sine, weights, ride=(), before=()):
     tokens, width = x.shape
-    cols = weights[0].shape[1]
+    cols = qkv_cols(width)
     return call(
         functools.partial(pre_kernel, len(weights)),
         "pre",
@@ -127,9 +159,20 @@
             pltpu.SemaphoreType.DMA,
         ],
         (order, x, cosine, sine, *weights),
-        2 * tokens * width * 3 * width,
-        width * cols * 2 + tokens * width * 10,
+        7,
+        ride,
+        before,
     )
+
+
+def gate_kernel(done_ref):
+    done_ref[...] = jnp.zeros_like(done_ref)
+
+
+def gate(before, ride):
+    return call(
+        gate_kernel, "gate", (jax.ShapeDtypeStruct((8, 128), F32),), [], (VMEM,), [], (), 0, ride, before
+    )[1]
 
 
 def load_bands(bands, kv_refs, kv_s, sem):
@@ -223,7 +266,7 @@
     lax.fori_loop(0, tokens // Q_TILE, q_step, 0)
 
 
-def attend(low, bands, queries, mark_row, mark_col, kv_list, total):
+def attend(low, bands, queries, mark_row, mark_col, kv_list, total, ride=(), before=()):
     tokens, width = queries.shape
     return call(
         functools.partial(attend_kernel, len(kv_list)),
@@ -243,18 +286,19 @@
             pltpu.SemaphoreType.DMA,
         ],
         (low, bands, queries, mark_row, mark_col, *kv_list),
-        8 * tokens * total * width,
-        total * width * 4 + tokens * width * 4,
+        15,
+        ride,
+        before,
     )
 
 
-def post_kernel(n_w, order, x_ref, att_ref, gains_ref, *refs):
-    a_refs, d_refs = refs[:n_w], refs[n_w : 2 * n_w]
-    out_ref, mid_ref, gu_ref, a_s, d_s, act_s, sem_a, sem_d = refs[2 * n_w :]
+def post_kernel(n_a, n_d, order_a, order_d, x_ref, att_ref, gains_ref, *refs):
+    a_refs, d_refs = refs[:n_a], refs[n_a : n_a + n_d]
+    out_ref, mid_ref, gu_ref, a_s, d_s, act_s, sem_a, sem_d = refs[n_a + n_d :]
     tokens, width = x_ref.shape
     ff = d_s.shape[0]
-    start_weights(order, a_refs, a_s, sem_a)
-    start_weights(order, d_refs, d_s, sem_d)
+    start_weights(order_a, a_refs, a_s, sem_a)
+    start_weights(order_d, d_refs, d_s, sem_d)
     wait_whole(a_s, sem_a)
     wait_whole(d_s, sem_d)
     gain = gains_ref[1:2, :]
@@ -278,19 +322,18 @@
     lax.fori_loop(0, tokens // tile, body, 0)
 
 
-def post(order, x, attended, gains, w_a, w_d):
+def post(order_a, order_d, ff, x, attended, gains, w_a, w_d, ride=(), before=()):
     tokens, width = x.shape
-    cols = w_a[0].shape[1]
-    ff = (cols - width) // 2
+    cols = width + 2 * ff
     return call(
-        functools.partial(post_kernel, len(w_a)),
+        functools.partial(post_kernel, len(w_a), len(w_d)),
         "post",
         (
             jax.ShapeDtypeStruct((tokens, width), F32),
             jax.ShapeDtypeStruct((tokens, width), F32),
             jax.ShapeDtypeStruct((tokens, 2 * ff), BF16),
         ),
-        [SMEM, VMEM, VMEM, VMEM] + [ANY] * (2 * len(w_a)),
+        [SMEM, SMEM, VMEM, VMEM, VMEM] + [ANY] * (len(w_a) + len(w_d)),
         (VMEM, VMEM, VMEM),
         [
             pltpu.VMEM((width, cols), BF16),
@@ -299,55 +342,104 @@
             pltpu.SemaphoreType.DMA,
             pltpu.SemaphoreType.DMA,
         ],
-        (order, x, attended, gains, *w_a, *w_d),
-        2 * tokens * width * (cols + ff),
-        (width * cols + ff * width) * 2 + tokens * width * 14 + tokens * ff * 4,
+        (order_a, order_d, x, attended, gains, *w_a, *w_d),
+        14,
+        ride,
+        before,
     )
 
 
-def mlp_back_kernel(n_w, n_g, order, order_g, flow_ref, mid_ref, gu_ref, att_ref, gains_ref, *refs):
-    a_refs, d_refs = refs[:n_w], refs[n_w : 2 * n_w]
-    refs = refs[2 * n_w :]
-    dmid_ref, datt_ref, ggain_ref = refs[:3]
-    ga_refs, gd_refs = refs[3 : 3 + n_g], refs[3 + n_g : 3 + 2 * n_g]
-    a_s, d_s, actt_s, db_s, dgu_s, hidt_s, attt_s, dattn_s, ga_s, gd_s, sem_a, sem_d = refs[
-        3 + 2 * n_g :
-    ]
+def mlp_back_kernel(
+    counts, order_d, table_a, table_d, flow_ref, mid_ref, gu_ref, gains_ref, *refs
+):
+    n_d, n_ga, n_gd = counts
+    d_refs, refs = refs[:n_d], refs[n_d:]
+    dgu_ref, ga_refs, gd_refs = refs[0], refs[1 : 1 + n_ga], refs[1 + n_ga : 1 + n_ga + n_gd]
+    d_s, actt_s, db_s, hidt_s, ga_s, gd_s, sem_a, sem_d = refs[1 + n_ga + n_gd :]
     tokens, width = mid_ref.shape
     ff = d_s.shape[0]
-    start_weights(order, d_refs, d_s, sem_d)
-    start_weights(order, a_refs, a_s, sem_a)
+    start_weights(order_d, d_refs, d_s, sem_d)
     gain = gains_ref[1:2, :]
     tile = row_tile(tokens)
-    wait_whole(d_s, sem_d)
-    wait_whole(a_s, sem_a)
-    ggain = jnp.zeros((1, width), F32)
     for start in range(0, tokens, tile):
         at = slice(start, start + tile)
-        low_flow = flow_ref[at, :].astype(BF16)
-        db_s[at, :] = low_flow
-
-        def columns(step, carry, at=at, low_flow=low_flow):
-            col = pl.multiple_of(step * 256, 256)
-            d_act = dot_nt(low_flow, d_s[pl.ds(col, 256), :])
+        db_s[at, :] = flow_ref[at, :].astype(BF16)
+        mid = mid_ref[at, :]
+        factor = lax.rsqrt(jnp.mean(mid * mid, -1, keepdims=True) + EPS)
+        hidt_s[:, at] = (mid * factor * gain).T.astype(BF16)
+    wait_whole(d_s, sem_d)
+
+    def columns(step, carry):
+        col = pl.multiple_of(step * 256, 256)
+        for start in range(0, tokens, tile):
+            at = slice(start, start + tile)
+            d_act = dot_nt(db_s[at, :], d_s[pl.ds(col, 256), :])
             gate = gu_ref[at, pl.ds(col, 256)].astype(F32)
             up = gu_ref[at, pl.ds(ff + col, 256)].astype(F32)
             sigma = jax.nn.sigmoid(gate)
             silu = gate * sigma
             actt_s[pl.ds(col, 256), at] = (silu * up).T.astype(BF16)
-            dgu_s[at, pl.ds(col, 256)] = (
+            dgu_ref[at, pl.ds(col, 256)] = (
                 d_act * up * (sigma * (1.0 + gate * (1.0 - sigma)))
             ).astype(BF16)
-            dgu_s[at, pl.ds(ff + col, 256)] = (d_act * silu).astype(BF16)
-            return carry
-
-        lax.fori_loop(0, ff // 256, columns, 0)
+            dgu_ref[at, pl.ds(ff + col, 256)] = (d_act * silu).astype(BF16)
+        for first in (0, ff):
+            ga_s[:, pl.ds(first + col, 256)] = dot(
+                hidt_s[...], dgu_ref[:, pl.ds(first + col, 256)]
+            ).astype(BF16)
+        rows = pl.ds(col, 256)
+        gd_s[rows, :] = dot(actt_s[rows, :], db_s[...]).astype(BF16)
+        return carry
+
+    lax.fori_loop(0, ff // 256, columns, 0)
+    send_out(table_a, ga_s, ga_refs, sem_a)
+    send_out(table_d, gd_s, gd_refs, sem_d)
+    wait_whole(ga_s, sem_a)
+    wait_whole(gd_s, sem_d)
+
+
+def mlp_back(order_d, tables, shapes, flow, mid, gu, gains, w_d, ride=(), before=()):
+    tokens, width = mid.shape
+    ff = gu.shape[1] // 2
+    ga, gd = shapes
+    return call(
+        functools.partial(mlp_back_kernel, (len(w_d), len(ga), len(gd))),
+        "mlp_back",
+        (jax.ShapeDtypeStruct((tokens, 2 * ff), BF16), *ga, *gd),
+        [SMEM] * 3 + [VMEM] * 4 + [ANY] * len(w_d),
+        (VMEM, *([ANY] * (len(ga) + len(gd)))),
+        [
+            pltpu.VMEM((ff, width), BF16),
+            pltpu.VMEM((ff, tokens), BF16),
+            pltpu.VMEM((tokens, width), BF16),
+            pltpu.VMEM((width, tokens), BF16),
+            pltpu.VMEM((width, 2 * ff), BF16),
+            pltpu.VMEM((ff, width), BF16),
+            pltpu.SemaphoreType.DMA,
+            pltpu.SemaphoreType.DMA,
+        ],
+        (order_d, *tables, flow, mid, gu, gains, *w_d),
+        20,
+        ride,
+        before,
+    )
+
+
+def mid_back_kernel(n_a, order_a, flow_ref, mid_ref, dgu_ref, gains_ref, *refs):
+    a_refs = refs[:n_a]
+    dmid_ref, dattn_ref, datt_ref, ggain_ref, a_s, sem = refs[n_a:]
+    tokens, width = mid_ref.shape
+    start_weights(order_a, a_refs, a_s, sem)
+    gain = gains_ref[1:2, :]
+    tile = row_tile(tokens)
+    wait_whole(a_s, sem)
+    ggain = jnp.zeros((1, width), F32)
+    for start in range(0, tokens, tile):
+        at = slice(start, start + tile)
         mid = mid_ref[at, :]
         factor = lax.rsqrt(jnp.mean(mid * mid, -1, keepdims=True) + EPS)
         normed = mid * factor
-        hidt_s[:, at] = (normed * gain).T.astype(BF16)
-        attt_s[:, at] = att_ref[at, :].astype(F32).T.astype(BF16)
-        d_hid = dot_nt(dgu_s[at, :], a_s[:, width:])
+        d_hid = dot_nt(dgu_ref[at, :], a_s[:, width:])
         ggain = ggain + jnp.sum(d_hid * normed, 0, keepdims=True)
         shaped = d_hid * gain
         d_mid = flow_ref[at, :].astype(F32) + factor * (
@@ -355,66 +447,32 @@
         )
         dmid_ref[at, :] = d_mid
         d_attn = d_mid.astype(BF16)
-        dattn_s[at, :] = d_attn
+        dattn_ref[at, :] = d_attn
         datt_ref[at, :] = dot_nt(d_attn, a_s[:, :width]).astype(BF16)
     ggain_ref[...] = jnp.broadcast_to(ggain, ggain_ref.shape)
 
-    def down_rows(step, carry):
-        at = pl.ds(pl.multiple_of(step * 256, 256), 256)
-        gd_s[at, :] = dot(actt_s[at, :], db_s[...]).astype(BF16)
-        return carry
-
-    lax.fori_loop(0, ff // 256, down_rows, 0)
-    send_out(order_g, gd_s, gd_refs, sem_d)
-    ga_s[:, :width] = dot(attt_s[...], dattn_s[...]).astype(BF16)
-
-    def gu_columns(step, carry):
-        col = pl.multiple_of(step * 256, 256)
-        ga_s[:, pl.ds(width + col, 256)] = dot(hidt_s[...], dgu_s[:, pl.ds(col, 256)]).astype(BF16)
-        return carry
-
-    lax.fori_loop(0, 2 * ff // 256, gu_columns, 0)
-    send_out(order_g, ga_s, ga_refs, sem_a)
-    wait_whole(gd_s, sem_d)
-    wait_whole(ga_s, sem_a)
-
-
-def mlp_back(order, order_g, parts, flow, mid, gu, attended, gains, w_a, w_d):
+
+def mid_back(order_a, flow, mid, dgu, gains, w_a, ride=(), before=()):
     tokens, width = mid.shape
-    cols = w_a[0].shape[1]
-    ff = (cols - width) // 2
-    n_g, per, pieces = parts
-    ga = jax.ShapeDtypeStruct((per, width // pieces, cols), BF16)
-    gd = jax.ShapeDtypeStruct((per, ff // pieces, width), BF16)
     return call(
-        functools.partial(mlp_back_kernel, len(w_a), n_g),
-        "mlp_back",
+        functools.partial(mid_back_kernel, len(w_a)),
+        "mid_back",
         (
             jax.ShapeDtypeStruct((tokens, width), F32),
             jax.ShapeDtypeStruct((tokens, width), BF16),
+            jax.ShapeDtypeStruct((tokens, width), BF16),
             jax.ShapeDtypeStruct((8, width), F32),
-            *([ga] * n_g),
-            *([gd] * n_g),
         ),
-        [SMEM, SMEM] + [VMEM] * 5 + [ANY] * (2 * len(w_a)),
-        (VMEM, VMEM, VMEM, *([ANY] * (2 * n_g))),
+        [SMEM] + [VMEM] * 4 + [ANY] * len(w_a),
+        (VMEM, VMEM, VMEM, VMEM),
         [
-            pltpu.VMEM((width, cols), BF16),
-            pltpu.VMEM((ff, width), BF16),
-            pltpu.VMEM((ff, tokens), BF16),
-            pltpu.VMEM((tokens, width), BF16),
-            pltpu.VMEM((tokens, 2 * ff), BF16),
-            pltpu.VMEM((width, tokens), BF16),
-            pltpu.VMEM((width, tokens), BF16),
-            pltpu.VMEM((tokens, width), BF16),
-            pltpu.VMEM((width, cols), BF16),
-            pltpu.VMEM((ff, width), BF16),
-            pltpu.SemaphoreType.DMA,
+            pltpu.VMEM((width, width + dgu.shape[1]), BF16),
             pltpu.SemaphoreType.DMA,
         ],
-        (order, order_g, flow, mid, gu, attended, gains, *w_a, *w_d),
-        4 * tokens * width * (cols + ff),
-        (width * cols + ff * width) * 4 + tokens * width * 16 + tokens * ff * 4,
+        (order_a, flow, mid, dgu, gains, *w_a),
+        13,
+        ride,
+        before,
     )
 
 
@@ -490,7 +548,7 @@
     wait_whole(dlow_s, sem)
 
 
-def attend_back(low, bands, queries, d_out, out, lse, mark_row, mark_col, cosine, sine, kv_list, total):
+def attend_back(low, bands, queries, d_out, out, lse, mark_row, mark_col, cosine, sine, kv_list, total, ride=(), before=()):
     tokens, width = queries.shape
     n_kv = len(kv_list)
     return call(
@@ -512,18 +570,33 @@
             pltpu.SemaphoreType.DMA,
         ],
         (low, bands, queries, d_out, out, lse, mark_row, mark_col, cosine, sine, *kv_list),
-        20 * tokens * total * width,
-        total * width * 8 + tokens * width * 8,
+        20,
+        ride,
+        before,
     )
 
 
 def pre_back_kernel(
-    n_w, n_g, n_kv, order, order_g, x_ref, dq_ref, cos_ref, sin_ref, gains_ref, dmid_ref, ggain_ref, *refs
+    n_w,
+    n_g,
+    n_kv,
+    order,
+    table,
+    x_ref,
+    dq_ref,
+    cos_ref,
+    sin_ref,
+    gains_ref,
+    dmid_ref,
+    ggain_ref,
+    att_ref,
+    dattn_ref,
+    *refs,
 ):
     dkv_refs, w_refs = refs[:n_kv], refs[n_kv : n_kv + n_w]
     refs = refs[n_kv + n_w :]
     flow_ref, g_refs = refs[0], refs[1 : 1 + n_g]
-    w_s, hidt_s, dqkv_s, g_s, sem = refs[1 + n_g :]
+    w_s, hidt_s, dqkv_s, attt_s, g_s, sem = refs[1 + n_g :]
     tokens, width = x_ref.shape
     start_weights(order, w_refs, w_s, sem)
     gain = gains_ref[0:1, :]
@@ -536,6 +609,7 @@
         factor = lax.rsqrt(jnp.mean(x * x, -1, keepdims=True) + EPS)
         normed = x * factor
         hidt_s[:, at] = (normed * gain).T.astype(BF16)
+        attt_s[:, at] = att_ref[at, :].astype(F32).T.astype(BF16)
         cosine, sine = cos_ref[at, :], sin_ref[at, :]
         dqkv_s[at, :width] = dq_ref[at, :]
         for col in range(0, 2 * width, 128):
@@ -553,7 +627,9 @@
         )
     row = lax.broadcasted_iota(jnp.int32, (128, width), 0)
     both = jnp.where(row == 0, ggain, jnp.where(row == 1, ggain_ref[0:1, :], 0.0))
-    g_s[:, 3 * width :] = both.T.astype(BF16)
+    g_s[:, 4 * width : 4 * width + 128] = both.T.astype(BF16)
+    g_s[:, 4 * width + 128 :] = jnp.zeros((width, 128), BF16)
+    g_s[:, 3 * width : 4 * width] = dot(attt_s[...], dattn_ref[...]).astype(BF16)
 
     def columns(step, carry):
         col = pl.multiple_of(step * 256, 256)
@@ -561,33 +637,61 @@
         return carry
 
     lax.fori_loop(0, 3 * width // 256, columns, 0)
-    send_out(order_g, g_s, g_refs, sem)
+    send_out(table, g_s, g_refs, sem)
     wait_whole(g_s, sem)
 
 
-def pre_back(order, order_g, parts, x, dq, cosine, sine, gains, d_mid, ggain, dkv_list, weights):
+def pre_back(
+    order,
+    table,
+    shapes,
+    x,
+    dq,
+    cosine,
+    sine,
+    gains,
+    d_mid,
+    ggain,
+    attended,
+    d_attn,
+    dkv_list,
+    weights,
+    ride=(),
+    before=(),
+):
     tokens, width = x.shape
-    cols = weights[0].shape[1]
-    n_g, per, pieces = parts
     return call(
-        functools.partial(pre_back_kernel, len(weights), n_g, len(dkv_list)),
+        functools.partial(pre_back_kernel, len(weights), len(shapes), len(dkv_list)),
         "pre_back",
-        (
-            jax.ShapeDtypeStruct((tokens, width), F32),
-            *([jax.ShapeDtypeStruct((per, width // pieces, cols), BF16)] * n_g),
-        ),
-        [SMEM, SMEM] + [VMEM] * (7 + len(dkv_list)) + [ANY] * len(weights),
-        (VMEM, *([ANY] * n_g)),
+        (jax.ShapeDtypeStruct((tokens, width), F32), *shapes),
+        [SMEM, SMEM] + [VMEM] * (9 + len(dkv_list)) + [ANY] * len(weights),
+        (VMEM, *([ANY] * len(shapes))),
         [
-            pltpu.VMEM((width, cols), BF16),
+            pltpu.VMEM((width, qkv_cols(width)), BF16),
             pltpu.VMEM((width, tokens), BF16),
             pltpu.VMEM((tokens, 3 * width), BF16),
-            pltpu.VMEM((width, cols), BF16),
+            pltpu.VMEM((width, tokens), BF16),
+            pltpu.VMEM((width, width + qkv_cols(width)), BF16),
             pltpu.SemaphoreType.DMA,
         ],
-        (order, order_g, x, dq, cosine, sine, gains, d_mid, ggain, *dkv_list, *weights),
-        4 * tokens * width * 3 * width,
-        width * cols * 4 + tokens * width * 20,
+        (
+            order,
+            table,
+            x,
+            dq,
+            cosine,
+            sine,
+            gains,
+            d_mid,
+            ggain,
+            attended,
+            d_attn,
+            *dkv_list,
+            *weights,
+        ),
+        15,
+        ride,
+        before,
     )
 
 
@@ -618,8 +722,8 @@
     def to_y(self, value):
         return self.send(value, lambda row, seq: (row ^ 2, seq))
 
-    def to_z(self, value):
-        return self.send(value, lambda row, seq: ((row + 4) % self.n_rows, seq))
+    def to_z(self, value, hops):
+        return self.send(value, lambda row, seq: ((row + 4 * hops) % self.n_rows, seq))
 
     def to_x(self, value):
         return self.send(value, lambda row, seq: (row, (seq + 1) % self.n_seq))
@@ -659,61 +763,178 @@
     total = tokens * n_seq
     lay = Layout(n_rows, n_seq, width, ff)
     row_at, seq_at = lax.axis_index("rows"), lax.axis_index("seq")
+    ringed = lay.ringed and n_seq == 2
+    depth = n_rows // 4
 
     def bundles(layer):
         gains = jnp.stack([norm_attn[layer], norm_mlp[layer]], 1)
-        gains = jnp.pad(gains, ((0, 0), (0, 126)))
-        return (
+        gains = jnp.pad(gains, ((0, 0), (0, 254)))
+        return [
             jnp.concatenate([w_q[layer], w_k[layer], w_v[layer], gains], 1),
             jnp.concatenate([w_o[layer], w_g[layer], w_u[layer]], 1),
             w_d[layer],
-        )
-
-    def gather(shard):
-        if not lay.ringed:
-            return [lax.all_gather(shard, "rows", axis=0, tiled=True)]
-        here = [shard]
-        while len(here) < n_rows // 4:
-            here.append(lay.to_z(here[-1]))
-        here = here + [lay.to_y(chunk) for chunk in here]
-        return here + [lay.to_core(chunk) for chunk in here]
-
-    if lay.ringed:
-        depth = n_rows // 4
-        order, order_g = [], []
-        for core in (0, 1):
-            for side in (0, 2):
-                for hop in range(depth):
-                    order.append(((row_at - 4 * hop) % n_rows) ^ core ^ side)
-                    order_g.append(((row_at + 4 * hop) % n_rows) ^ core ^ side)
-        order, order_g = jnp.stack(order).astype(jnp.int32), jnp.stack(order_g).astype(jnp.int32)
-        parts = (4, depth, n_rows)
-    else:
-        order = order_g = jnp.zeros((1,), jnp.int32)
-        parts = (1, 1, 1)
-
-    def scatter(stacks):
-        if not lay.ringed:
-            summed = lax.psum_scatter(stacks[0][0], "rows", scatter_dimension=0, tiled=True)
-            return lax.psum(summed, "seq").astype(F32)
-        far = (stacks[1].astype(F32) + lay.to_core(stacks[3]).astype(F32)).astype(BF16)
-        far = lay.to_y(far).astype(F32)
-        near = stacks[0].astype(F32) + lay.to_core(stacks[2]).astype(F32)
-        both = near + far
-        depth = both.shape[0]
-        moving = both[depth - 1].astype(BF16)
-        for hop in range(depth - 2, -1, -1):
-            moving = (lay.to_z(moving).astype(F32) + both[hop]).astype(BF16)
-        if n_seq != 2:
-            return lax.psum(moving, "seq").astype(F32)
-        return moving.astype(F32) + lay.to_x(moving).astype(F32)
+        ]
+
+    def split(cols, parts):
+        if not ringed:
+            return [(0, cols, "offload")]
+        found, first = [], 0
+        for count, (share, mode) in enumerate(parts, 1):
+            size = cols - first if count == len(parts) else round(cols * share / 256) * 256
+            found.append((first, size, mode))
+            first += size
+        return found
+
+    def table(sign, pieces):
+        numbers, columns = [], []
+        for first, size, mode in pieces:
+            if mode == "offload":
+                numbers.append(jnp.int32(0))
+                columns.append(jnp.int32(first // 128))
+                continue
+            for core in (0, 1):
+                for half in (0, 1) if mode == "half" else (0,):
+                    for side in (0, 2):
+                        for hop in range(depth):
+                            numbers.append(((row_at + sign * 4 * hop) % n_rows) ^ core ^ side)
+                            columns.append(
+                                first // 128 + (seq_at ^ half) * (size // 256)
+                                if mode == "half"
+                                else jnp.int32(first // 128)
+                            )
+        return jnp.stack([jnp.stack(numbers), jnp.stack(columns)]).astype(jnp.int32)
+
+    def shapes(rows, pieces):
+        found = []
+        for _, size, mode in pieces:
+            if mode == "offload":
+                found.append(jax.ShapeDtypeStruct((1, rows, size), BF16))
+            elif mode == "half":
+                found += [jax.ShapeDtypeStruct((2 * depth, rows // n_rows, size // 2), BF16)] * 4
+            else:
+                found += [jax.ShapeDtypeStruct((depth, rows // n_rows, size), BF16)] * 4
+        return found
+
+    def up(value):
+        return value.astype(F32)
+
+    class Gather:
+        def __init__(self, shard, mode):
+            self.mode, self.stacks, self.level = mode, None, 0
+            if mode == "offload":
+                self.stacks = [lax.all_gather(shard, "rows", axis=0, tiled=True)[None]]
+                return
+            if mode == "half":
+                columns = shard.shape[1] // 2
+                shard = lax.dynamic_slice_in_dim(shard, seq_at * columns, columns, 1)
+            self.stay, self.flying = [shard], []
+            while len(self.flying) + 1 < depth:
+                self.flying.append(lay.to_z((self.stay + self.flying)[-1], 1))
+
+        def step(self):
+            self.level += 1
+            if self.stacks is not None:
+                return
+            if self.level == 1:
+                near = jnp.stack(self.stay + self.flying)
+                self.stay, self.flying = [near], [lay.to_y(near)]
+            elif self.level == 2 and self.mode == "whole":
+                near, far = self.stay[0], self.flying[0]
+                self.stacks = [near, far, lay.to_core(near), lay.to_core(far)]
+            elif self.level == 2:
+                both = jnp.concatenate([self.stay[0], self.flying[0]])
+                self.stay, self.flying = [both], [lay.to_x(both)]
+            else:
+                both, other = self.stay[0], self.flying[0]
+                self.stacks = [both, other, lay.to_core(both), lay.to_core(other)]
+
+        def finish(self):
+            while self.stacks is None:
+                self.step()
+            return self.stacks
+
+    class Scatter:
+        def __init__(self, stack, mode):
+            self.mode, self.sum, self.level, self.old = mode, None, 0, False
+            if mode == "offload":
+                summed = lax.psum_scatter(stack[0][0], "rows", scatter_dimension=0, tiled=True)
+                if n_seq == 2:
+                    self.stay, self.flying, self.level = [summed], [lay.to_x(summed)], 9
+                else:
+                    self.sum = up(lax.psum(summed, "seq"))
+                return
+            self.flying = [lay.to_core(stack[3]), lay.to_core(stack[2])]
+            self.stay = [stack[1], stack[0]]
+
+        def along_z(self, both):
+            sent = [both[hop].astype(BF16) for hop in range(1, depth)]
+            self.flying = [lay.to_z(value, hop) for hop, value in enumerate(sent, 1)]
+            self.stay = [both[0]]
+            return sent
+
+        def step(self):
+            if self.sum is not None:
+                return []
+            self.level += 1
+            half = self.mode == "half"
+            stay, flying = self.stay, self.flying
+            if self.level == 1:
+                first = (up(stay[0]) + up(flying[0])).astype(BF16)
+                self.stay = [stay[1]]
+                self.flying = [lay.to_x(first) if half else lay.to_y(first), flying[1]]
+                return [first]
+            if self.level == 2:
+                both = up(stay[0]) + up(flying[1]) + up(flying[0])
+                if not half:
+                    return self.along_z(both)
+                far = both[depth:].astype(BF16)
+                self.stay, self.flying = [both[:depth]], [lay.to_y(far)]
+                return [far]
+            if self.level == 3 and half:
+                return self.along_z(stay[0] + up(flying[0]))
+            if self.level == (4 if half else 3):
+                total = up(stay[0])
+                for value in flying:
+                    total = total + up(value)
+                total = total.astype(BF16)
+                self.stay, self.flying = [total], [lay.to_x(total)]
+                return [total]
+            mine, other = stay[0], flying[0]
+            if not half:
+                self.sum = up(mine) + up(other)
+                return []
+            self.sum = up(
+                jnp.where(
+                    seq_at == 0,
+                    jnp.concatenate([mine, other], 1),
+                    jnp.concatenate([other, mine], 1),
+                )
+            )
+            return []
+
+        def finish(self):
+            while self.sum is None:
+                self.step()
+            return self.sum
+
+    def scatters(arrays, pieces):
+        found, at = [], 0
+        for _, _, mode in pieces:
+            size = 1 if mode == "offload" else 4
+            found.append(Scatter(arrays[at : at + size], mode))
+            at += size
+        return found
+
+    def joined(chains):
+        sums = [chain.finish() for chain in chains]
+        return sums[0] if len(sums) == 1 else jnp.concatenate(sums, 1)
 
     x_in = lay.into_groups(inputs[0])
     starts_mine = lay.into_groups(seg_start[0])
     d_top = lay.into_groups(cotangent[0])
     groups = lay.groups()
-    half = n_seq // 2
-    band = (seq_at % half) * 2 + row_at % 2 if lay.paired else seq_at
+    half_seq = n_seq // 2
+    band = (seq_at % half_seq) * 2 + row_at % 2 if lay.paired else seq_at
     two = lay.paired and n_seq == 2
 
     def exchange(value):
@@ -747,31 +968,115 @@
     reach = jnp.where(starts_mine >= 0, starts_mine, index)
     low = (jnp.min(reach.reshape(-1, Q_TILE), 1) // K_TILE).astype(jnp.int32)
 
+    in_widths = (qkv_cols(width), width + 2 * ff, width)
+    out_widths = (width + qkv_cols(width), 2 * ff, width)
+    in_pieces = [[split(c, p) for c, p in zip(in_widths, parts)] for parts in IN_PARTS]
+    out_pieces = [[split(c, p) for c, p in zip(out_widths, parts)] for parts in OUT_PARTS]
+    known = {}
+
+    def table_of(sign, pieces):
+        key = (sign, *pieces)
+        if key not in known:
+            known[key] = table(sign, pieces)
+        return known[key]
+
+    orders = [[table_of(-1, pieces) for pieces in in_pieces[layer]] for layer in range(LAYERS)]
+    tables = [[table_of(1, pieces) for pieces in out_pieces[layer]] for layer in range(LAYERS)]
+
+    def gathers(shard, pieces):
+        return [Gather(shard[:, first : first + size], mode) for first, size, mode in pieces]
+
+    def arrived(chains):
+        return [stack for chain in chains for stack in chain.finish()]
+
     kept = []
     current = x_in
+    weights = []
+
+    def near_of(bundles_of_chains):
+        found = []
+        for chains_here in bundles_of_chains:
+            for chain in chains_here:
+                if chain.stacks is None:
+                    chain.step()
+                    found += chain.stay
+        return found
+
+    shards = bundles(0)
+    moving = [[gathers(shards[0], in_pieces[0][0])], None]
+    if ringed:
+        _ = ([value for chain in moving[0][0] for value in chain.flying], shards[1:])
+    moving[0] += [gathers(s, p) for s, p in zip(shards[1:], in_pieces[0][1:])]
     for layer in range(LAYERS):
-        qkv_shard, ogu_shard, down_shard = bundles(layer)
-        w_qkv = gather(qkv_shard)
-        w_ogu = gather(ogu_shard)
-        w_down = gather(down_shard)
-        queries, kv, gains = pre(order, current, cosine, sine, w_qkv)
+        last = layer + 1 == LAYERS
+        o_qkv, o_ogu, o_down = orders[layer]
+        w_qkv = arrived(moving[layer][0])
+        (queries, kv, gains), ridden = pre(
+            o_qkv,
+            current,
+            cosine,
+            sine,
+            w_qkv,
+            ride=[] if last else bundles(layer + 1),
+        )
         kv_list = exchange(kv)
-        attended, lse = attend(low, bands, queries, mark_row, mark_col, kv_list, total)
-        following, mid, gu = post(order, current, attended, gains, w_ogu, w_down)
-        kept.append((current, queries, kv_list, attended, lse, mid, gu, gains, w_qkv, w_ogu, w_down))
-        current = following
-    output = lay.out_of_groups(current)
-
-    grads = [None] * LAYERS
+        (attended, lse), _ = attend(
+            low,
+            bands,
+            queries,
+            mark_row,
+            mark_col,
+            kv_list,
+            total,
+        )
+        before = []
+        if not last:
+            moving[layer + 1] = [gathers(s, p) for s, p in zip(ridden, in_pieces[layer + 1])]
+        w_ogu, w_down = arrived(moving[layer][1]), arrived(moving[layer][2])
+        (result, mid, gu), _ = post(
+            o_ogu, o_down, ff, current, attended, gains, w_ogu, w_down, before=before
+        )
+        kept.append((current, queries, kv_list, attended, lse, mid, gu, gains))
+        weights.append((w_qkv, w_ogu, w_down))
+        current = result
+    output = lay.out_of_groups(current.astype(BF16)).astype(F32)
+
     flow = d_top
+    chains = [None] * LAYERS
+    live = []
+
+    def through(kernel, *args, **more):
+        if not ringed:
+            return kernel(*args, **more)[0]
+        sent = more.pop("before", [])
+        for chain in live:
+            if chain.level < 9:
+                sent = sent + (chain.step() if chain.old else [])
+            chain.old = True
+        holders = [chain for chain in live if chain.sum is None and chain.level < 9]
+        ride = [value for chain in holders for value in chain.stay]
+        results, ridden = kernel(*args, ride=ride, before=sent, **more)
+        for chain in holders:
+            chain.stay, ridden = ridden[: len(chain.stay)], ridden[len(chain.stay) :]
+        return results
+
     for layer in reversed(range(LAYERS)):
-        x, queries, kv_list, attended, lse, mid, gu, gains, w_qkv, w_ogu, w_down = kept[layer]
-        n_g = parts[0]
-        results = mlp_back(order, order_g, parts, flow, mid, gu, attended, gains, w_ogu, w_down)
-        d_mid, d_att, ggain = results[:3]
-        g_ogu = scatter(results[3 : 3 + n_g])
-        g_down = scatter(results[3 + n_g : 3 + 2 * n_g])
-        results = attend_back(
+        x, queries, kv_list, attended, lse, mid, gu, gains = kept[layer]
+        o_qkv, o_ogu, o_down = orders[layer]
+        w_qkv, w_ogu, w_down = weights[layer]
+        t_qkv, t_gu, t_down = tables[layer]
+        p_qkv, p_gu, p_down = out_pieces[layer]
+        s_gu, s_down = shapes(width, p_gu), shapes(ff, p_down)
+        results = through(
+            mlp_back, o_down, (t_gu, t_down), (s_gu, s_down), flow, mid, gu, gains, w_down
+        )
+        dgu = results[0]
+        c_gu = scatters(results[1 : 1 + len(s_gu)], p_gu)
+        c_down = scatters(results[1 + len(s_gu) :], p_down)
+        live += c_gu + c_down
+        d_mid, d_attn, d_att, ggain = through(mid_back, o_ogu, flow, mid, dgu, gains, w_ogu)
+        results = through(
+            attend_back,
             low,
             bands,
             queries,
@@ -794,13 +1099,33 @@
                     jnp.stack(dkv), BOTH, scatter_dimension=0, axis_index_groups=groups
                 )
             ]
-        results = pre_back(
-            order, order_g, parts, x, dq, cosine, sine, gains, d_mid, ggain, dkv_list, w_qkv
+        s_qkv = shapes(width, p_qkv)
+        results = through(
+            pre_back,
+            o_qkv,
+            t_qkv,
+            s_qkv,
+            x,
+            dq,
+            cosine,
+            sine,
+            gains,
+            d_mid,
+            ggain,
+            attended,
+            d_attn,
+            dkv_list,
+            w_qkv,
+            before=[output] if layer == 0 else [],
         )
         flow = results[0]
-        g_qkv = scatter(results[1:])
-        grads[layer] = (g_qkv, g_ogu, g_down)
-    grad_input = lay.out_of_groups(flow)
+        c_qkv = scatters(results[1:], p_qkv)
+        live += c_qkv
+        chains[layer] = (c_qkv, c_gu, c_down)
+    while ringed and any(chain.sum is None and chain.level < 9 for chain in live):
+        through(lambda ride, before: ([], gate(before, ride)))
+    grads = [[joined(part) for part in chains[layer]] for layer in range(LAYERS)]
+    grad_input = lay.out_of_groups(flow.astype(BF16)).astype(F32)
 
     def stack(which, first, size):
         return jnp.stack([grads[layer][which][:, first : first + size] for layer in range(LAYERS)])
@@ -811,12 +1136,12 @@
         stack(0, 0, width),
         stack(0, width, width),
         stack(0, 2 * width, width),
-        stack(1, 0, width),
-        stack(1, width, ff),
-        stack(1, width + ff, ff),
+        stack(0, 3 * width, width),
+        stack(1, 0, ff),
+        stack(1, ff, ff),
         stack(2, 0, width),
-        stack(0, 3 * width, 1)[..., 0],
-        stack(0, 3 * width + 1, 1)[..., 0],
+        stack(0, 4 * width, 1)[..., 0],
+        stack(0, 4 * width + 1, 1)[..., 0],
     )
 
 

time: 757 us -> 648 us (0.86)
  waiting for transfers between devices: 402 us -> 213 us
  starting transfers between devices: 96.6 us -> 116 us
  local copies, waits for them, and re-layouts: 16.5 us -> 35.4 us
  other arithmetic: 23 us -> 38.6 us
  between operations: 2.96 us -> 16.2 us
  Pallas kernels: 206 us -> 219 us
    ppermute x140 -> x95, waiting for transfers between devices: 402 us -> 212 us  [send(): return lax.ppermute(value, BOTH, self.pairs(move))]
    pallas_call x12 -> x19, Pallas kernels: 206 us -> 219 us  [call(): pl.pallas_call(wrapped, name=name, out_shape=(*out_shape, *(jax.ShapeDtyp...]
    ppermute x140 -> x95, starting transfers between devices: 93.7 us -> 104 us  [send(): return lax.ppermute(value, BOTH, self.pairs(move))]
    reduce_scatter x0 -> x2, starting transfers between devices: none -> 9.94 us  [__init__(): lax.psum_scatter(stack[0][0], 'rows', scatter_dimension=0, tiled=True)]
    unnamed x204 -> x174, local copies, waits for them, and re-layouts: 7.04 us -> 16 us
  transfers between devices with their start and end apart: 142 -> 99, of which waited for: 49 -> 31; matrix products, arithmetic and copies ran while one was open for 4% -> 10% of each run, Pallas kernels for 23% -> 31%
where the time goes in v2:
time: 648 us; the launch traced here: 637 us
  Pallas kernels  219 us (34%)
  waiting for transfers between devices  213 us (33%)
  starting transfers between devices  116 us (18%)
  other arithmetic  38.6 us (6%)
  local copies, waits for them, and re-layouts  35.4 us (5%)
  between operations  16.2 us (2%)
    pallas_call x19, Pallas kernels, call(): pl.pallas_call(wrapped, name=name, out_shape=(*out_shape, *(jax.ShapeDtyp...  219 us
    ppermute x95, waiting for transfers between devices, send(): return lax.ppermute(value, BOTH, self.pairs(move))  212 us
    ppermute x95, starting transfers between devices, send(): return lax.ppermute(value, BOTH, self.pairs(move))  104 us
    unnamed x174, local copies, waits for them, and re-layouts  16 us
  transfers between devices with their start and end apart: 99, of which 31 were waited for; matrix products, arithmetic and copies ran while one was open for 10% of the time, Pallas kernels for 31%

profile of v2, /device:TPU:0, one launch (start us, length us, event | category | flops | bytes accessed | tf_op | source)
XLA Modules:
  0.0 637.4 jit_solution(18108875572641178430)
XLA Ops:
  15.4 7.4 %collective-permute-start = (bf16[512,768]{1,0:T(8,128)(2,1)}, bf16[512,768]{1,0:T(8,128)(2,1)}, u32[]{:S(2)}, u32[]{:S(2)}) collective-permute-start(bf16[512,768]{1,0:T(8,128)(2,1)} %bitcast.267), channel_id=1, source_target_pairs={{0,0},{1,2},{2,1},{3,3},{4,4},{5,6},{6,5},{7,7},{8,8},{9,10},{10,9... | collective-permute-start | bytes 2359304 | tf_op jit(solution)/shard_map/ppermute | solution.py:717
  37.1 7.5 %collective-permute-done.3 = bf16[48,2560]{1,0:T(8,128)(2,1)S(1)} collective-permute-done((bf16[48,2560]{1,0:T(8,128)(2,1)S(1)}, bf16[48,2560]{1,0:T(8,128)(2,1)S(1)}, u32[]{:S(2)}, u32[]{:S(2)}) %collective-permute-start.3) | collective-permute-done | bytes 245792 | tf_op jit(solution)/shard_map/ppermute | solution.py:717
  64.1 13.5 %collective-permute-done.5.refs_5_.refs_14_ = bf16[4,48,2560]{2,1,0:T(8,128)(2,1)S(1)} collective-permute-done((bf16[4,48,2560]{2,1,0:T(8,128)(2,1)S(1)}, bf16[4,48,2560]{2,1,0:T(8,128)(2,1)S(1)}, u32[]{:S(2)}, u32[]{:S(2)}) %collective-permute-start.5) | collective-permute-done | bytes 983072 | tf_op jit(solution)/shard_map/ppermute | solution.py:717
  130.0 13.2 %collective-permute-done.20.refs_10_ = bf16[8,48,1152]{2,1,0:T(8,128)(2,1)} collective-permute-done((bf16[8,48,1152]{2,1,0:T(8,128)(2,1)S(1)}, bf16[8,48,1152]{2,1,0:T(8,128)(2,1)}, u32[]{:S(2)}, u32[]{:S(2)}) %collective-permute-start.20) | collective-permute-done | bytes 884768 | tf_op jit(solution)/shard_map/ppermute | solution.py:717
  143.9 14.3 %collective-permute-done.40 = bf16[48,4864]{1,0:T(8,128)(2,1)S(1)} collective-permute-done((bf16[48,4864]{1,0:T(8,128)(2,1)S(1)}, bf16[48,4864]{1,0:T(8,128)(2,1)S(1)}, u32[]{:S(2)}, u32[]{:S(2)}) %collective-permute-start.40) | collective-permute-done | bytes 466976 | tf_op jit(solution)/shard_map/ppermute | solution.py:717
  168.1 14.2 %attend.2 = (bf16[512,768]{1,0:T(8,128)(2,1)}, f32[16,512]{1,0:T(8,128)}) custom-call(s32[4]{0:T(128)} %and_select_fusion.refs_0_, s32[3]{0:T(128)} %pad_add_fusion.6.refs_1_, bf16[512,768]{1,0:T(8,128)(2,1)} %get-tuple-element.99.refs_2_, s32[8,512]{1,0:T(8,128)} %broadcast_in_dim.13.refs_3_.refs_6_, s32[1024,128]{1,0:T(8,128)} %broadcast_in_dim.26.refs_4_.refs_7_, ...), custom_call_target="tpu_custom_call" | custom-call | flops 16499999744 | tf_op jit(solution)/shard_map/attend/pallas_call | solution.py:86
  186.6 14.3 %post.2 = (f32[512,768]{1,0:T(8,128)}, f32[512,768]{1,0:T(8,128)}, bf16[512,4096]{1,0:T(8,128)(2,1)}) custom-call(s32[2,48]{1,0:T(2,128)} %pad_add_fusion.4.refs_0_, s32[2,32]{1,0:T(2,128)} %get-tuple-element.259.refs_1_.refs_0_, bf16[512,768]{1,0:T(8,128)(2,1)} %collective-permute-done.refs_1_.refs_2_, ...), custom_call_target="tpu_custom_call" | custom-call | flops 15399999488 | tf_op jit(solution)/shard_map/post/pallas_call | solution.py:86
  201.9 7.5 %pre.3 = (bf16[512,768]{1,0:T(8,128)(2,1)}, bf16[512,1536]{1,0:T(8,128)(2,1)}, f32[8,768]{1,0:T(8,128)}) custom-call(s32[2,32]{1,0:T(2,128)} %get-tuple-element.260.refs_0_, f32[512,768]{1,0:T(8,128)} %get-tuple-element.103.refs_1_.refs_2_, f32[512,128]{1,0:T(8,128)} %copy.92.refs_2_.refs_8_.refs_4_, f32[512,128]{1,0:T(8,128)} %pad_maximum_fusion.14.refs_3_.refs_9_.refs_5_, ...), custom_call_target="tpu_custom_call" | custom-call | flops 7699999744 | tf_op jit(solution)/shard_map/pre/pallas_call | solution.py:86
  210.6 25.2 %collective-permute-done.47 = bf16[4,128,384]{2,1,0:T(8,128)(2,1)S(1)} collective-permute-done((bf16[4,128,384]{2,1,0:T(8,128)(2,1)S(1)}, bf16[4,128,384]{2,1,0:T(8,128)(2,1)S(1)}, u32[]{:S(2)}, u32[]{:S(2)}) %collective-permute-start.47) | collective-permute-done | bytes 393248 | tf_op jit(solution)/shard_map/ppermute | solution.py:717
  237.3 18.1 %collective-permute-done.48.refs_10_.refs_8_ = bf16[8,128,384]{2,1,0:T(8,128)(2,1)} collective-permute-done((bf16[8,128,384]{2,1,0:T(8,128)(2,1)S(1)}, bf16[8,128,384]{2,1,0:T(8,128)(2,1)}, u32[]{:S(2)}, u32[]{:S(2)}) %collective-permute-start.48) | collective-permute-done | bytes 786464 | tf_op jit(solution)/shard_map/ppermute | solution.py:717
  256.6 14.2 %attend.3 = (bf16[512,768]{1,0:T(8,128)(2,1)}, f32[16,512]{1,0:T(8,128)}) custom-call(s32[4]{0:T(128)} %and_select_fusion.refs_0_, s32[3]{0:T(128)} %pad_add_fusion.6.refs_1_, bf16[512,768]{1,0:T(8,128)(2,1)} %get-tuple-element.105.refs_2_, s32[8,512]{1,0:T(8,128)} %broadcast_in_dim.13.refs_3_.refs_6_, s32[1024,128]{1,0:T(8,128)} %broadcast_in_dim.26.refs_4_.refs_7_, ...), custom_call_target="tpu_custom_call" | custom-call | flops 16499999744 | tf_op jit(solution)/shard_map/attend/pallas_call | solution.py:86
  270.9 14.6 %post.3 = (f32[512,768]{1,0:T(8,128)}, f32[512,768]{1,0:T(8,128)}, bf16[512,4096]{1,0:T(8,128)(2,1)}) custom-call(s32[2,16]{1,0:T(2,128)} %stack.279.refs_0_, s32[2,32]{1,0:T(2,128)} %get-tuple-element.259.refs_1_.refs_0_, f32[512,768]{1,0:T(8,128)} %get-tuple-element.103.refs_1_.refs_2_, bf16[512,768]{1,0:T(8,128)(2,1)} %get-tuple-element.107.refs_3_.refs_4_.refs_9_, ...), custom_call_target="tpu_custom_call" | custom-call | flops 15399999488 | tf_op jit(solution)/shard_map/post/pallas_call | solution.py:86
  286.4 22.3 %mlp_back.2 = (bf16[512,4096]{1,0:T(8,128)(2,1)}, bf16[1,768,4096]{2,1,0:T(8,128)(2,1)}, bf16[8,128,384]{2,1,0:T(8,128)(2,1)}, bf16[8,128,384]{2,1,0:T(8,128)(2,...) custom-call(s32[2,32]{1,0:T(2,128)} %get-tuple-element.259.refs_1_.refs_0_, ...), custom_call_target="tpu_custom_call" | custom-call | flops 22000001024 | tf_op jit(solution)/shard_map/mlp_back/pallas_call | solution.py:86
  310.9 9.9 %reduce-scatter.3.cloned.1.call-start = ((), (), s32[]{:S(2)}) async-start(), calls=%async_computation.2 | async-start | bytes 6684672 | tf_op jit(solution)/shard_map/reduce_scatter | solution.py:860
  320.8 14.4 %mid_back.2 = (f32[512,768]{1,0:T(8,128)}, bf16[512,768]{1,0:T(8,128)(2,1)}, bf16[512,768]{1,0:T(8,128)(2,1)}, f32[8,768]{1,0:T(8,128)}, bf16[8,128,384]{2,1,0:T(8,128)(2,1)}, /*index=5*/bf16[8,128,384]{2,1,0:T(8,128)(2,1)}) custom-call(s32[2,16]{1,0:T(2,128)} %stack.279.refs_0_, ...), custom_call_target="tpu_custom_call", output_to_operand_aliasing={{4}: (9, {}), {5}: (10, {})} | custom-call | flops 14300000256 | tf_op jit(solution)/shard_map/mid_back/pallas_call | solution.py:86
  337.4 19.0 %attend_back.2 = (bf16[512,768]{1,0:T(8,128)(2,1)}, bf16[512,1536]{1,0:T(8,128)(2,1)}, bf16[512,1536]{1,0:T(8,128)(2,1)}, bf16[8,128,384]{2,1,0:T(8,128)(2,1)}) custom-call(s32[4]{0:T(128)} %and_select_fusion.refs_0_, s32[3]{0:T(128)} %pad_add_fusion.6.refs_1_, bf16[512,768]{1,0:T(8,128)(2,1)} %get-tuple-element.105.refs_2_, ...), custom_call_target="tpu_custom_call", output_to_operand_aliasing={{3}: (12, {})} | custom-call | flops 22000001024 | tf_op jit(solution)/shard_map/attend_back/pallas_call | solution.py:86
  366.1 22.6 %collective-permute-done.56 = bf16[8,128,384]{2,1,0:T(8,128)(2,1)S(1)} collective-permute-done((bf16[8,128,384]{2,1,0:T(8,128)(2,1)S(1)}, bf16[8,128,384]{2,1,0:T(8,128)(2,1)S(1)}, u32[]{:S(2)}, u32[]{:S(2)}) %collective-permute-start.56) | collective-permute-done | bytes 786464 | tf_op jit(solution)/shard_map/ppermute | solution.py:717
  390.7 15.8 %pre_back.2 = (f32[512,768]{1,0:T(8,128)}, bf16[8,48,1664]{2,1,0:T(8,128)(2,1)}, bf16[8,48,1664]{2,1,0:T(8,128)(2,1)}, bf16[8,48,1664]{2,1,0:T(8,128)(2,1)}, bf1...) custom-call(s32[2,32]{1,0:T(2,128)} %get-tuple-element.260.refs_0_, ...), custom_call_target="tpu_custom_call", output_to_operand_aliasing={{5}: (17, {})} | custom-call | flops 16499999744 | tf_op jit(solution)/shard_map/pre_back/pallas_call | solution.py:86
  417.8 22.6 %mlp_back.3 = (bf16[512,4096]{1,0:T(8,128)(2,1)}, bf16[1,768,4096]{2,1,0:T(8,128)(2,1)}, bf16[8,128,384]{2,1,0:T(8,128)(2,1)}, bf16[8,128,384]{2,1,0:T(8,128)(2,...) custom-call(s32[2,32]{1,0:T(2,128)} %get-tuple-element.259.refs_1_.r, ...), custom_call_target="tpu_custom_call", output_to_operand_aliasing={{6}: (11, {}), {7}: (12, {}), {8}: (13, {})} | custom-call | flops 22000001024 | tf_op jit(solution)/shard_map/mlp_back/pallas_call | solution.py:86
  445.8 14.8 %mid_back.3 = (f32[512,768]{1,0:T(8,128)}, bf16[512,768]{1,0:T(8,128)(2,1)}, bf16[512,768]{1,0:T(8,128)(2,1)}, f32[8,768]{1,0:T(8,128)}, bf16[128,384]{1,0:T(8,1...) custom-call(s32[2,48]{1,0:T(2,128)} %pad_add_fusion.4.refs_0_, ...), custom_call_target="tpu_custom_call", output_to_operand_aliasing={{4}: (13, {}), {5}: (14, {}), {6}: (15, {}), {7}: (16, {})} | custom-call | flops 14300000256 | tf_op jit(solution)/shard_map/mid_back/pallas_call | solution.py:86
  463.3 12.8 %collective-permute-done.63 = bf16[8,48,1664]{2,1,0:T(8,128)(2,1)S(1)} collective-permute-done((bf16[8,48,1664]{2,1,0:T(8,128)(2,1)S(1)}, bf16[8,48,1664]{2,1,0:T(8,128)(2,1)S(1)}, u32[]{:S(2)}, u32[]{:S(2)}) %collective-permute-start.63) | collective-permute-done | bytes 1277984 | tf_op jit(solution)/shard_map/ppermute | solution.py:717
  478.8 18.9 %attend_back.3 = (bf16[512,768]{1,0:T(8,128)(2,1)}, bf16[512,1536]{1,0:T(8,128)(2,1)}, bf16[512,1536]{1,0:T(8,128)(2,1)}, f32[4,48,1664]{2,1,0:T(8,128)}, bf16[8,128,384]{2,1,0:T(8,128)(2,1)}) custom-call(s32[4]{0:T(128)} %and_select_fusion.refs_0_, s32[3]{0:T(128)} %pad_add_fusion.6.refs_1_, ...), custom_call_target="tpu_custom_call", output_to_operand_aliasing={{3}: (12, {}), {4}: (13, {})} | custom-call | flops 22000001024 | tf_op jit(solution)/shard_map/attend_back/pallas_call | solution.py:86
  509.6 15.6 %pre_back.3 = (f32[512,768]{1,0:T(8,128)}, bf16[4,48,1536]{2,1,0:T(8,128)(2,1)}, bf16[4,48,1536]{2,1,0:T(8,128)(2,1)}, bf16[4,48,1536]{2,1,0:T(8,128)(2,1)}, bf1...) custom-call(s32[2,16]{1,0:T(2,128)} %stack.279.refs_0_, ...), custom_call_target="tpu_custom_call", output_to_operand_aliasing={{9}: (17, {}), {10}: (18, {})} | custom-call | flops 16499999744 | tf_op jit(solution)/shard_map/pre_back/pallas_call | solution.py:86
  553.8 8.2 %collective-permute-done.95 = bf16[128,384]{1,0:T(8,128)(2,1)S(1)} collective-permute-done((bf16[128,384]{1,0:T(8,128)(2,1)S(1)}, bf16[128,384]{1,0:T(8,128)(2,1)S(1)}, u32[]{:S(2)}, u32[]{:S(2)}) %collective-permute-start.95) | collective-permute-done | bytes 98336 | tf_op jit(solution)/shard_map/ppermute | solution.py:717
  (489 shorter events, 260.1 us)
Async XLA Ops:
  7.2 601.3 %reduce-scatter.5.cloned.1.call-start = ((), (), s32[]{:S(2)}) async-start(), calls=%async_computation.3 | async-start | bytes 6684672 | tf_op jit(solution)/shard_map/reduce_scatter | solution.py:860
  15.4 76.9 %collective-permute-start = (bf16[512,768]{1,0:T(8,128)(2,1)}, bf16[512,768]{1,0:T(8,128)(2,1)}, u32[]{:S(2)}, u32[]{:S(2)}) collective-permute-start(bf16[512,768]{1,0:T(8,128)(2,1)} %bitcast.267), channel_id=1, source_target_pairs={{0,0},{1,2},{2,1},{3,3},{4,4},{5,6},{6,5},{7,7},{8,8},{9,10},{10,9... | collective-permute-start | bytes 2359304 | tf_op jit(solution)/shard_map/ppermute | solution.py:717
  23.6 32.4 %collective-permute-start.16 = (bf16[48,1152]{1,0:T(8,128)(2,1)S(1)}, bf16[48,1152]{1,0:T(8,128)(2,1)S(1)}, u32[]{:S(2)}, u32[]{:S(2)}) collective-permute-start(bf16[48,1152]{1,0:T(8,128)(2,1)S(1)} %get-tuple-element.208), channel_id=1, source_target_pairs={{0,8},{1,9},{2,10},{3,11},{4,12},{5,13},{6,14},{7,15},{8,16},{9,17... | collective-permute-start | bytes 331784 | tf_op jit(solution)/shard_map/ppermute | solution.py:717
  26.5 28.8 %collective-permute-start.23 = (bf16[128,384]{1,0:T(8,128)(2,1)S(1)}, bf16[128,384]{1,0:T(8,128)(2,1)S(1)}, u32[]{:S(2)}, u32[]{:S(2)}) collective-permute-start(bf16[128,384]{1,0:T(8,128)(2,1)S(1)} %bitcast.234), channel_id=1, source_target_pairs={{0,8},{1,9},{2,10},{3,11},{4,12},{5,13},{6,14},{7,15},{8,16},{9,17... | collective-permute-start | bytes 294920 | tf_op jit(solution)/shard_map/ppermute | solution.py:717
  33.2 45.1 %collective-permute-start.10 = (bf16[48,2560]{1,0:T(8,128)(2,1)S(1)}, bf16[48,2560]{1,0:T(8,128)(2,1)S(1)}, u32[]{:S(2)}, u32[]{:S(2)}) collective-permute-start(bf16[48,2560]{1,0:T(8,128)(2,1)S(1)} %pad_maximum_fusion.15), channel_id=1, source_target_pairs={{0,8},{1,9},{2,10},{3,11},{4,12},{5,13},{6,14},{7,15},{8,16},{9,17... | collective-permute-start | bytes 737288 | tf_op jit(solution)/shard_map/ppermute | solution.py:717
  64.1 28.2 %collective-permute-start.6 = (bf16[4,48,2560]{2,1,0:T(8,128)(2,1)S(1)}, bf16[4,48,2560]{2,1,0:T(8,128)(2,1)S(1)}, u32[]{:S(2)}, u32[]{:S(2)}) collective-permute-start(bf16[4,48,2560]{2,1,0:T(8,128)(2,1)S(1)} %pad_maximum_fusion.1.refs_4_.refs_13_), channel_id=1, source_target_pairs={{0,2},{1,3},{2,0},{3,1},{4,6},{5,7},{6,4},{7,5},{8,10},{9,11},{10,... | collective-permute-start | bytes 2949128 | tf_op jit(solution)/shard_map/ppermute | solution.py:717
  128.3 36.3 %collective-permute-start.9 = (bf16[512,1536]{1,0:T(8,128)(2,1)S(1)}, bf16[512,1536]{1,0:T(8,128)(2,1)S(1)}, u32[]{:S(2)}, u32[]{:S(2)}) collective-permute-start(bf16[512,1536]{1,0:T(8,128)(2,1)S(1)} %copy-done.59), channel_id=1, source_target_pairs={{0,2},{1,3},{2,0},{3,1},{4,6},{5,7},{6,4},{7,5},{8,10},{9,11},{10,... | collective-permute-start | bytes 4718600 | tf_op jit(solution)/shard_map/ppermute | solution.py:717
  128.5 30.7 %collective-permute-start.13 = (bf16[4,48,2560]{2,1,0:T(8,128)(2,1)S(1)}, bf16[4,48,2560]{2,1,0:T(8,128)(2,1)}, u32[]{:S(2)}, u32[]{:S(2)}) collective-permute-start(bf16[4,48,2560]{2,1,0:T(8,128)(2,1)S(1)} %pad_maximum_fusion.2.refs_5_), channel_id=1, source_target_pairs={{0,4},{1,5},{2,6},{3,7},{4,0},{5,1},{6,2},{7,3},{8,12},{9,13},{10,... | collective-permute-start | bytes 2949128 | tf_op jit(solution)/shard_map/ppermute | solution.py:717
  182.3 27.7 %collective-permute-start.46 = (bf16[128,384]{1,0:T(8,128)(2,1)S(1)}, bf16[128,384]{1,0:T(8,128)(2,1)S(1)}, u32[]{:S(2)}, u32[]{:S(2)}) collective-permute-start(bf16[128,384]{1,0:T(8,128)(2,1)S(1)} %collective-permute-done.45), channel_id=1, source_target_pairs={{0,8},{1,9},{2,10},{3,11},{4,12},{5,13},{6,14},{7,15},{8,16},{9,17... | collective-permute-start | bytes 294920 | tf_op jit(solution)/shard_map/ppermute | solution.py:717
  184.0 52.1 %collective-permute-start.41 = (bf16[4,48,4864]{2,1,0:T(8,128)(2,1)S(1)}, bf16[4,48,4864]{2,1,0:T(8,128)(2,1)S(1)}, u32[]{:S(2)}, u32[]{:S(2)}) collective-permute-start(bf16[4,48,4864]{2,1,0:T(8,128)(2,1)S(1)} %pad_maximum_fusion.refs_5_), channel_id=1, source_target_pairs={{0,4},{1,5},{2,6},{3,7},{4,0},{5,1},{6,2},{7,3},{8,12},{9,13},{10,... | collective-permute-start | bytes 5603336 | tf_op jit(solution)/shard_map/ppermute | solution.py:717
  209.4 46.0 %collective-permute-start.37 = (bf16[512,1536]{1,0:T(8,128)(2,1)}, bf16[512,1536]{1,0:T(8,128)(2,1)S(1)}, u32[]{:S(2)}, u32[]{:S(2)}) collective-permute-start(bf16[512,1536]{1,0:T(8,128)(2,1)} %get-tuple-element.106.refs_5_.refs_10_), channel_id=1, source_target_pairs={{0,2},{1,3},{2,0},{3,1},{4,6},{5,7},{6,4},{7,5},{8,10},{9,11},{10,... | collective-permute-start | bytes 4718600 | tf_op jit(solution)/shard_map/ppermute | solution.py:717
  236.0 34.9 %collective-permute-start.42 = (bf16[4,48,4864]{2,1,0:T(8,128)(2,1)S(1)}, bf16[4,48,4864]{2,1,0:T(8,128)(2,1)}, u32[]{:S(2)}, u32[]{:S(2)}) collective-permute-start(bf16[4,48,4864]{2,1,0:T(8,128)(2,1)S(1)} %pad_maximum_fusion.refs_5_), channel_id=1, source_target_pairs={{0,2},{1,3},{2,0},{3,1},{4,6},{5,7},{6,4},{7,5},{8,10},{9,11},{10,... | collective-permute-start | bytes 5603336 | tf_op jit(solution)/shard_map/ppermute | solution.py:717
  236.1 34.8 %collective-permute-start.43 = (bf16[4,48,4864]{2,1,0:T(8,128)(2,1)S(1)}, bf16[4,48,4864]{2,1,0:T(8,128)(2,1)}, u32[]{:S(2)}, u32[]{:S(2)}) collective-permute-start(bf16[4,48,4864]{2,1,0:T(8,128)(2,1)S(1)} %collective-permute-done.41.refs_6_), channel_id=1, source_target_pairs={{0,2},{1,3},{2,0},{3,1},{4,6},{5,7},{6,4},{7,5},{8,10},{9,11},{10,... | collective-permute-start | bytes 5603336 | tf_op jit(solution)/shard_map/ppermute | solution.py:717
  236.6 49.0 %collective-permute-start.52 = (bf16[512,768]{1,0:T(8,128)(2,1)S(1)}, bf16[512,768]{1,0:T(8,128)(2,1)S(1)}, u32[]{:S(2)}, u32[]{:S(2)}) collective-permute-start(bf16[512,768]{1,0:T(8,128)(2,1)S(1)} %bitcast.268), channel_id=1, source_target_pairs={{0,0},{1,2},{2,1},{3,3},{4,4},{5,6},{6,5},{7,7},{8,8},{9,10},{10,9... | collective-permute-start | bytes 2359304 | tf_op jit(solution)/shard_map/ppermute | solution.py:717
  310.9 308.5 %reduce-scatter.3.cloned.1.call-start = ((), (), s32[]{:S(2)}) async-start(), calls=%async_computation.2 | async-start | bytes 6684672 | tf_op jit(solution)/shard_map/reduce_scatter | solution.py:860
  356.4 33.6 %collective-permute-start.54 = (bf16[512,1536]{1,0:T(8,128)(2,1)}, bf16[512,1536]{1,0:T(8,128)(2,1)}, u32[]{:S(2)}, u32[]{:S(2)}) collective-permute-start(bf16[512,1536]{1,0:T(8,128)(2,1)} %get-tuple-element.127), channel_id=1, source_target_pairs={{0,2},{1,3},{2,0},{3,1},{4,6},{5,7},{6,4},{7,5},{8,10},{9,11},{10,... | collective-permute-start | bytes 4718600 | tf_op jit(solution)/shard_map/ppermute | solution.py:717
  360.4 28.3 %collective-permute-start.56 = (bf16[8,128,384]{2,1,0:T(8,128)(2,1)S(1)}, bf16[8,128,384]{2,1,0:T(8,128)(2,1)S(1)}, u32[]{:S(2)}, u32[]{:S(2)}) collective-permute-start(bf16[8,128,384]{2,1,0:T(8,128)(2,1)S(1)} %copy-done.24), channel_id=1, source_target_pairs={{0,1},{1,0},{2,3},{3,2},{4,5},{5,4},{6,7},{7,6},{8,9},{9,8},{10,11... | collective-permute-start | bytes 2359304 | tf_op jit(solution)/shard_map/ppermute | solution.py:717
  406.5 37.9 %collective-permute-start.61 = (bf16[8,48,1664]{2,1,0:T(8,128)(2,1)}, bf16[8,48,1664]{2,1,0:T(8,128)(2,1)S(1)}, u32[]{:S(2)}, u32[]{:S(2)}) collective-permute-start(bf16[8,48,1664]{2,1,0:T(8,128)(2,1)} %get-tuple-element.142), channel_id=1, source_target_pairs={{0,2},{1,3},{2,0},{3,1},{4,6},{5,7},{6,4},{7,5},{8,10},{9,11},{10,... | collective-permute-start | bytes 3833864 | tf_op jit(solution)/shard_map/ppermute | solution.py:717
  408.6 32.0 %collective-permute-start.58 = (bf16[128,384]{1,0:T(8,128)(2,1)}, bf16[128,384]{1,0:T(8,128)(2,1)}, u32[]{:S(2)}, u32[]{:S(2)}) collective-permute-start(bf16[128,384]{1,0:T(8,128)(2,1)} %get-tuple-element.230.refs_14_), channel_id=1, source_target_pairs={{0,8},{1,9},{2,10},{3,11},{4,12},{5,13},{6,14},{7,15},{8,16},{9,17... | collective-permute-start | bytes 294920 | tf_op jit(solution)/shard_map/ppermute | solution.py:717
  412.0 29.1 %collective-permute-start.59 = (bf16[128,384]{1,0:T(8,128)(2,1)}, bf16[128,384]{1,0:T(8,128)(2,1)}, u32[]{:S(2)}, u32[]{:S(2)}) collective-permute-start(bf16[128,384]{1,0:T(8,128)(2,1)} %get-tuple-element.229.refs_15_), channel_id=1, source_target_pairs={{0,16},{1,17},{2,18},{3,19},{4,20},{5,21},{6,22},{7,23},{8,24},{9,... | collective-permute-start | bytes 294920 | tf_op jit(solution)/shard_map/ppermute | solution.py:717
  441.1 57.8 %collective-permute-start.67 = (bf16[8,128,384]{2,1,0:T(8,128)(2,1)}, bf16[8,128,384]{2,1,0:T(8,128)(2,1)}, u32[]{:S(2)}, u32[]{:S(2)}) collective-permute-start(bf16[8,128,384]{2,1,0:T(8,128)(2,1)} %get-tuple-element.158), channel_id=1, source_target_pairs={{0,2},{1,3},{2,0},{3,1},{4,6},{5,7},{6,4},{7,5},{8,10},{9,11},{10,... | collective-permute-start | bytes 2359304 | tf_op jit(solution)/shard_map/ppermute | solution.py:717
  444.8 31.3 %collective-permute-start.63 = (bf16[8,48,1664]{2,1,0:T(8,128)(2,1)S(1)}, bf16[8,48,1664]{2,1,0:T(8,128)(2,1)S(1)}, u32[]{:S(2)}, u32[]{:S(2)}) collective-permute-start(bf16[8,48,1664]{2,1,0:T(8,128)(2,1)S(1)} %add_convert_fusion.refs_18_), channel_id=1, source_target_pairs={{0,1},{1,0},{2,3},{3,2},{4,5},{5,4},{6,7},{7,6},{8,9},{9,8},{10,11... | collective-permute-start | bytes 3833864 | tf_op jit(solution)/shard_map/ppermute | solution.py:717
  462.2 36.8 %collective-permute-start.68 = (bf16[8,128,384]{2,1,0:T(8,128)(2,1)S(1)}, bf16[8,128,384]{2,1,0:T(8,128)(2,1)S(1)}, u32[]{:S(2)}, u32[]{:S(2)}) collective-permute-start(bf16[8,128,384]{2,1,0:T(8,128)(2,1)S(1)} %add_convert_fusion.1.refs_15_), channel_id=1, source_target_pairs={{0,1},{1,0},{2,3},{3,2},{4,5},{5,4},{6,7},{7,6},{8,9},{9,8},{10,11... | collective-permute-start | bytes 2359304 | tf_op jit(solution)/shard_map/ppermute | solution.py:717
  544.2 31.6 %collective-permute-start.81 = (bf16[8,48,896]{2,1,0:T(8,128)(2,1)S(1)}, bf16[8,48,896]{2,1,0:T(8,128)(2,1)S(1)}, u32[]{:S(2)}, u32[]{:S(2)}) collective-permute-start(bf16[8,48,896]{2,1,0:T(8,128)(2,1)S(1)} %copy-done.74), channel_id=1, source_target_pairs={{0,2},{1,3},{2,0},{3,1},{4,6},{5,7},{6,4},{7,5},{8,10},{9,11},{10,... | collective-permute-start | bytes 2064392 | tf_op jit(solution)/shard_map/ppermute | solution.py:717
  (152 other events, 2048.9 us)
Sparse Core Ops, SparseCore 0:
  311.0 86.1 reduce-scatter.4
  440.7 111.1 reduce-scatter.2

commit v3 on v2

--- a/solution.py
+++ b/solution.py
@@ -19,9 +19,11 @@
 SMEM = pl.BlockSpec(memory_space=pltpu.SMEM)
 VMEM = pl.BlockSpec(memory_space=pltpu.VMEM)
 ANY = pl.BlockSpec(memory_space=pl.ANY)
-VMEM_BYTES = 56 * 1024 * 1024
-Q_TILE = 128
-K_TILE = 256
+VMEM_MIB = dict(
+    gate=2, pre=18, attend=14, post=32, mlp_back=38, mid_back=28, attend_back=28, pre_back=34
+)
+Q_TILE, K_TILE = 128, 128
+Q_BACK, K_BACK = 256, 256
 FLOPS_PER_US = 1.1e9
 IN_PARTS = (
     ([(1.0, "whole")], [(0.5, "whole"), (0.5, "half")], [(1.0, "half")]),
@@ -91,7 +93,7 @@
         out_specs=(*out_specs, *([ANY] * n_ride)),
         scratch_shapes=scratch,
         input_output_aliases={n_in + i: n_out + i for i in range(n_ride)},
-        compiler_params=pltpu.CompilerParams(vmem_limit_bytes=VMEM_BYTES),
+        compiler_params=pltpu.CompilerParams(vmem_limit_bytes=VMEM_MIB[name] * 1024 * 1024),
         cost_estimate=pl.CostEstimate(
             flops=int(micros * FLOPS_PER_US), bytes_accessed=0, transcendentals=0
         ),
@@ -196,11 +198,15 @@
     )
 
 
-def transpose_into(dest, source, first, columns, rows):
-    for col in range(0, columns, 128):
-        for row in range(0, rows, 128):
-            block = source[row : row + 128, first + col : first + col + 128]
-            dest[col : col + 128, row : row + 128] = block.astype(F32).T.astype(BF16)
+def transpose_tiles(dest, source, first, columns, low, high, k_tile):
+    def body(tile, carry):
+        at = pl.ds(pl.multiple_of(tile * k_tile, k_tile), k_tile)
+        for col in range(0, columns, 128):
+            block = source[at, first + col : first + col + 128]
+            dest[col : col + 128, at] = block.astype(F32).T.astype(BF16)
+        return carry
+
+    lax.fori_loop(low, high, body, 0)
 
 
 def attend_kernel(n_kv, low, bands, q_ref, row_ref, col_ref, *refs):
@@ -210,8 +216,8 @@
     total = kv_s.shape[0]
     load_bands(bands, kv_refs, kv_s, sem)
     wait_whole(kv_s, sem)
-    transpose_into(vt_s, kv_s, width, width, total)
     first = bands[0] * tokens
+    transpose_tiles(vt_s, kv_s, width, width, low[0] // K_TILE, (first + tokens - 1) // K_TILE + 1, K_TILE)
     lse_ref[...] = jnp.zeros_like(lse_ref)
 
     def q_step(q_index, carry):
@@ -248,7 +254,7 @@
             return inner
 
         high = (first + q_at + Q_TILE - 1) // K_TILE + 1
-        lax.fori_loop(low[q_index], high, k_step, 0)
+        lax.fori_loop(low[q_index] // K_TILE, high, k_step, 0)
         for pair in range(HEADS // 2):
             lanes = slice(128 * pair, 128 * pair + 128)
             scale = 1.0 / sum_s[pair : pair + 1, :]
@@ -484,6 +490,7 @@
     dkv_refs = refs[n_kv + 1 : 2 * n_kv + 1]
     kv_s, kt_s, dqt_s, dkv_s, dlow_s, delta_s, sem = refs[2 * n_kv + 1 :]
     tokens, width = q_ref.shape
+    q_tile = min(Q_BACK, tokens)
     total = kv_s.shape[0]
     load_bands(bands, kv_refs, kv_s, sem)
     head_of = lax.broadcasted_iota(jnp.int32, (16, width), 1) // HEAD_DIM
@@ -494,19 +501,19 @@
     delta_s[...] = dot_nt(picks, upper) + dot_nt(picks, lower)
     dkv_s[...] = jnp.zeros_like(dkv_s)
     wait_whole(kv_s, sem)
-    transpose_into(kt_s, kv_s, 0, width, total)
     first = bands[0] * tokens
+    transpose_tiles(kt_s, kv_s, 0, width, low[0] // K_BACK, (first + tokens - 1) // K_BACK + 1, K_BACK)
 
     def q_step(q_index, carry):
-        q_at = pl.multiple_of(q_index * Q_TILE, Q_TILE)
-        q_rows = pl.ds(q_at, Q_TILE)
+        q_at = pl.multiple_of(q_index * q_tile, q_tile)
+        q_rows = pl.ds(q_at, q_tile)
         dqt_s[...] = jnp.zeros_like(dqt_s)
         mark_row = row_ref[0:1, q_rows]
 
         def k_step(k_index, inner):
-            k_at = pl.multiple_of(k_index * K_TILE, K_TILE)
-            k_rows = pl.ds(k_at, K_TILE)
-            bias = bias_tile(col_ref[k_rows, :], mark_row, k_at, first + q_at, K_TILE, Q_TILE)
+            k_at = pl.multiple_of(k_index * K_BACK, K_BACK)
+            k_rows = pl.ds(k_at, K_BACK)
+            bias = bias_tile(col_ref[k_rows, 0:1], mark_row, k_at, first + q_at, K_BACK, q_tile)
             bias = jnp.concatenate([bias, bias], 1)
             for pair in range(HEADS // 2):
                 lanes = slice(128 * pair, 128 * pair + 128)
@@ -527,12 +534,12 @@
                 dkv_s[k_rows, lanes] += dot(d_scores, queries)
                 for side in (0, 1):
                     heads = slice(128 * pair + 64 * side, 128 * pair + 64 * side + 64)
-                    part = slice(Q_TILE * side, Q_TILE * side + Q_TILE)
+                    part = slice(q_tile * side, q_tile * side + q_tile)
                     dqt_s[heads, :] += dot(kt_s[heads, k_rows], d_scores[:, part])
             return inner
 
-        high = (first + q_at + Q_TILE - 1) // K_TILE + 1
-        lax.fori_loop(low[q_index], high, k_step, 0)
+        high = (first + q_at + q_tile - 1) // K_BACK + 1
+        lax.fori_loop(low[q_at // Q_TILE] // K_BACK, high, k_step, 0)
         cosine, sine = cos_ref[q_rows, :], sin_ref[q_rows, :]
         for pair in range(HEADS // 2):
             lanes = slice(128 * pair, 128 * pair + 128)
@@ -540,7 +547,7 @@
             dq_ref[q_rows, lanes] = (block * cosine - swap_halves(block) * sine).astype(BF16)
         return carry
 
-    lax.fori_loop(0, tokens // Q_TILE, q_step, 0)
+    lax.fori_loop(0, tokens // q_tile, q_step, 0)
     for index, ref in enumerate(dkv_refs):
         at = pl.multiple_of(bands[index + 1] * tokens, tokens)
         dlow_s[index] = dkv_s[pl.ds(at, tokens), :].astype(BF16)
@@ -563,7 +570,7 @@
         [
             pltpu.VMEM((total, 2 * width), BF16),
             pltpu.VMEM((width, total), BF16),
-            pltpu.VMEM((width, Q_TILE), F32),
+            pltpu.VMEM((width, min(Q_BACK, tokens)), F32),
             pltpu.VMEM((total, 2 * width), F32),
             pltpu.VMEM((n_kv, tokens, 2 * width), BF16),
             pltpu.VMEM((16, tokens), F32),
@@ -966,7 +973,7 @@
         marks_all = jnp.concatenate(pieces)
     mark_col = jnp.broadcast_to(marks_all[:, None], (total, 128))
     reach = jnp.where(starts_mine >= 0, starts_mine, index)
-    low = (jnp.min(reach.reshape(-1, Q_TILE), 1) // K_TILE).astype(jnp.int32)
+    low = jnp.min(reach.reshape(-1, Q_TILE), 1).astype(jnp.int32)
 
     in_widths = (qkv_cols(width), width + 2 * ff, width)
     out_widths = (width + qkv_cols(width), 2 * ff, width)

time: 648 us -> 609 us (0.940)
  Pallas kernels: 219 us -> 163 us
  local copies, waits for them, and re-layouts: 35.4 us -> 51.4 us
  waiting for transfers between devices: 213 us -> 227 us
  starting transfers between devices: 116 us -> 109 us
    pallas_call x19, Pallas kernels: 219 us -> 163 us  [call(): pl.pallas_call(wrapped, name=name, out_shape=(*out_shape, *(jax.ShapeDtyp...]
    unnamed x174 -> x294, local copies, waits for them, and re-layouts: 16 us -> 41.9 us
    ppermute x95, waiting for transfers between devices: 212 us -> 227 us  [send(): return lax.ppermute(value, BOTH, self.pairs(move))]
    reduce_scatter x2, starting transfers between devices: 9.94 us -> 0.54 us  [__init__(): lax.psum_scatter(stack[0][0], 'rows', scatter_dimension=0, tiled=True)]
  transfers between devices with their start and end apart: 99 -> 99, of which waited for: 31 -> 35; matrix products, arithmetic and copies ran while one was open for 10% -> 7% of each run, Pallas kernels for 31% -> 24%
where the time goes in v3:
time: 609 us; the launch traced here: 600 us
  waiting for transfers between devices  227 us (37%)
  Pallas kernels  163 us (27%)
  starting transfers between devices  109 us (18%)
  local copies, waits for them, and re-layouts  51.4 us (8%)
  other arithmetic  32.4 us (5%)
  between operations  17 us (3%)
    ppermute x95, waiting for transfers between devices, send(): return lax.ppermute(value, BOTH, self.pairs(move))  227 us
    pallas_call x19, Pallas kernels, call(): pl.pallas_call(wrapped, name=name, out_shape=(*out_shape, *(jax.ShapeDtyp...  163 us
    ppermute x95, starting transfers between devices, send(): return lax.ppermute(value, BOTH, self.pairs(move))  100 us
    unnamed x294, local copies, waits for them, and re-layouts  41.9 us
  transfers between devices with their start and end apart: 99, of which 35 were waited for; matrix products, arithmetic and copies ran while one was open for 7% of the time, Pallas kernels for 24%

profile of v3, /device:TPU:0, one launch (start us, length us, event | category | flops | bytes accessed | tf_op | source)
XLA Modules:
  0.0 600.1 jit_solution(16068101371011154494)
XLA Ops:
  33.8 8.4 %collective-permute-done.3 = bf16[48,2560]{1,0:T(8,128)(2,1)} collective-permute-done((bf16[48,2560]{1,0:T(8,128)(2,1)}, bf16[48,2560]{1,0:T(8,128)(2,1)}, u32[]{:S(2)}, u32[]{:S(2)}) %collective-permute-start.3) | collective-permute-done | bytes 245792 | tf_op jit(solution)/shard_map/ppermute | solution.py:724
  63.0 13.3 %collective-permute-done.5.refs_5_.refs_14_ = bf16[4,48,2560]{2,1,0:T(8,128)(2,1)S(1)} collective-permute-done((bf16[4,48,2560]{2,1,0:T(8,128)(2,1)S(1)}, bf16[4,48,2560]{2,1,0:T(8,128)(2,1)S(1)}, u32[]{:S(2)}, u32[]{:S(2)}) %collective-permute-start.5) | collective-permute-done | bytes 983072 | tf_op jit(solution)/shard_map/ppermute | solution.py:724
  91.0 9.5 %pre.2 = (bf16[512,768]{1,0:T(8,128)(2,1)S(1)}, bf16[512,1536]{1,0:T(8,128)(2,1)S(1)}, f32[8,768]{1,0:T(8,128)S(1)}, bf16[48,2560]{1,0:T(8,128)(2,1)S(1)}, bf16[...) custom-call(s32[2,16]{1,0:T(2,128)S(1)} %stack.279.refs_0_, ...), custom_call_target="tpu_custom_call", output_to_operand_aliasing={{3}: (8, {}), {4}: (9, {}), {5}: (10, {})} | custom-call | flops 7699999744 | tf_op jit(solution)/shard_map/pre/pallas_call | solution.py:88
  116.3 9.0 %collective-permute-done.32 = bf16[48,1280]{1,0:T(8,128)(2,1)S(1)} collective-permute-done((bf16[48,1280]{1,0:T(8,128)(2,1)S(1)}, bf16[48,1280]{1,0:T(8,128)(2,1)S(1)}, u32[]{:S(2)}, u32[]{:S(2)}) %collective-permute-start.32) | collective-permute-done | bytes 122912 | tf_op jit(solution)/shard_map/ppermute | solution.py:724
  127.6 11.8 %collective-permute-done.20.refs_10_ = bf16[8,48,1152]{2,1,0:T(8,128)(2,1)S(1)} collective-permute-done((bf16[8,48,1152]{2,1,0:T(8,128)(2,1)}, bf16[8,48,1152]{2,1,0:T(8,128)(2,1)S(1)}, u32[]{:S(2)}, u32[]{:S(2)}) %collective-permute-start.20) | collective-permute-done | bytes 884768 | tf_op jit(solution)/shard_map/ppermute | solution.py:724
  140.1 14.4 %collective-permute-done.40 = bf16[48,4864]{1,0:T(8,128)(2,1)S(1)} collective-permute-done((bf16[48,4864]{1,0:T(8,128)(2,1)S(1)}, bf16[48,4864]{1,0:T(8,128)(2,1)S(1)}, u32[]{:S(2)}, u32[]{:S(2)}) %collective-permute-start.40) | collective-permute-done | bytes 466976 | tf_op jit(solution)/shard_map/ppermute | solution.py:724
  169.5 13.2 %collective-permute-done.34.refs_5_.refs_14_ = bf16[8,48,1280]{2,1,0:T(8,128)(2,1)S(1)} collective-permute-done((bf16[8,48,1280]{2,1,0:T(8,128)(2,1)S(1)}, bf16[8,48,1280]{2,1,0:T(8,128)(2,1)S(1)}, u32[]{:S(2)}, u32[]{:S(2)}) %collective-permute-start.34) | collective-permute-done | bytes 983072 | tf_op jit(solution)/shard_map/ppermute | solution.py:724
  182.8 11.3 %post.2 = (f32[512,768]{1,0:T(8,128)S(1)}, f32[512,768]{1,0:T(8,128)S(1)}, bf16[512,4096]{1,0:T(8,128)(2,1)S(1)}) custom-call(s32[2,48]{1,0:T(2,128)S(1)} %pad_add_fusion.4.refs_0_, s32[2,32]{1,0:T(2,128)S(1)} %get-tuple-element.259.refs_1_.refs_0_, bf16[512,768]{1,0:T(8,128)(2,1)} %collective-permute-done.refs_1_.refs_2_, ...), custom_call_target="tpu_custom_call" | custom-call | flops 15399999488 | tf_op jit(solution)/shard_map/post/pallas_call | solution.py:88
  199.5 21.5 %collective-permute-done.47 = bf16[4,128,384]{2,1,0:T(8,128)(2,1)S(1)} collective-permute-done((bf16[4,128,384]{2,1,0:T(8,128)(2,1)S(1)}, bf16[4,128,384]{2,1,0:T(8,128)(2,1)S(1)}, u32[]{:S(2)}, u32[]{:S(2)}) %collective-permute-start.47) | collective-permute-done | bytes 393248 | tf_op jit(solution)/shard_map/ppermute | solution.py:724
  223.5 16.8 %collective-permute-done.48.refs_10_.refs_8_ = bf16[8,128,384]{2,1,0:T(8,128)(2,1)S(1)} collective-permute-done((bf16[8,128,384]{2,1,0:T(8,128)(2,1)S(1)}, bf16[8,128,384]{2,1,0:T(8,128)(2,1)S(1)}, u32[]{:S(2)}, u32[]{:S(2)}) %collective-permute-start.48) | collective-permute-done | bytes 786464 | tf_op jit(solution)/shard_map/ppermute | solution.py:724
  240.8 7.8 %attend.3 = (bf16[512,768]{1,0:T(8,128)(2,1)S(1)}, f32[16,512]{1,0:T(8,128)S(1)}) custom-call(s32[4]{0:T(128)S(1)} %fusion.9.refs_0_, s32[3]{0:T(128)S(1)} %pad_add_fusion.6.refs_1_, bf16[512,768]{1,0:T(8,128)(2,1)S(1)} %get-tuple-element.105.refs_2_, s32[8,512]{1,0:T(8,128)S(1)} %broadcast_in_dim.13.refs_3_.refs_6_, ...), custom_call_target="tpu_custom_call" | custom-call | flops 16499999744 | tf_op jit(solution)/shard_map/attend/pallas_call | solution.py:88
  248.7 13.1 %post.3 = (f32[512,768]{1,0:T(8,128)S(1)}, f32[512,768]{1,0:T(8,128)S(1)}, bf16[512,4096]{1,0:T(8,128)(2,1)S(1)}) custom-call(s32[2,16]{1,0:T(2,128)S(1)} %stack.279.refs_0_, s32[2,32]{1,0:T(2,128)S(1)} %get-tuple-element.259.refs_1_.refs_0_, f32[512,768]{1,0:T(8,128)S(1)} %get-tuple-element.103.refs_1_.refs_2_, ...), custom_call_target="tpu_custom_call" | custom-call | flops 15399999488 | tf_op jit(solution)/shard_map/post/pallas_call | solution.py:88
  264.9 18.5 %mlp_back.2 = (bf16[512,4096]{1,0:T(8,128)(2,1)S(1)}, bf16[1,768,4096]{2,1,0:T(8,128)(2,1)}, bf16[8,128,384]{2,1,0:T(8,128)(2,1)S(1)}, bf16[8,128,384]{2,1,0:T(8...) custom-call(s32[2,32]{1,0:T(2,128)S(1)} %get-tuple-element.259.refs_1_.refs_0_, ...), custom_call_target="tpu_custom_call" | custom-call | flops 22000001024 | tf_op jit(solution)/shard_map/mlp_back/pallas_call | solution.py:88
  298.8 11.4 %mid_back.2 = (f32[512,768]{1,0:T(8,128)S(1)}, bf16[512,768]{1,0:T(8,128)(2,1)S(1)}, bf16[512,768]{1,0:T(8,128)(2,1)S(1)}, f32[8,768]{1,0:T(8,128)S(1)}, bf16[8,...) custom-call(s32[2,16]{1,0:T(2,128)S(1)} %stack.279.refs_0_, ...), custom_call_target="tpu_custom_call", output_to_operand_aliasing={{4}: (9, {}), {5}: (10, {})} | custom-call | flops 14300000256 | tf_op jit(solution)/shard_map/mid_back/pallas_call | solution.py:88
  313.1 10.8 %attend_back.2 = (bf16[512,768]{1,0:T(8,128)(2,1)S(1)}, bf16[512,1536]{1,0:T(8,128)(2,1)S(1)}, bf16[512,1536]{1,0:T(8,128)(2,1)S(1)}, bf16[8,128,384]{2,1,0:T(8,128)(2,1)S(1)}) custom-call(s32[4]{0:T(128)S(1)} %fusion.9.refs_0_, s32[3]{0:T(128)S(1)} %pad_add_fusion.6.refs_1_, bf16[512,768]{1,0:T(8,128)(2,1)S(1)} %copy-done.99, ...), custom_call_target="tpu_custom_call", output_to_operand_aliasing={{3}: (12, {})} | custom-call | flops 22000001024 | tf_op jit(solution)/shard_map/attend_back/pallas_call | solution.py:88
  330.6 7.6 %collective-permute-start.51 = (bf16[512,768]{1,0:T(8,128)(2,1)}, bf16[512,768]{1,0:T(8,128)(2,1)}, u32[]{:S(2)}, u32[]{:S(2)}) collective-permute-start(bf16[512,768]{1,0:T(8,128)(2,1)} %convert_element_type.268), channel_id=1, source_target_pairs={{0,0},{2,1},{1,2},{3,3},{4,4},{6,5},{5,6},{7,7},{8,8},{10,9},{9,10... | collective-permute-start | bytes 2359304 | tf_op jit(solution)/shard_map/ppermute | solution.py:750
  345.6 17.3 %collective-permute-done.56 = bf16[8,128,384]{2,1,0:T(8,128)(2,1)} collective-permute-done((bf16[8,128,384]{2,1,0:T(8,128)(2,1)S(1)}, bf16[8,128,384]{2,1,0:T(8,128)(2,1)}, u32[]{:S(2)}, u32[]{:S(2)}) %collective-permute-start.56) | collective-permute-done | bytes 786464 | tf_op jit(solution)/shard_map/ppermute | solution.py:724
  369.8 11.4 %pre_back.2 = (f32[512,768]{1,0:T(8,128)S(1)}, bf16[8,48,1664]{2,1,0:T(8,128)(2,1)S(1)}, bf16[8,48,1664]{2,1,0:T(8,128)(2,1)S(1)}, bf16[8,48,1664]{2,1,0:T(8,128...) custom-call(s32[2,32]{1,0:T(2,128)S(1)} %get-tuple-element.260.refs_0_, ...), custom_call_target="tpu_custom_call", output_to_operand_aliasing={{5}: (17, {})} | custom-call | flops 16499999744 | tf_op jit(solution)/shard_map/pre_back/pallas_call | solution.py:88
  389.5 19.5 %mlp_back.3 = (bf16[512,4096]{1,0:T(8,128)(2,1)}, bf16[1,768,4096]{2,1,0:T(8,128)(2,1)}, bf16[8,128,384]{2,1,0:T(8,128)(2,1)S(1)}, bf16[8,128,384]{2,1,0:T(8,128...) custom-call(s32[2,32]{1,0:T(2,128)S(1)} %copy-done.34, ...), custom_call_target="tpu_custom_call", output_to_operand_aliasing={{6}: (11, {}), {7}: (12, {}), {8}: (13, {})} | custom-call | flops 22000001024 | tf_op jit(solution)/shard_map/mlp_back/pallas_call | solution.py:88
  426.8 9.3 %mid_back.3 = (f32[512,768]{1,0:T(8,128)S(1)}, bf16[512,768]{1,0:T(8,128)(2,1)S(1)}, bf16[512,768]{1,0:T(8,128)(2,1)S(1)}, f32[8,768]{1,0:T(8,128)S(1)}, bf16[12...) custom-call(s32[2,48]{1,0:T(2,128)S(1)} %copy-done.29, ...), custom_call_target="tpu_custom_call", output_to_operand_aliasing={{4}: (13, {}), {5}: (14, {}), {6}: (15, {}), {7}: (16, {})} | custom-call | flops 14300000256 | tf_op jit(solution)/shard_map/mid_back/pallas_call | solution.py:88
  438.9 8.0 %collective-permute-done.63 = bf16[8,48,1664]{2,1,0:T(8,128)(2,1)S(1)} collective-permute-done((bf16[8,48,1664]{2,1,0:T(8,128)(2,1)S(1)}, bf16[8,48,1664]{2,1,0:T(8,128)(2,1)S(1)}, u32[]{:S(2)}, u32[]{:S(2)}) %collective-permute-start.63) | collective-permute-done | bytes 1277984 | tf_op jit(solution)/shard_map/ppermute | solution.py:724
  449.7 11.0 %attend_back.3 = (bf16[512,768]{1,0:T(8,128)(2,1)S(1)}, bf16[512,1536]{1,0:T(8,128)(2,1)S(1)}, bf16[512,1536]{1,0:T(8,128)(2,1)S(1)}, f32[4,48,1664]{2,1,0:T(8,128)S(1)}, bf16[8,128,384]{2,1,0:T(8,128)(2,1)S(1)}) custom-call(s32[4]{0:T(128)S(1)} %copy-done.36, s32[3]{0:T(128)S(1)} %copy-done.88, ...), custom_call_target="tpu_custom_call", output_to_operand_aliasing={{3}: (12, {}), {4}: (13, {})} | custom-call | flops 22000001024 | tf_op jit(solution)/shard_map/attend_back/pallas_call | solution.py:88
  479.0 15.1 %pre_back.3 = (f32[512,768]{1,0:T(8,128)S(1)}, bf16[4,48,1536]{2,1,0:T(8,128)(2,1)S(1)}, bf16[4,48,1536]{2,1,0:T(8,128)(2,1)S(1)}, bf16[4,48,1536]{2,1,0:T(8,128...) custom-call(s32[2,16]{1,0:T(2,128)S(1)} %copy-done.27, ...), custom_call_target="tpu_custom_call", output_to_operand_aliasing={{9}: (17, {}), {10}: (18, {})} | custom-call | flops 16499999744 | tf_op jit(solution)/shard_map/pre_back/pallas_call | solution.py:88
  518.9 9.8 %collective-permute-done.95 = bf16[128,384]{1,0:T(8,128)(2,1)S(1)} collective-permute-done((bf16[128,384]{1,0:T(8,128)(2,1)S(1)}, bf16[128,384]{1,0:T(8,128)(2,1)S(1)}, u32[]{:S(2)}, u32[]{:S(2)}) %collective-permute-start.95) | collective-permute-done | bytes 98336 | tf_op jit(solution)/shard_map/ppermute | solution.py:724
  (608 shorter events, 283.6 us)
Async XLA Ops:
  7.2 565.3 %reduce-scatter.5.cloned.1.call-start = ((), (), s32[]{:S(2)}) async-start(), calls=%async_computation.3 | async-start | bytes 6684672 | tf_op jit(solution)/shard_map/reduce_scatter | solution.py:867
  17.3 73.7 %collective-permute-start = (bf16[512,768]{1,0:T(8,128)(2,1)}, bf16[512,768]{1,0:T(8,128)(2,1)}, u32[]{:S(2)}, u32[]{:S(2)}) collective-permute-start(bf16[512,768]{1,0:T(8,128)(2,1)} %bitcast.261), channel_id=1, source_target_pairs={{0,0},{1,2},{2,1},{3,3},{4,4},{5,6},{6,5},{7,7},{8,8},{9,10},{10,9... | collective-permute-start | bytes 2359304 | tf_op jit(solution)/shard_map/ppermute | solution.py:724
  25.4 29.2 %collective-permute-start.16 = (bf16[48,1152]{1,0:T(8,128)(2,1)S(1)}, bf16[48,1152]{1,0:T(8,128)(2,1)S(1)}, u32[]{:S(2)}, u32[]{:S(2)}) collective-permute-start(bf16[48,1152]{1,0:T(8,128)(2,1)S(1)} %get-tuple-element.208), channel_id=1, source_target_pairs={{0,8},{1,9},{2,10},{3,11},{4,12},{5,13},{6,14},{7,15},{8,16},{9,17... | collective-permute-start | bytes 331784 | tf_op jit(solution)/shard_map/ppermute | solution.py:724
  31.9 45.0 %collective-permute-start.10 = (bf16[48,2560]{1,0:T(8,128)(2,1)S(1)}, bf16[48,2560]{1,0:T(8,128)(2,1)}, u32[]{:S(2)}, u32[]{:S(2)}) collective-permute-start(bf16[48,2560]{1,0:T(8,128)(2,1)S(1)} %pad_maximum_fusion.15), channel_id=1, source_target_pairs={{0,8},{1,9},{2,10},{3,11},{4,12},{5,13},{6,14},{7,15},{8,16},{9,17... | collective-permute-start | bytes 737288 | tf_op jit(solution)/shard_map/ppermute | solution.py:724
  62.9 28.0 %collective-permute-start.6 = (bf16[4,48,2560]{2,1,0:T(8,128)(2,1)S(1)}, bf16[4,48,2560]{2,1,0:T(8,128)(2,1)S(1)}, u32[]{:S(2)}, u32[]{:S(2)}) collective-permute-start(bf16[4,48,2560]{2,1,0:T(8,128)(2,1)S(1)} %pad_maximum_fusion.1.refs_4_.refs_13_), channel_id=1, source_target_pairs={{0,2},{1,3},{2,0},{3,1},{4,6},{5,7},{6,4},{7,5},{8,10},{9,11},{10,... | collective-permute-start | bytes 2949128 | tf_op jit(solution)/shard_map/ppermute | solution.py:724
  125.9 34.9 %collective-permute-start.9 = (bf16[512,1536]{1,0:T(8,128)(2,1)S(1)}, bf16[512,1536]{1,0:T(8,128)(2,1)S(1)}, u32[]{:S(2)}, u32[]{:S(2)}) collective-permute-start(bf16[512,1536]{1,0:T(8,128)(2,1)S(1)} %get-tuple-element.100.refs_5_.refs_10_), channel_id=1, source_target_pairs={{0,2},{1,3},{2,0},{3,1},{4,6},{5,7},{6,4},{7,5},{8,10},{9,11},{10,... | collective-permute-start | bytes 4718600 | tf_op jit(solution)/shard_map/ppermute | solution.py:724
  126.0 30.9 %collective-permute-start.13 = (bf16[4,48,2560]{2,1,0:T(8,128)(2,1)S(1)}, bf16[4,48,2560]{2,1,0:T(8,128)(2,1)S(1)}, u32[]{:S(2)}, u32[]{:S(2)}) collective-permute-start(bf16[4,48,2560]{2,1,0:T(8,128)(2,1)S(1)} %pad_maximum_fusion.2.refs_5_), channel_id=1, source_target_pairs={{0,4},{1,5},{2,6},{3,7},{4,0},{5,1},{6,2},{7,3},{8,12},{9,13},{10,... | collective-permute-start | bytes 2949128 | tf_op jit(solution)/shard_map/ppermute | solution.py:724
  169.1 29.8 %collective-permute-start.46 = (bf16[128,384]{1,0:T(8,128)(2,1)S(1)}, bf16[128,384]{1,0:T(8,128)(2,1)S(1)}, u32[]{:S(2)}, u32[]{:S(2)}) collective-permute-start(bf16[128,384]{1,0:T(8,128)(2,1)S(1)} %collective-permute-done.45), channel_id=1, source_target_pairs={{0,8},{1,9},{2,10},{3,11},{4,12},{5,13},{6,14},{7,15},{8,16},{9,17... | collective-permute-start | bytes 294920 | tf_op jit(solution)/shard_map/ppermute | solution.py:724
  169.5 52.8 %collective-permute-start.41 = (bf16[4,48,4864]{2,1,0:T(8,128)(2,1)S(1)}, bf16[4,48,4864]{2,1,0:T(8,128)(2,1)S(1)}, u32[]{:S(2)}, u32[]{:S(2)}) collective-permute-start(bf16[4,48,4864]{2,1,0:T(8,128)(2,1)S(1)} %pad_maximum_fusion.refs_5_), channel_id=1, source_target_pairs={{0,4},{1,5},{2,6},{3,7},{4,0},{5,1},{6,2},{7,3},{8,12},{9,13},{10,... | collective-permute-start | bytes 5603336 | tf_op jit(solution)/shard_map/ppermute | solution.py:724
  198.6 41.7 %collective-permute-start.37 = (bf16[512,1536]{1,0:T(8,128)(2,1)S(1)}, bf16[512,1536]{1,0:T(8,128)(2,1)S(1)}, u32[]{:S(2)}, u32[]{:S(2)}) collective-permute-start(bf16[512,1536]{1,0:T(8,128)(2,1)S(1)} %get-tuple-element.106.refs_5_.refs_10_), channel_id=1, source_target_pairs={{0,2},{1,3},{2,0},{3,1},{4,6},{5,7},{6,4},{7,5},{8,10},{9,11},{10,... | collective-permute-start | bytes 4718600 | tf_op jit(solution)/shard_map/ppermute | solution.py:724
  222.3 26.4 %collective-permute-start.42 = (bf16[4,48,4864]{2,1,0:T(8,128)(2,1)S(1)}, bf16[4,48,4864]{2,1,0:T(8,128)(2,1)S(1)}, u32[]{:S(2)}, u32[]{:S(2)}) collective-permute-start(bf16[4,48,4864]{2,1,0:T(8,128)(2,1)S(1)} %pad_maximum_fusion.refs_5_), channel_id=1, source_target_pairs={{0,2},{1,3},{2,0},{3,1},{4,6},{5,7},{6,4},{7,5},{8,10},{9,11},{10,... | collective-permute-start | bytes 5603336 | tf_op jit(solution)/shard_map/ppermute | solution.py:724
  222.3 26.4 %collective-permute-start.43 = (bf16[4,48,4864]{2,1,0:T(8,128)(2,1)S(1)}, bf16[4,48,4864]{2,1,0:T(8,128)(2,1)S(1)}, u32[]{:S(2)}, u32[]{:S(2)}) collective-permute-start(bf16[4,48,4864]{2,1,0:T(8,128)(2,1)S(1)} %collective-permute-done.41.refs_6_), channel_id=1, source_target_pairs={{0,2},{1,3},{2,0},{3,1},{4,6},{5,7},{6,4},{7,5},{8,10},{9,11},{10,... | collective-permute-start | bytes 5603336 | tf_op jit(solution)/shard_map/ppermute | solution.py:724
  222.8 42.1 %collective-permute-start.52 = (bf16[512,768]{1,0:T(8,128)(2,1)S(1)}, bf16[512,768]{1,0:T(8,128)(2,1)S(1)}, u32[]{:S(2)}, u32[]{:S(2)}) collective-permute-start(bf16[512,768]{1,0:T(8,128)(2,1)S(1)} %bitcast.262), channel_id=1, source_target_pairs={{0,0},{1,2},{2,1},{3,3},{4,4},{5,6},{6,5},{7,7},{8,8},{9,10},{10,9... | collective-permute-start | bytes 2359304 | tf_op jit(solution)/shard_map/ppermute | solution.py:724
  287.6 294.9 %reduce-scatter.3.cloned.1.call-start = ((), (), s32[]{:S(2)}) async-start(), calls=%async_computation.2 | async-start | bytes 6684672 | tf_op jit(solution)/shard_map/reduce_scatter | solution.py:867
  324.8 40.3 %collective-permute-start.54 = (bf16[512,1536]{1,0:T(8,128)(2,1)S(1)}, bf16[512,1536]{1,0:T(8,128)(2,1)}, u32[]{:S(2)}, u32[]{:S(2)}) collective-permute-start(bf16[512,1536]{1,0:T(8,128)(2,1)S(1)} %get-tuple-element.127), channel_id=1, source_target_pairs={{0,2},{1,3},{2,0},{3,1},{4,6},{5,7},{6,4},{7,5},{8,10},{9,11},{10,... | collective-permute-start | bytes 4718600 | tf_op jit(solution)/shard_map/ppermute | solution.py:724
  381.2 32.9 %collective-permute-start.61 = (bf16[8,48,1664]{2,1,0:T(8,128)(2,1)}, bf16[8,48,1664]{2,1,0:T(8,128)(2,1)}, u32[]{:S(2)}, u32[]{:S(2)}) collective-permute-start(bf16[8,48,1664]{2,1,0:T(8,128)(2,1)} %get-tuple-element.142), channel_id=1, source_target_pairs={{0,2},{1,3},{2,0},{3,1},{4,6},{5,7},{6,4},{7,5},{8,10},{9,11},{10,... | collective-permute-start | bytes 3833864 | tf_op jit(solution)/shard_map/ppermute | solution.py:724
  382.2 28.6 %collective-permute-start.58 = (bf16[128,384]{1,0:T(8,128)(2,1)}, bf16[128,384]{1,0:T(8,128)(2,1)}, u32[]{:S(2)}, u32[]{:S(2)}) collective-permute-start(bf16[128,384]{1,0:T(8,128)(2,1)} %get-tuple-element.230.refs_14_), channel_id=1, source_target_pairs={{0,8},{1,9},{2,10},{3,11},{4,12},{5,13},{6,14},{7,15},{8,16},{9,17... | collective-permute-start | bytes 294920 | tf_op jit(solution)/shard_map/ppermute | solution.py:724
  383.7 27.7 %collective-permute-start.59 = (bf16[128,384]{1,0:T(8,128)(2,1)}, bf16[128,384]{1,0:T(8,128)(2,1)}, u32[]{:S(2)}, u32[]{:S(2)}) collective-permute-start(bf16[128,384]{1,0:T(8,128)(2,1)} %get-tuple-element.229.refs_15_), channel_id=1, source_target_pairs={{0,16},{1,17},{2,18},{3,19},{4,20},{5,21},{6,22},{7,23},{8,24},{9,... | collective-permute-start | bytes 294920 | tf_op jit(solution)/shard_map/ppermute | solution.py:724
  410.8 28.1 %collective-permute-start.62 = (bf16[8,48,1664]{2,1,0:T(8,128)(2,1)}, bf16[8,48,1664]{2,1,0:T(8,128)(2,1)S(1)}, u32[]{:S(2)}, u32[]{:S(2)}) collective-permute-start(bf16[8,48,1664]{2,1,0:T(8,128)(2,1)} %copy-done.51), channel_id=1, source_target_pairs={{0,2},{1,3},{2,0},{3,1},{4,6},{5,7},{6,4},{7,5},{8,10},{9,11},{10,... | collective-permute-start | bytes 3833864 | tf_op jit(solution)/shard_map/ppermute | solution.py:724
  411.4 52.8 %collective-permute-start.67 = (bf16[8,128,384]{2,1,0:T(8,128)(2,1)}, bf16[8,128,384]{2,1,0:T(8,128)(2,1)S(1)}, u32[]{:S(2)}, u32[]{:S(2)}) collective-permute-start(bf16[8,128,384]{2,1,0:T(8,128)(2,1)} %copy-done.82), channel_id=1, source_target_pairs={{0,2},{1,3},{2,0},{3,1},{4,6},{5,7},{6,4},{7,5},{8,10},{9,11},{10,... | collective-permute-start | bytes 2359304 | tf_op jit(solution)/shard_map/ppermute | solution.py:724
  415.9 31.0 %collective-permute-start.63 = (bf16[8,48,1664]{2,1,0:T(8,128)(2,1)S(1)}, bf16[8,48,1664]{2,1,0:T(8,128)(2,1)S(1)}, u32[]{:S(2)}, u32[]{:S(2)}) collective-permute-start(bf16[8,48,1664]{2,1,0:T(8,128)(2,1)S(1)} %add_convert_fusion.refs_18_), channel_id=1, source_target_pairs={{0,1},{1,0},{2,3},{3,2},{4,5},{5,4},{6,7},{7,6},{8,9},{9,8},{10,11... | collective-permute-start | bytes 3833864 | tf_op jit(solution)/shard_map/ppermute | solution.py:724
  437.5 26.7 %collective-permute-start.68 = (bf16[8,128,384]{2,1,0:T(8,128)(2,1)S(1)}, bf16[8,128,384]{2,1,0:T(8,128)(2,1)S(1)}, u32[]{:S(2)}, u32[]{:S(2)}) collective-permute-start(bf16[8,128,384]{2,1,0:T(8,128)(2,1)S(1)} %add_convert_fusion.1.refs_15_), channel_id=1, source_target_pairs={{0,1},{1,0},{2,3},{3,2},{4,5},{5,4},{6,7},{7,6},{8,9},{9,8},{10,11... | collective-permute-start | bytes 2359304 | tf_op jit(solution)/shard_map/ppermute | solution.py:724
  464.6 31.2 %collective-permute-start.73 = (bf16[4,128,384]{2,1,0:T(8,128)(2,1)S(1)}, bf16[4,128,384]{2,1,0:T(8,128)(2,1)S(1)}, u32[]{:S(2)}, u32[]{:S(2)}) collective-permute-start(bf16[4,128,384]{2,1,0:T(8,128)(2,1)S(1)} %slice.379.refs_23_), channel_id=1, source_target_pairs={{0,4},{1,5},{2,6},{3,7},{4,0},{5,1},{6,2},{7,3},{8,12},{9,13},{10,... | collective-permute-start | bytes 1179656 | tf_op jit(solution)/shard_map/ppermute | solution.py:724
  511.7 28.1 %collective-permute-start.81 = (bf16[8,48,896]{2,1,0:T(8,128)(2,1)S(1)}, bf16[8,48,896]{2,1,0:T(8,128)(2,1)S(1)}, u32[]{:S(2)}, u32[]{:S(2)}) collective-permute-start(bf16[8,48,896]{2,1,0:T(8,128)(2,1)S(1)} %get-tuple-element.176), channel_id=1, source_target_pairs={{0,2},{1,3},{2,0},{3,1},{4,6},{5,7},{6,4},{7,5},{8,10},{9,11},{10,... | collective-permute-start | bytes 2064392 | tf_op jit(solution)/shard_map/ppermute | solution.py:724
  (212 other events, 4753.7 us)
Sparse Core Ops, SparseCore 0:
  287.7 87.7 reduce-scatter.4
  410.9 110.6 reduce-scatter.2

commit v4 on v3

--- a/solution.py
+++ b/solution.py
@@ -1052,12 +1052,12 @@
     chains = [None] * LAYERS
     live = []
 
-    def through(kernel, *args, **more):
+    def through(kernel, *args, still=(), **more):
         if not ringed:
             return kernel(*args, **more)[0]
         sent = more.pop("before", [])
         for chain in live:
-            if chain.level < 9:
+            if chain.level < 9 and chain not in still:
                 sent = sent + (chain.step() if chain.old else [])
             chain.old = True
         holders = [chain for chain in live if chain.sum is None and chain.level < 9]
@@ -1124,13 +1124,23 @@
             dkv_list,
             w_qkv,
             before=[output] if layer == 0 else [],
+            still=live if layer > 0 else [],
         )
         flow = results[0]
         c_qkv = scatters(results[1:], p_qkv)
         live += c_qkv
         chains[layer] = (c_qkv, c_gu, c_down)
+    laps = 0
     while ringed and any(chain.sum is None and chain.level < 9 for chain in live):
-        through(lambda ride, before: ([], gate(before, ride)))
+        done = [
+            value
+            for layer, lap in ((1, 0), (0, 2))
+            for chain in chains[layer][1]
+            if chain.level == 9 and lap == laps
+            for value in chain.flying
+        ]
+        through(lambda ride, before: ([], gate(before, ride)), before=done)
+        laps += 1
     grads = [[joined(part) for part in chains[layer]] for layer in range(LAYERS)]
     grad_input = lay.out_of_groups(flow.astype(BF16)).astype(F32)
 

time: 609 us -> 593 us (0.974)
  waiting for transfers between devices: 227 us -> 198 us
  local copies, waits for them, and re-layouts: 51.4 us -> 63.2 us
    ppermute x95, waiting for transfers between devices: 227 us -> 198 us  [send(): return lax.ppermute(value, BOTH, self.pairs(move))]
    unnamed x294 -> x290, local copies, waits for them, and re-layouts: 41.9 us -> 51.3 us
  transfers between devices with their start and end apart: 99 -> 99, of which waited for: 35 -> 26; matrix products, arithmetic and copies ran while one was open for 7% -> 8% of each run, Pallas kernels for 24% -> 25%
where the time goes in v4:
time: 593 us; the launch traced here: 583 us
  waiting for transfers between devices  198 us (33%)
  Pallas kernels  164 us (28%)
  starting transfers between devices  106 us (18%)
  local copies, waits for them, and re-layouts  63.2 us (11%)
  other arithmetic  35.3 us (6%)
  between operations  16.8 us (3%)
    ppermute x95, waiting for transfers between devices, send(): return lax.ppermute(value, BOTH, self.pairs(move))  198 us
    pallas_call x19, Pallas kernels, call(): pl.pallas_call(wrapped, name=name, out_shape=(*out_shape, *(jax.ShapeDtyp...  164 us
    ppermute x95, starting transfers between devices, send(): return lax.ppermute(value, BOTH, self.pairs(move))  96.1 us
    unnamed x290, local copies, waits for them, and re-layouts  51.3 us
  transfers between devices with their start and end apart: 99, of which 26 were waited for; matrix products, arithmetic and copies ran while one was open for 8% of the time, Pallas kernels for 25%

profile of v4, /device:TPU:0, one launch (start us, length us, event | category | flops | bytes accessed | tf_op | source)
XLA Modules:
  0.0 583.0 jit_solution(1467844574859948301)
XLA Ops:
  32.1 8.4 %collective-permute-done.3 = bf16[48,2560]{1,0:T(8,128)(2,1)} collective-permute-done((bf16[48,2560]{1,0:T(8,128)(2,1)}, bf16[48,2560]{1,0:T(8,128)(2,1)}, u32[]{:S(2)}, u32[]{:S(2)}) %collective-permute-start.3) | collective-permute-done | bytes 245792 | tf_op jit(solution)/shard_map/ppermute | solution.py:724
  61.3 13.3 %collective-permute-done.5.refs_5_.refs_14_ = bf16[4,48,2560]{2,1,0:T(8,128)(2,1)S(1)} collective-permute-done((bf16[4,48,2560]{2,1,0:T(8,128)(2,1)S(1)}, bf16[4,48,2560]{2,1,0:T(8,128)(2,1)S(1)}, u32[]{:S(2)}, u32[]{:S(2)}) %collective-permute-start.5) | collective-permute-done | bytes 983072 | tf_op jit(solution)/shard_map/ppermute | solution.py:724
  89.3 9.5 %pre.2 = (bf16[512,768]{1,0:T(8,128)(2,1)S(1)}, bf16[512,1536]{1,0:T(8,128)(2,1)S(1)}, f32[8,768]{1,0:T(8,128)S(1)}, bf16[48,2560]{1,0:T(8,128)(2,1)S(1)}, bf16[...) custom-call(s32[2,16]{1,0:T(2,128)S(1)} %stack.279.refs_0_, ...), custom_call_target="tpu_custom_call", output_to_operand_aliasing={{3}: (8, {}), {4}: (9, {}), {5}: (10, {})} | custom-call | flops 7699999744 | tf_op jit(solution)/shard_map/pre/pallas_call | solution.py:88
  114.6 9.0 %collective-permute-done.32 = bf16[48,1280]{1,0:T(8,128)(2,1)S(1)} collective-permute-done((bf16[48,1280]{1,0:T(8,128)(2,1)S(1)}, bf16[48,1280]{1,0:T(8,128)(2,1)S(1)}, u32[]{:S(2)}, u32[]{:S(2)}) %collective-permute-start.32) | collective-permute-done | bytes 122912 | tf_op jit(solution)/shard_map/ppermute | solution.py:724
  126.0 11.8 %collective-permute-done.20.refs_10_ = bf16[8,48,1152]{2,1,0:T(8,128)(2,1)S(1)} collective-permute-done((bf16[8,48,1152]{2,1,0:T(8,128)(2,1)}, bf16[8,48,1152]{2,1,0:T(8,128)(2,1)S(1)}, u32[]{:S(2)}, u32[]{:S(2)}) %collective-permute-start.20) | collective-permute-done | bytes 884768 | tf_op jit(solution)/shard_map/ppermute | solution.py:724
  138.4 14.4 %collective-permute-done.40 = bf16[48,4864]{1,0:T(8,128)(2,1)S(1)} collective-permute-done((bf16[48,4864]{1,0:T(8,128)(2,1)S(1)}, bf16[48,4864]{1,0:T(8,128)(2,1)S(1)}, u32[]{:S(2)}, u32[]{:S(2)}) %collective-permute-start.40) | collective-permute-done | bytes 466976 | tf_op jit(solution)/shard_map/ppermute | solution.py:724
  168.8 12.2 %collective-permute-done.34.refs_5_.refs_14_ = bf16[8,48,1280]{2,1,0:T(8,128)(2,1)S(1)} collective-permute-done((bf16[8,48,1280]{2,1,0:T(8,128)(2,1)S(1)}, bf16[8,48,1280]{2,1,0:T(8,128)(2,1)S(1)}, u32[]{:S(2)}, u32[]{:S(2)}) %collective-permute-start.34) | collective-permute-done | bytes 983072 | tf_op jit(solution)/shard_map/ppermute | solution.py:724
  181.1 11.3 %post.2 = (f32[512,768]{1,0:T(8,128)S(1)}, f32[512,768]{1,0:T(8,128)S(1)}, bf16[512,4096]{1,0:T(8,128)(2,1)S(1)}) custom-call(s32[2,48]{1,0:T(2,128)S(1)} %pad_add_fusion.4.refs_0_, s32[2,32]{1,0:T(2,128)S(1)} %get-tuple-element.261.refs_1_.refs_0_, bf16[512,768]{1,0:T(8,128)(2,1)} %collective-permute-done.refs_1_.refs_2_, ...), custom_call_target="tpu_custom_call" | custom-call | flops 15399999488 | tf_op jit(solution)/shard_map/post/pallas_call | solution.py:88
  197.8 22.0 %collective-permute-done.47 = bf16[4,128,384]{2,1,0:T(8,128)(2,1)S(1)} collective-permute-done((bf16[4,128,384]{2,1,0:T(8,128)(2,1)S(1)}, bf16[4,128,384]{2,1,0:T(8,128)(2,1)S(1)}, u32[]{:S(2)}, u32[]{:S(2)}) %collective-permute-start.47) | collective-permute-done | bytes 393248 | tf_op jit(solution)/shard_map/ppermute | solution.py:724
  222.9 16.7 %collective-permute-done.48.refs_10_.refs_8_ = bf16[8,128,384]{2,1,0:T(8,128)(2,1)S(1)} collective-permute-done((bf16[8,128,384]{2,1,0:T(8,128)(2,1)S(1)}, bf16[8,128,384]{2,1,0:T(8,128)(2,1)S(1)}, u32[]{:S(2)}, u32[]{:S(2)}) %collective-permute-start.48) | collective-permute-done | bytes 786464 | tf_op jit(solution)/shard_map/ppermute | solution.py:724
  248.1 13.1 %post.3 = (f32[512,768]{1,0:T(8,128)S(1)}, f32[512,768]{1,0:T(8,128)S(1)}, bf16[512,4096]{1,0:T(8,128)(2,1)S(1)}) custom-call(s32[2,16]{1,0:T(2,128)S(1)} %stack.279.refs_0_, s32[2,32]{1,0:T(2,128)S(1)} %get-tuple-element.261.refs_1_.refs_0_, f32[512,768]{1,0:T(8,128)S(1)} %get-tuple-element.104.refs_1_.refs_2_, ...), custom_call_target="tpu_custom_call" | custom-call | flops 15399999488 | tf_op jit(solution)/shard_map/post/pallas_call | solution.py:88
  264.4 18.3 %mlp_back.2 = (bf16[512,4096]{1,0:T(8,128)(2,1)S(1)}, bf16[1,768,4096]{2,1,0:T(8,128)(2,1)}, bf16[8,128,384]{2,1,0:T(8,128)(2,1)S(1)}, bf16[8,128,384]{2,1,0:T(8...) custom-call(s32[2,32]{1,0:T(2,128)S(1)} %get-tuple-element.261.refs_1_.refs_0_, ...), custom_call_target="tpu_custom_call" | custom-call | flops 22000001024 | tf_op jit(solution)/shard_map/mlp_back/pallas_call | solution.py:88
  299.2 11.4 %mid_back.2 = (f32[512,768]{1,0:T(8,128)S(1)}, bf16[512,768]{1,0:T(8,128)(2,1)S(1)}, bf16[512,768]{1,0:T(8,128)(2,1)S(1)}, f32[8,768]{1,0:T(8,128)S(1)}, bf16[8,...) custom-call(s32[2,16]{1,0:T(2,128)S(1)} %stack.279.refs_0_, ...), custom_call_target="tpu_custom_call", output_to_operand_aliasing={{4}: (9, {}), {5}: (10, {})} | custom-call | flops 14300000256 | tf_op jit(solution)/shard_map/mid_back/pallas_call | solution.py:88
  313.2 11.8 %attend_back.2 = (bf16[512,768]{1,0:T(8,128)(2,1)S(1)}, bf16[512,1536]{1,0:T(8,128)(2,1)S(1)}, bf16[512,1536]{1,0:T(8,128)(2,1)}, bf16[8,128,384]{2,1,0:T(8,128)(2,1)S(1)}) custom-call(s32[4]{0:T(128)S(1)} %fusion.9.refs_0_, s32[3]{0:T(128)S(1)} %pad_add_fusion.6.refs_1_, bf16[512,768]{1,0:T(8,128)(2,1)S(1)} %copy-done.98, ...), custom_call_target="tpu_custom_call", output_to_operand_aliasing={{3}: (12, {})} | custom-call | flops 22000001024 | tf_op jit(solution)/shard_map/attend_back/pallas_call | solution.py:88
  352.0 10.4 %pre_back.2 = (f32[512,768]{1,0:T(8,128)S(1)}, bf16[8,48,1664]{2,1,0:T(8,128)(2,1)S(1)}, bf16[8,48,1664]{2,1,0:T(8,128)(2,1)S(1)}, bf16[8,48,1664]{2,1,0:T(8,128...) custom-call(s32[2,32]{1,0:T(2,128)S(1)} %get-tuple-element.262.refs_0_, ...), custom_call_target="tpu_custom_call", output_to_operand_aliasing={{5}: (17, {})} | custom-call | flops 16499999744 | tf_op jit(solution)/shard_map/pre_back/pallas_call | solution.py:88
  363.7 17.2 %collective-permute-start.58 = (bf16[8,48,1664]{2,1,0:T(8,128)(2,1)}, bf16[8,48,1664]{2,1,0:T(8,128)(2,1)}, u32[]{:S(2)}, u32[]{:S(2)}) collective-permute-start(bf16[8,48,1664]{2,1,0:T(8,128)(2,1)} %get-tuple-element.143), channel_id=1, source_target_pairs={{0,2},{1,3},{2,0},{3,1},{4,6},{5,7},{6,4},{7,5},{8,10},{9,11},{10,... | collective-permute-start | bytes 3833864 | tf_op jit(solution)/shard_map/ppermute | solution.py:724
  381.2 19.5 %mlp_back.3 = (bf16[512,4096]{1,0:T(8,128)(2,1)}, bf16[1,768,4096]{2,1,0:T(8,128)(2,1)}, bf16[8,128,384]{2,1,0:T(8,128)(2,1)S(1)}, bf16[8,128,384]{2,1,0:T(8,128...) custom-call(s32[2,32]{1,0:T(2,128)S(1)} %get-tuple-element.261.refs_, ...), custom_call_target="tpu_custom_call", output_to_operand_aliasing={{6}: (11, {}), {7}: (12, {}), {8}: (13, {})} | custom-call | flops 22000001024 | tf_op jit(solution)/shard_map/mlp_back/pallas_call | solution.py:88
  423.4 9.3 %mid_back.3 = (f32[512,768]{1,0:T(8,128)S(1)}, bf16[512,768]{1,0:T(8,128)(2,1)S(1)}, bf16[512,768]{1,0:T(8,128)(2,1)S(1)}, f32[8,768]{1,0:T(8,128)S(1)}, f32[128...) custom-call(s32[2,48]{1,0:T(2,128)S(1)} %copy-done.30, ...), custom_call_target="tpu_custom_call", output_to_operand_aliasing={{4}: (13, {}), {5}: (14, {}), {6}: (15, {}), {7}: (16, {})} | custom-call | flops 14300000256 | tf_op jit(solution)/shard_map/mid_back/pallas_call | solution.py:88
  436.4 9.2 %collective-permute-done.63 = bf16[8,48,1664]{2,1,0:T(8,128)(2,1)S(1)} collective-permute-done((bf16[8,48,1664]{2,1,0:T(8,128)(2,1)S(1)}, bf16[8,48,1664]{2,1,0:T(8,128)(2,1)S(1)}, u32[]{:S(2)}, u32[]{:S(2)}) %collective-permute-start.63) | collective-permute-done | bytes 1277984 | tf_op jit(solution)/shard_map/ppermute | solution.py:724
  449.5 10.8 %attend_back.3 = (bf16[512,768]{1,0:T(8,128)(2,1)S(1)}, bf16[512,1536]{1,0:T(8,128)(2,1)S(1)}, bf16[512,1536]{1,0:T(8,128)(2,1)S(1)}, bf16[128,384]{1,0:T(8,128)...) custom-call(s32[4]{0:T(128)S(1)} %fusion.9.refs_0_, ...), custom_call_target="tpu_custom_call", output_to_operand_aliasing={{3}: (12, {}), {4}: (13, {}), {5}: (14, {})} | custom-call | flops 22000001024 | tf_op jit(solution)/shard_map/attend_back/pallas_call | solution.py:88
  474.9 15.8 %pre_back.3 = (f32[512,768]{1,0:T(8,128)S(1)}, bf16[4,48,1536]{2,1,0:T(8,128)(2,1)S(1)}, bf16[4,48,1536]{2,1,0:T(8,128)(2,1)S(1)}, bf16[4,48,1536]{2,1,0:T(8,128...) custom-call(s32[2,16]{1,0:T(2,128)S(1)} %stack.279.refs_0_, ...), custom_call_target="tpu_custom_call", output_to_operand_aliasing={{9}: (17, {}), {10}: (18, {})} | custom-call | flops 16499999744 | tf_op jit(solution)/shard_map/pre_back/pallas_call | solution.py:88
  506.4 8.1 %collective-permute-done.74.refs_6_ = bf16[48,4096]{1,0:T(8,128)(2,1)S(1)} collective-permute-done((bf16[48,4096]{1,0:T(8,128)(2,1)}, bf16[48,4096]{1,0:T(8,128)(2,1)S(1)}, u32[]{:S(2)}, u32[]{:S(2)}) %collective-permute-start.74) | collective-permute-done | bytes 393248 | tf_op jit(solution)/shard_map/ppermute | solution.py:724
  526.5 14.5 %collective-permute-done.95 = bf16[128,384]{1,0:T(8,128)(2,1)S(1)} collective-permute-done((bf16[128,384]{1,0:T(8,128)(2,1)S(1)}, bf16[128,384]{1,0:T(8,128)(2,1)S(1)}, u32[]{:S(2)}, u32[]{:S(2)}) %collective-permute-start.95) | collective-permute-done | bytes 98336 | tf_op jit(solution)/shard_map/ppermute | solution.py:724
  549.8 8.3 %collective-permute-done.84.refs_2_ = bf16[48,4096]{1,0:T(8,128)(2,1)S(1)} collective-permute-done((bf16[48,4096]{1,0:T(8,128)(2,1)}, bf16[48,4096]{1,0:T(8,128)(2,1)S(1)}, u32[]{:S(2)}, u32[]{:S(2)}) %collective-permute-start.84) | collective-permute-done | bytes 393248 | tf_op jit(solution)/shard_map/ppermute | solution.py:724
  (604 shorter events, 259.8 us)
Async XLA Ops:
  7.2 493.3 %reduce-scatter.3.cloned.1.call-start = ((), (), s32[]{:S(2)}) async-start(), calls=%async_computation.2 | async-start | bytes 6684672 | tf_op jit(solution)/shard_map/reduce_scatter | solution.py:867
  16.1 73.2 %collective-permute-start = (bf16[512,768]{1,0:T(8,128)(2,1)}, bf16[512,768]{1,0:T(8,128)(2,1)}, u32[]{:S(2)}, u32[]{:S(2)}) collective-permute-start(bf16[512,768]{1,0:T(8,128)(2,1)} %bitcast.261), channel_id=1, source_target_pairs={{0,0},{1,2},{2,1},{3,3},{4,4},{5,6},{6,5},{7,7},{8,8},{9,10},{10,9... | collective-permute-start | bytes 2359304 | tf_op jit(solution)/shard_map/ppermute | solution.py:724
  24.2 28.7 %collective-permute-start.16 = (bf16[48,1152]{1,0:T(8,128)(2,1)S(1)}, bf16[48,1152]{1,0:T(8,128)(2,1)S(1)}, u32[]{:S(2)}, u32[]{:S(2)}) collective-permute-start(bf16[48,1152]{1,0:T(8,128)(2,1)S(1)} %get-tuple-element.210), channel_id=1, source_target_pairs={{0,8},{1,9},{2,10},{3,11},{4,12},{5,13},{6,14},{7,15},{8,16},{9,17... | collective-permute-start | bytes 331784 | tf_op jit(solution)/shard_map/ppermute | solution.py:724
  30.3 45.0 %collective-permute-start.10 = (bf16[48,2560]{1,0:T(8,128)(2,1)S(1)}, bf16[48,2560]{1,0:T(8,128)(2,1)}, u32[]{:S(2)}, u32[]{:S(2)}) collective-permute-start(bf16[48,2560]{1,0:T(8,128)(2,1)S(1)} %pad_maximum_fusion.15), channel_id=1, source_target_pairs={{0,8},{1,9},{2,10},{3,11},{4,12},{5,13},{6,14},{7,15},{8,16},{9,17... | collective-permute-start | bytes 737288 | tf_op jit(solution)/shard_map/ppermute | solution.py:724
  61.3 28.0 %collective-permute-start.6 = (bf16[4,48,2560]{2,1,0:T(8,128)(2,1)S(1)}, bf16[4,48,2560]{2,1,0:T(8,128)(2,1)S(1)}, u32[]{:S(2)}, u32[]{:S(2)}) collective-permute-start(bf16[4,48,2560]{2,1,0:T(8,128)(2,1)S(1)} %pad_maximum_fusion.1.refs_4_.refs_13_), channel_id=1, source_target_pairs={{0,2},{1,3},{2,0},{3,1},{4,6},{5,7},{6,4},{7,5},{8,10},{9,11},{10,... | collective-permute-start | bytes 2949128 | tf_op jit(solution)/shard_map/ppermute | solution.py:724
  124.3 34.9 %collective-permute-start.9 = (bf16[512,1536]{1,0:T(8,128)(2,1)S(1)}, bf16[512,1536]{1,0:T(8,128)(2,1)S(1)}, u32[]{:S(2)}, u32[]{:S(2)}) collective-permute-start(bf16[512,1536]{1,0:T(8,128)(2,1)S(1)} %get-tuple-element.101.refs_5_.refs_10_), channel_id=1, source_target_pairs={{0,2},{1,3},{2,0},{3,1},{4,6},{5,7},{6,4},{7,5},{8,10},{9,11},{10,... | collective-permute-start | bytes 4718600 | tf_op jit(solution)/shard_map/ppermute | solution.py:724
  124.4 30.9 %collective-permute-start.13 = (bf16[4,48,2560]{2,1,0:T(8,128)(2,1)S(1)}, bf16[4,48,2560]{2,1,0:T(8,128)(2,1)S(1)}, u32[]{:S(2)}, u32[]{:S(2)}) collective-permute-start(bf16[4,48,2560]{2,1,0:T(8,128)(2,1)S(1)} %pad_maximum_fusion.2.refs_5_), channel_id=1, source_target_pairs={{0,4},{1,5},{2,6},{3,7},{4,0},{5,1},{6,2},{7,3},{8,12},{9,13},{10,... | collective-permute-start | bytes 2949128 | tf_op jit(solution)/shard_map/ppermute | solution.py:724
  167.4 29.7 %collective-permute-start.46 = (bf16[128,384]{1,0:T(8,128)(2,1)S(1)}, bf16[128,384]{1,0:T(8,128)(2,1)S(1)}, u32[]{:S(2)}, u32[]{:S(2)}) collective-permute-start(bf16[128,384]{1,0:T(8,128)(2,1)S(1)} %collective-permute-done.45), channel_id=1, source_target_pairs={{0,8},{1,9},{2,10},{3,11},{4,12},{5,13},{6,14},{7,15},{8,16},{9,17... | collective-permute-start | bytes 294920 | tf_op jit(solution)/shard_map/ppermute | solution.py:724
  168.2 53.4 %collective-permute-start.41 = (bf16[4,48,4864]{2,1,0:T(8,128)(2,1)S(1)}, bf16[4,48,4864]{2,1,0:T(8,128)(2,1)S(1)}, u32[]{:S(2)}, u32[]{:S(2)}) collective-permute-start(bf16[4,48,4864]{2,1,0:T(8,128)(2,1)S(1)} %pad_maximum_fusion.refs_5_), channel_id=1, source_target_pairs={{0,4},{1,5},{2,6},{3,7},{4,0},{5,1},{6,2},{7,3},{8,12},{9,13},{10,... | collective-permute-start | bytes 5603336 | tf_op jit(solution)/shard_map/ppermute | solution.py:724
  196.9 42.8 %collective-permute-start.37 = (bf16[512,1536]{1,0:T(8,128)(2,1)S(1)}, bf16[512,1536]{1,0:T(8,128)(2,1)S(1)}, u32[]{:S(2)}, u32[]{:S(2)}) collective-permute-start(bf16[512,1536]{1,0:T(8,128)(2,1)S(1)} %get-tuple-element.107.refs_5_.refs_10_), channel_id=1, source_target_pairs={{0,2},{1,3},{2,0},{3,1},{4,6},{5,7},{6,4},{7,5},{8,10},{9,11},{10,... | collective-permute-start | bytes 4718600 | tf_op jit(solution)/shard_map/ppermute | solution.py:724
  222.2 42.2 %collective-permute-start.52 = (bf16[512,768]{1,0:T(8,128)(2,1)S(1)}, bf16[512,768]{1,0:T(8,128)(2,1)S(1)}, u32[]{:S(2)}, u32[]{:S(2)}) collective-permute-start(bf16[512,768]{1,0:T(8,128)(2,1)S(1)} %bitcast.262), channel_id=1, source_target_pairs={{0,0},{1,2},{2,1},{3,3},{4,4},{5,6},{6,5},{7,7},{8,8},{9,10},{10,9... | collective-permute-start | bytes 2359304 | tf_op jit(solution)/shard_map/ppermute | solution.py:724
  286.5 261.5 %reduce-scatter.5.cloned.1.call-start = ((), (), s32[]{:S(2)}) async-start(), calls=%async_computation.3 | async-start | bytes 6684672 | tf_op jit(solution)/shard_map/reduce_scatter | solution.py:867
  332.8 29.7 %collective-permute-start.55 = (bf16[8,128,384]{2,1,0:T(8,128)(2,1)}, bf16[8,128,384]{2,1,0:T(8,128)(2,1)S(1)}, u32[]{:S(2)}, u32[]{:S(2)}) collective-permute-start(bf16[8,128,384]{2,1,0:T(8,128)(2,1)} %get-tuple-element.134), channel_id=1, source_target_pairs={{0,2},{1,3},{2,0},{3,1},{4,6},{5,7},{6,4},{7,5},{8,10},{9,11},{10,... | collective-permute-start | bytes 2359304 | tf_op jit(solution)/shard_map/ppermute | solution.py:724
  334.5 28.0 %collective-permute-start.56 = (bf16[8,128,384]{2,1,0:T(8,128)(2,1)S(1)}, bf16[8,128,384]{2,1,0:T(8,128)(2,1)S(1)}, u32[]{:S(2)}, u32[]{:S(2)}) collective-permute-start(bf16[8,128,384]{2,1,0:T(8,128)(2,1)S(1)} %add_convert_fusion.2.refs_13_), channel_id=1, source_target_pairs={{0,1},{1,0},{2,3},{3,2},{4,5},{5,4},{6,7},{7,6},{8,9},{9,8},{10,11... | collective-permute-start | bytes 2359304 | tf_op jit(solution)/shard_map/ppermute | solution.py:724
  363.7 45.8 %collective-permute-start.58 = (bf16[8,48,1664]{2,1,0:T(8,128)(2,1)}, bf16[8,48,1664]{2,1,0:T(8,128)(2,1)}, u32[]{:S(2)}, u32[]{:S(2)}) collective-permute-start(bf16[8,48,1664]{2,1,0:T(8,128)(2,1)} %get-tuple-element.143), channel_id=1, source_target_pairs={{0,2},{1,3},{2,0},{3,1},{4,6},{5,7},{6,4},{7,5},{8,10},{9,11},{10,... | collective-permute-start | bytes 3833864 | tf_op jit(solution)/shard_map/ppermute | solution.py:724
  403.4 30.8 %collective-permute-start.64 = (bf16[8,128,384]{2,1,0:T(8,128)(2,1)}, bf16[8,128,384]{2,1,0:T(8,128)(2,1)}, u32[]{:S(2)}, u32[]{:S(2)}) collective-permute-start(bf16[8,128,384]{2,1,0:T(8,128)(2,1)} %get-tuple-element.151), channel_id=1, source_target_pairs={{0,2},{1,3},{2,0},{3,1},{4,6},{5,7},{6,4},{7,5},{8,10},{9,11},{10,... | collective-permute-start | bytes 2359304 | tf_op jit(solution)/shard_map/ppermute | solution.py:724
  404.9 31.5 %collective-permute-start.62 = (bf16[8,48,1664]{2,1,0:T(8,128)(2,1)}, bf16[8,48,1664]{2,1,0:T(8,128)(2,1)}, u32[]{:S(2)}, u32[]{:S(2)}) collective-permute-start(bf16[8,48,1664]{2,1,0:T(8,128)(2,1)} %get-tuple-element.148), channel_id=1, source_target_pairs={{0,2},{1,3},{2,0},{3,1},{4,6},{5,7},{6,4},{7,5},{8,10},{9,11},{10,... | collective-permute-start | bytes 3833864 | tf_op jit(solution)/shard_map/ppermute | solution.py:724
  414.5 31.1 %collective-permute-start.63 = (bf16[8,48,1664]{2,1,0:T(8,128)(2,1)S(1)}, bf16[8,48,1664]{2,1,0:T(8,128)(2,1)S(1)}, u32[]{:S(2)}, u32[]{:S(2)}) collective-permute-start(bf16[8,48,1664]{2,1,0:T(8,128)(2,1)S(1)} %add_convert_fusion.refs_20_), channel_id=1, source_target_pairs={{0,1},{1,0},{2,3},{3,2},{4,5},{5,4},{6,7},{7,6},{8,9},{9,8},{10,11... | collective-permute-start | bytes 3833864 | tf_op jit(solution)/shard_map/ppermute | solution.py:724
  432.7 27.7 %collective-permute-start.67 = (bf16[8,128,384]{2,1,0:T(8,128)(2,1)S(1)}, bf16[8,128,384]{2,1,0:T(8,128)(2,1)S(1)}, u32[]{:S(2)}, u32[]{:S(2)}) collective-permute-start(bf16[8,128,384]{2,1,0:T(8,128)(2,1)S(1)} %copy-done.78), channel_id=1, source_target_pairs={{0,2},{1,3},{2,0},{3,1},{4,6},{5,7},{6,4},{7,5},{8,10},{9,11},{10,... | collective-permute-start | bytes 2359304 | tf_op jit(solution)/shard_map/ppermute | solution.py:724
  432.8 31.1 %collective-permute-start.96 = (bf16[128,384]{1,0:T(8,128)(2,1)S(1)}, bf16[128,384]{1,0:T(8,128)(2,1)S(1)}, u32[]{:S(2)}, u32[]{:S(2)}) collective-permute-start(bf16[128,384]{1,0:T(8,128)(2,1)S(1)} %add_convert_fusion.8.refs_15_), channel_id=1, source_target_pairs={{0,1},{1,0},{2,3},{3,2},{4,5},{5,4},{6,7},{7,6},{8,9},{9,8},{10,11... | collective-permute-start | bytes 294920 | tf_op jit(solution)/shard_map/ppermute | solution.py:724
  463.6 35.8 %collective-permute-start.73 = (bf16[4,128,384]{2,1,0:T(8,128)(2,1)S(1)}, bf16[4,128,384]{2,1,0:T(8,128)(2,1)S(1)}, u32[]{:S(2)}, u32[]{:S(2)}) collective-permute-start(bf16[4,128,384]{2,1,0:T(8,128)(2,1)S(1)} %slice.379.refs_23_), channel_id=1, source_target_pairs={{0,4},{1,5},{2,6},{3,7},{4,0},{5,1},{6,2},{7,3},{8,12},{9,13},{10,... | collective-permute-start | bytes 1179656 | tf_op jit(solution)/shard_map/ppermute | solution.py:724
  468.1 31.0 %collective-permute-start.70 = (bf16[48,1664]{1,0:T(8,128)(2,1)S(1)}, bf16[48,1664]{1,0:T(8,128)(2,1)S(1)}, u32[]{:S(2)}, u32[]{:S(2)}) collective-permute-start(bf16[48,1664]{1,0:T(8,128)(2,1)S(1)} %get-tuple-element.223.refs_20_), channel_id=1, source_target_pairs={{0,8},{1,9},{2,10},{3,11},{4,12},{5,13},{6,14},{7,15},{8,16},{9,17... | collective-permute-start | bytes 479240 | tf_op jit(solution)/shard_map/ppermute | solution.py:724
  471.0 28.2 %collective-permute-start.71 = (bf16[48,1664]{1,0:T(8,128)(2,1)S(1)}, bf16[48,1664]{1,0:T(8,128)(2,1)S(1)}, u32[]{:S(2)}, u32[]{:S(2)}) collective-permute-start(bf16[48,1664]{1,0:T(8,128)(2,1)S(1)} %get-tuple-element.222.refs_21_), channel_id=1, source_target_pairs={{0,16},{1,17},{2,18},{3,19},{4,20},{5,21},{6,22},{7,23},{8,24},{9,... | collective-permute-start | bytes 479240 | tf_op jit(solution)/shard_map/ppermute | solution.py:724
  518.8 28.3 %collective-permute-start.82 = (bf16[8,48,896]{2,1,0:T(8,128)(2,1)S(1)}, bf16[8,48,896]{2,1,0:T(8,128)(2,1)S(1)}, u32[]{:S(2)}, u32[]{:S(2)}) collective-permute-start(bf16[8,48,896]{2,1,0:T(8,128)(2,1)S(1)} %copy-done.83), channel_id=1, source_target_pairs={{0,2},{1,3},{2,0},{3,1},{4,6},{5,7},{6,4},{7,5},{8,10},{9,11},{10,... | collective-permute-start | bytes 2064392 | tf_op jit(solution)/shard_map/ppermute | solution.py:724
  (210 other events, 3390.6 us)
Sparse Core Ops, SparseCore 0:
  286.6 87.8 reduce-scatter.2
  405.0 99.5 reduce-scatter.4
